TPU v7x, 512 devices: a whole 4x4x16 slice. The times are simulated.
512 devices in a mesh: section: 16 (over x, y), expert: 32 (over z, core).
Axes of the slice: x: 4, y: 4, z: 16, core: 2. Of those that a mesh axis runs over, the one named last changes fastest.
Arguments:
- carried: bfloat16 [2, 16, 1536, 3584], P(None, 'section', 'expert'), may hold values from -6 to 6
- norm_gain: bfloat16 [16, 3584], P('section'), may hold values from 0.099609375 to 1.8984375
- router: bfloat16 [16, 3584, 8], P('section'), may hold values from -0.09375 to 0.09375
- w_up: bfloat16 [16, 3584, 8192], P('section', None, 'expert'), may hold values from -0.09375 to 0.09375
- w_down: bfloat16 [16, 8192, 3584], P('section', 'expert'), may hold values from -0.1875 to 0.1875
- expert_ids: int32 [16, 2, 1536, 1], P('section', None, 'expert'), may hold values from 0 to 7; in each aligned block of 48 rows (0 to 47, 48 to 95, ..., all dimensions but the last counted through in order) at most 9 rows name the same one
Outputs:
- advanced: bfloat16 [2, 16, 1536, 3584], P(None, 'section', 'expert')
Inputs may be any that keep to these rules, and one draw needn't show every extreme that they name: `expert_ids`: within each aligned block of 48 tokens of one section and direction (the tokens of one device), at most 9 tokens choose any one expert, and some block reaches 9.
All inputs are finite; a program needn't handle non-finite values.
Results may differ from a plain program's by a relative error of at most 0.01.
Values may be sent and summed in bfloat16 or wider, within the bound.
No kernel may reach another device: no remote copies, remote signals or barrier semaphores. Data moves between devices by JAX's collectives and lax.ppermute only.
A program may use at most 64 MiB of HBM per device.

v0:
```python
import jax
import jax.numpy as jnp
from jax import lax
from jax.sharding import PartitionSpec as P

SPLIT = 4


epsilon = 1e-06
route_scale = 2.5


def passed_along(block, axis, distance):
    devices = range(lax.axis_size(axis))
    route = [(i - distance, i) for i in devices if i - distance in devices]
    return lax.ppermute(block, axis, route)


def normalize(activations, gain):
    widened = activations.astype(jnp.float32)
    mean_square = jnp.mean(widened * widened, axis=-1, keepdims=True)
    return (widened * lax.rsqrt(mean_square + epsilon) * gain.astype(jnp.float32)).astype(
        jnp.bfloat16
    )


def prepare(activations, gain, router_matrix, chosen_ids, experts, capacity):
    normed = normalize(activations, gain)
    logits = jnp.dot(normed, router_matrix, preferred_element_type=jnp.float32)
    chosen = chosen_ids[:, 0]
    one_hot = (chosen[:, None] == jnp.arange(experts, dtype=jnp.int32)[None, :]).astype(jnp.int32)
    gate_value = route_scale * jax.nn.sigmoid(
        jnp.sum(logits * one_hot.astype(jnp.float32), axis=-1)
    )
    slot = jnp.sum((jnp.cumsum(one_hot, axis=0) - one_hot) * one_hot, axis=-1)
    target = chosen * capacity + slot
    placer = (target[None, :] == jnp.arange(experts * capacity, dtype=jnp.int32)[:, None]).astype(
        jnp.bfloat16
    )
    slot_rows = jnp.dot(placer, normed, preferred_element_type=jnp.float32).astype(jnp.bfloat16)
    slot_rows = slot_rows.reshape(experts, capacity, normed.shape[1])
    return (jnp.repeat(slot_rows, SPLIT, axis=0), gate_value, target)


def per_device(carried, norm_gain, router, w_up, w_down, expert_ids):
    groups = lax.axis_size("expert")
    experts = groups // SPLIT
    tokens_here = carried.shape[2]
    width = carried.shape[3]
    capacity = tokens_here * expert_ids.shape[3] * 3 // (2 * experts)
    prepared = [
        prepare(
            carried[direction, 0],
            norm_gain[0],
            router[0],
            expert_ids[0, direction],
            experts,
            capacity,
        )
        for direction in range(2)
    ]
    up_matrix = w_up[0]
    down_matrix = w_down[0]
    stacked = jnp.concatenate([prepared[0][0], prepared[1][0]], axis=1)
    received = lax.all_to_all(stacked, "expert", split_axis=0, concat_axis=0, tiled=True)
    items = received.shape[1]
    flat_rows = received.reshape(-1, width)
    hidden_pre = jnp.dot(flat_rows, up_matrix, preferred_element_type=jnp.float32)
    activated = jax.nn.silu(hidden_pre).astype(jnp.bfloat16)
    partial_value = jnp.dot(activated, down_matrix, preferred_element_type=jnp.float32).astype(
        jnp.bfloat16
    )
    partial_value = partial_value.reshape(received.shape)
    returned = lax.all_to_all(partial_value, "expert", split_axis=0, concat_axis=0, tiled=True)
    members = returned.reshape(experts, SPLIT, items, width).astype(jnp.float32)
    pair_low = (members[:, 0] + members[:, 1]).astype(jnp.bfloat16)
    pair_high = (members[:, 2] + members[:, 3]).astype(jnp.bfloat16)
    expert_rows = (pair_low.astype(jnp.float32) + pair_high.astype(jnp.float32)).astype(
        jnp.bfloat16
    )
    results = [expert_rows[:, :capacity], expert_rows[:, capacity:]]
    layer_outputs = []
    for direction in range(2):
        gate_value = prepared[direction][1]
        target = prepared[direction][2]
        routed = jnp.take(
            results[direction].reshape(experts * capacity, width), target, axis=0
        ).astype(jnp.float32)
        widened = carried[direction, 0].astype(jnp.float32)
        layer_outputs.append((widened + gate_value[:, None] * routed).astype(jnp.bfloat16))
    section_index = lax.axis_index("section")
    last_section = lax.axis_size("section") - 1
    from_below = passed_along(layer_outputs[0], "section", 1)
    from_above = passed_along(layer_outputs[1], "section", -1)
    new_up = jnp.where(section_index == 0, layer_outputs[1], from_below)
    new_down = jnp.where(section_index == last_section, layer_outputs[0], from_above)
    return jnp.stack([new_up, new_down])[:, None]


def solution(mesh):
    in_specs = (
        P(None, "section", "expert", None),
        P("section", None),
        P("section", None, None),
        P("section", None, "expert"),
        P("section", "expert", None),
        P("section", None, "expert", None),
    )
    out_specs = P(None, "section", "expert", None)
    return jax.shard_map(
        per_device, mesh=mesh, in_specs=in_specs, out_specs=out_specs, check_vma=False
    )
```

profile of v0, /device:TPU:24, one launch (start us, length us, event | category | flops | bytes accessed | tf_op | source)
XLA Modules:
  0.0 587.8 jit_solution(10776819538911192593)
XLA Ops:
  0.0 0.0 copy-start
  0.0 0.8 slice_bitcast_fusion.4
  0.8 1.3 fusion.22
  2.2 0.8 convert_reduce_fusion
  2.9 0.1 copy.16
  3.0 0.1 reduce_window_sum.18
  3.1 0.1 copy.17
  3.1 0.1 copy.18
  3.2 0.1 reduce_window_sum.17
  3.3 0.1 copy.19
  3.4 0.7 compare_and_fusion
  4.1 1.3 convolution_convert_fusion.1
  5.4 0.2 reshape.123
  5.6 1.3 convolution_convert_fusion.2
  7.0 1.1 reshape.121
  8.1 1.6 broadcast_in_dim.12
  9.7 2.2 broadcast_in_dim.13
  12.0 3.6 pad_maximum_fusion
  15.5 262.8 %all_to_all.10 = bf16[32,18,3584]{2,1,0:T(8,128)(2,1)} all-to-all(bf16[32,18,3584]{2,1,0:T(8,128)(2,1)S(1)} %pad_maximum_fusion), channel_id=1, replica_groups=mesh['section'=16,'expert'=32] {'expert'}, dimensions={0} | all-to-all | bytes 8257536 | tf_op jit(solution)/shard_map/all_to_all | solution.py:65
  278.4 7.3 %reshape.125 = bf16[576,3584]{1,0:T(8,128)(2,1)} reshape(bf16[32,18,3584]{2,1,0:T(8,128)(2,1)} %all_to_all.10) | data formatting | bytes 8257536 | tf_op jit(solution)/shard_map/reshape | solution.py:67
  285.7 0.0 copy-done
  285.7 9.2 %convolution_convert_fusion = bf16[576,3584]{1,0:T(8,128)(2,1)} fusion(bf16[1,256,3584]{2,1,0:T(8,128)(2,1)S(1)} %copy-done, bf16[576,3584]{1,0:T(8,128)(2,1)} %reshape.125, bf16[1,3584,256]{2,1,0:T(8,128)(2,1)} %param.11), kind=kOutput, calls=%fused_computation.2 | convolution fusion | flops 2116730880 | bytes 11927552 | tf_op jit(solution)/shard_map/dot_general | solution.py:70
  294.9 7.2 %reshape.126 = bf16[32,18,3584]{2,1,0:T(8,128)(2,1)} reshape(bf16[576,3584]{1,0:T(8,128)(2,1)} %convolution_convert_fusion) | data formatting | bytes 8257536 | tf_op jit(solution)/shard_map/reshape | solution.py:73
  302.1 0.0 copy-start.1
  302.1 0.0 copy-start.2
  302.1 5.0 all-to-all-start.1
  307.2 0.0 copy-done.1
  307.2 0.0 copy-done.2
  307.2 0.3 fusion.9
  307.5 247.1 %all-to-all-done.1 = bf16[32,18,3584]{2,1,0:T(8,128)(2,1)} async-done(((bf16[32,18,3584]{2,1,0:T(8,128)(2,1)}), bf16[32,18,3584]{2,1,0:T(8,128)(2,1)}, u32[]{:S(2)}, u32[]{:S(2)}) %all-to-all-start.1) | async-done | bytes 4128800 | tf_op jit(solution)/shard_map/all_to_all | solution.py:74
  554.7 4.0 convert.8
  558.7 0.8 fusion.7
  559.5 1.4 fusion.59
  560.9 1.4 reshape.128
  562.4 0.8 gather_fusion.1
  563.1 0.9 fusion.25
  564.0 3.0 collective-permute-start
  567.1 0.3 fusion.8
  567.4 1.4 reshape.127
  568.8 0.8 gather_fusion
  569.6 3.9 collective-permute-done
  573.5 2.0 select_bitcast_fusion.1
  575.4 2.6 collective-permute-start.1
  578.1 8.8 %collective-permute-done.1 = bf16[48,3584]{1,0:T(8,128)(2,1)S(1)} collective-permute-done((bf16[48,3584]{1,0:T(8,128)(2,1)}, bf16[48,3584]{1,0:T(8,128)(2,1)S(1)}, u32[]{:S(2)}, u32[]{:S(2)}) %collective-permute-start.1) | collective-permute-done | bytes 344096 | tf_op jit(solution)/shard_map/ppermute | solution.py:16
  586.9 0.9 maximum_bitcast_fusion
  (11 shorter events, 0.1 us)
Async XLA Ops:
  0.0 285.7 %copy-start = (bf16[1,256,3584]{2,1,0:T(8,128)(2,1)S(1)}, bf16[1,256,3584]{2,1,0:T(8,128)(2,1)}, u32[]{:S(2)}) copy-start(bf16[1,256,3584]{2,1,0:T(8,128)(2,1)} %param.12) | copy-start | bytes 5505028
  302.1 5.1 copy-start.1
  302.1 5.1 copy-start.2
  302.1 252.5 %all-to-all-start.1 = ((bf16[32,18,3584]{2,1,0:T(8,128)(2,1)}), bf16[32,18,3584]{2,1,0:T(8,128)(2,1)}, u32[]{:S(2)}, u32[]{:S(2)}) async-start(bf16[32,18,3584]{2,1,0:T(8,128)(2,1)} %reshape.126), calls=%async_computation.1 | async-start | bytes 11010048 | tf_op jit(solution)/shard_map/all_to_all | solution.py:74
  564.0 9.4 %collective-permute-start = (bf16[48,3584]{1,0:T(8,128)(2,1)}, bf16[48,3584]{1,0:T(8,128)(2,1)}, u32[]{:S(2)}, u32[]{:S(2)}) collective-permute-start(bf16[48,3584]{1,0:T(8,128)(2,1)} %fusion.25), channel_id=1, source_target_pairs={{0,32},{32,64},{64,96},{96,128},{128,160},{160,192},{192,224},{224... | collective-permute-start | bytes 1032200 | tf_op jit(solution)/shard_map/ppermute | solution.py:16
  575.4 11.5 %collective-permute-start.1 = (bf16[48,3584]{1,0:T(8,128)(2,1)}, bf16[48,3584]{1,0:T(8,128)(2,1)S(1)}, u32[]{:S(2)}, u32[]{:S(2)}) collective-permute-start(bf16[48,3584]{1,0:T(8,128)(2,1)} %get-tuple-element.9), channel_id=1, source_target_pairs={{32,0},{64,32},{96,64},{128,96},{160,128},{192,160},{224,192},{256... | collective-permute-start | bytes 1032200 | tf_op jit(solution)/shard_map/ppermute | solution.py:16
where the time goes:
time: 591 us; the launch traced here: 588 us
  blocking collectives  263 us (45%)
  waiting for transfers between devices  260 us (44%)
  local copies, waits for them, and re-layouts  26.6 us (5%)
  other arithmetic  15.2 us (3%)
  matrix products  12.4 us (2%)
  starting transfers between devices  10.7 us (2%)
    all_to_all x1, blocking collectives, per_device(): lax.all_to_all(stacked, 'expert', split_axis=0, concat_axis=0, tiled=True)  263 us
    all_to_all x1, waiting for transfers between devices, per_device(): lax.all_to_all(partial_value, 'expert', split_axis=0, concat_axis=0, tile...  247 us
    ppermute x2, waiting for transfers between devices, passed_along(): return lax.ppermute(block, axis, route)  12.7 us
  transfers between devices with their start and end apart: 3, of which 3 were waited for; matrix products, arithmetic and copies ran while one was open for 0% of the time, Pallas kernels for 0%

commit v1 on v0

v1 whole, which is shorter than its diff:
```python
import jax
import jax.numpy as jnp
from jax import lax
from jax.experimental import pallas as pl
from jax.experimental.pallas import tpu as pltpu
from jax.sharding import PartitionSpec as P

SPLIT = 4
LANES = 128
MAIN = 8

epsilon = 1e-06
route_scale = 2.5


def iota(shape, dimension):
    return lax.broadcasted_iota(jnp.int32, shape, dimension)


def tail_spread(experts, chunks, padded, back):
    shape = (chunks * experts, experts * padded) if back else (experts * padded, chunks * experts)
    by_expert = iota(shape, 1 if back else 0)
    by_chunk = iota(shape, 0 if back else 1)
    same_expert = by_expert // padded == by_chunk % experts
    same_chunk = by_expert % padded == by_chunk // experts
    return (same_expert & same_chunk).astype(jnp.float32).astype(jnp.bfloat16)


def write_packet(packet_ref, pair, columns):
    experts = packet_ref.shape[0]
    low = columns[:, :LANES].reshape(experts, MAIN, LANES)
    high = columns[:, LANES:].reshape(experts, MAIN, LANES)
    packet_ref[:, pair] = jnp.concatenate([low, high], axis=1).astype(jnp.bfloat16)


def write_tail(packet_ref, stacked):
    experts, blocks = packet_ref.shape[:2]
    pairs = blocks - 2
    spread = tail_spread(experts, 2 * pairs, 32, False)
    tail = jnp.dot(spread, stacked, preferred_element_type=jnp.float32).astype(jnp.bfloat16)
    packet_ref[:, pairs:] = tail.reshape(experts, 2, 16, LANES)


def read_pair(packet_ref, pair):
    experts = packet_ref.shape[0]
    block = packet_ref[:, pair].astype(jnp.float32).reshape(experts, 2, MAIN, LANES)
    low = block[:, 0].reshape(experts * MAIN, LANES)
    high = block[:, 1].reshape(experts * MAIN, LANES)
    return jnp.concatenate([low, high], axis=1).astype(jnp.bfloat16)


def read_tail(packet_ref):
    experts, blocks = packet_ref.shape[:2]
    pairs = blocks - 2
    gather = tail_spread(experts, 2 * pairs, 32, True)
    tail = packet_ref[:, pairs:].reshape(experts * 32, LANES)
    return jnp.dot(gather, tail, preferred_element_type=jnp.float32)


def prepare_kernel(x_ref, gain_ref, router_ref, ids_ref, packet_ref, gate_ref, row_ref):
    experts = packet_ref.shape[0]
    pairs = packet_ref.shape[1] - 2
    tokens = x_ref.shape[2]
    x = x_ref[0, 0].astype(jnp.float32)
    mean_square = jnp.mean(x * x, axis=-1, keepdims=True)
    normed = (x * lax.rsqrt(mean_square + epsilon) * gain_ref[...].astype(jnp.float32)).astype(
        jnp.bfloat16
    )
    logits = jnp.dot(normed, router_ref[0], preferred_element_type=jnp.float32)
    chosen = ids_ref[0, 0]
    one_hot = (iota((tokens, experts), 1) == chosen).astype(jnp.float32)
    gate = route_scale * jax.nn.sigmoid(jnp.sum(logits * one_hot, axis=-1, keepdims=True))
    earlier = (iota((tokens, tokens), 1) < iota((tokens, tokens), 0)).astype(jnp.float32)
    before = jnp.dot(
        earlier.astype(jnp.bfloat16),
        one_hot.astype(jnp.bfloat16),
        preferred_element_type=jnp.float32,
    )
    slot = jnp.sum(before * one_hot, axis=-1, keepdims=True)
    expert = chosen.astype(jnp.float32)
    row = jnp.where(slot < MAIN, expert * MAIN + slot, experts * MAIN + expert)
    gate_ref[...] = jnp.broadcast_to(gate, gate_ref.shape)
    row_ref[...] = jnp.broadcast_to(row, row_ref.shape)
    diagonal = iota((tokens, tokens), 0) == iota((tokens, tokens), 1)
    row_along = jnp.sum(jnp.where(diagonal, row, 0.0), axis=0, keepdims=True)
    rows = experts * (MAIN + 1)
    placer = (iota((rows, tokens), 0).astype(jnp.float32) == row_along).astype(jnp.float32)
    slots = jnp.dot(placer.astype(jnp.bfloat16), normed, preferred_element_type=jnp.float32)
    main, tail = slots[: experts * MAIN], slots[experts * MAIN :]
    for pair in range(pairs):
        write_packet(packet_ref, pair, main[:, pair * 256 : (pair + 1) * 256])
    stacked = jnp.concatenate(
        [tail[:, c * LANES : (c + 1) * LANES] for c in range(2 * pairs)], axis=0
    )
    write_tail(packet_ref, stacked.astype(jnp.bfloat16))


def expert_kernel(own_ref, core_ref, chip_ref, both_ref, up_ref, down_ref, *rest):
    outs, rows_ref = rest[:4], rest[4]
    ins = (own_ref, core_ref, chip_ref, both_ref)
    experts = own_ref.shape[0]
    pairs = own_ref.shape[1] - 2
    main = experts * MAIN
    tails = [read_tail(ref) for ref in ins]
    for pair in range(pairs):
        columns = slice(pair * 256, (pair + 1) * 256)
        for index, ref in enumerate(ins):
            rows_ref[index * main : (index + 1) * main, columns] = read_pair(ref, pair)
        for half in range(2):
            chunk = 2 * pair + half
            block = jnp.concatenate(
                [tail[chunk * experts : (chunk + 1) * experts] for tail in tails], axis=0
            )
            rows_ref[4 * main :, chunk * LANES : (chunk + 1) * LANES] = block.astype(jnp.bfloat16)
    hidden_pre = jnp.dot(rows_ref[...], up_ref[0], preferred_element_type=jnp.float32)
    activated = (hidden_pre / (1.0 + jnp.exp(-hidden_pre))).astype(jnp.bfloat16)
    tail_chunks = [[] for _ in ins]
    for pair in range(pairs):
        columns = slice(pair * 256, (pair + 1) * 256)
        partial = jnp.dot(activated, down_ref[0, :, columns], preferred_element_type=jnp.float32)
        for index, ref in enumerate(outs):
            write_packet(ref, pair, partial[index * main : (index + 1) * main])
            first = 4 * main + index * experts
            for half in range(2):
                tail_chunks[index].append(
                    partial[first : first + experts, half * LANES : (half + 1) * LANES]
                )
    for index, ref in enumerate(outs):
        write_tail(ref, jnp.concatenate(tail_chunks[index], axis=0).astype(jnp.bfloat16))


def finish_kernel(x_ref, packet_ref, gate_ref, row_ref, out_ref):
    experts = packet_ref.shape[0]
    pairs = packet_ref.shape[1] - 2
    tokens = x_ref.shape[2]
    rows = experts * (MAIN + 1)
    row = row_ref[:, :1]
    gate = gate_ref[:, :1]
    chooser = (iota((tokens, rows), 1).astype(jnp.float32) == row).astype(jnp.float32)
    choose_main = chooser[:, : experts * MAIN].astype(jnp.bfloat16)
    choose_tail = chooser[:, experts * MAIN :].astype(jnp.bfloat16)
    tail = read_tail(packet_ref)
    for pair in range(pairs):
        columns = slice(pair * 256, (pair + 1) * 256)
        first = 2 * pair * experts
        tail_pair = jnp.concatenate(
            [tail[first : first + experts], tail[first + experts : first + 2 * experts]], axis=1
        ).astype(jnp.bfloat16)
        routed = jnp.dot(
            choose_main, read_pair(packet_ref, pair), preferred_element_type=jnp.float32
        ) + jnp.dot(choose_tail, tail_pair, preferred_element_type=jnp.float32)
        x = x_ref[0, 0, :, columns].astype(jnp.float32)
        out_ref[:, columns] = (x + gate * routed).astype(jnp.bfloat16)


def params():
    return pltpu.CompilerParams(vmem_limit_bytes=48 * 1024 * 1024)


def whole(array):
    return pl.BlockSpec(array.shape, lambda _: (0,) * array.ndim)


def prepare(direction, carried, gain, router, ids, experts):
    tokens, width = carried.shape[2:]
    blocks = width // 256 + 2
    packet = jax.ShapeDtypeStruct((experts, blocks, 16, LANES), jnp.bfloat16)
    notes = jax.ShapeDtypeStruct((tokens, LANES), jnp.float32)
    return pl.pallas_call(
        prepare_kernel,
        grid=(1,),
        out_shape=(packet, notes, notes),
        in_specs=[
            pl.BlockSpec((1, 1, tokens, width), lambda _: (direction, 0, 0, 0)),
            whole(gain),
            whole(router),
            pl.BlockSpec((1, 1, tokens, 1), lambda _: (0, direction, 0, 0)),
        ],
        out_specs=(whole(packet), whole(notes), whole(notes)),
        compiler_params=params(),
        name="prepare",
    )(carried, gain, router, ids)


def run_expert(own, core, chip, both, up, down):
    experts = own.shape[0]
    packet = jax.ShapeDtypeStruct(own.shape, own.dtype)
    rows = 4 * experts * (MAIN + 1)
    width = up.shape[1]
    return pl.pallas_call(
        expert_kernel,
        grid=(1,),
        out_shape=(packet,) * 4,
        in_specs=[whole(a) for a in (own, core, chip, both, up, down)],
        out_specs=(whole(packet),) * 4,
        scratch_shapes=[pltpu.VMEM((rows, width), jnp.bfloat16)],
        compiler_params=params(),
        name="expert",
    )(own, core, chip, both, up, down)


def finish(direction, carried, packet, gate, row):
    tokens, width = carried.shape[2:]
    out = jax.ShapeDtypeStruct((tokens, width), jnp.bfloat16)
    return pl.pallas_call(
        finish_kernel,
        grid=(1,),
        out_shape=out,
        in_specs=[
            pl.BlockSpec((1, 1, tokens, width), lambda _: (direction, 0, 0, 0)),
            whole(packet),
            whole(gate),
            whole(row),
        ],
        out_specs=whole(out),
        compiler_params=params(),
        name="finish",
    )(carried, packet, gate, row)


def passed_along(block, axis, distance):
    devices = range(lax.axis_size(axis))
    route = [(i - distance, i) for i in devices if i - distance in devices]
    return lax.ppermute(block, axis, route)


def swapped(block, bit):
    return lax.ppermute(
        block, "expert", [(i, i ^ bit) for i in range(lax.axis_size("expert"))]
    )


def exchanged(packet):
    experts = lax.axis_size("expert") // SPLIT
    groups = [[e * SPLIT + k for e in range(experts)] for k in range(SPLIT)]
    return lax.all_to_all(
        packet, "expert", split_axis=0, concat_axis=0, axis_index_groups=groups, tiled=True
    )


def added(left, right):
    return (left.astype(jnp.float32) + right.astype(jnp.float32)).astype(jnp.bfloat16)


def per_device(carried, norm_gain, router, w_up, w_down, expert_ids):
    experts = lax.axis_size("expert") // SPLIT
    layer_outputs = []
    prepared = [
        prepare(direction, carried, norm_gain, router, expert_ids, experts)
        for direction in range(2)
    ]
    for direction in range(2):
        packet, gate, row = prepared[direction]
        own = exchanged(packet)
        chip = swapped(own, 2)
        core = swapped(own, 1)
        both = swapped(chip, 1)
        for_own, for_core, for_chip, for_both = run_expert(own, core, chip, both, w_up, w_down)
        own_sum = added(for_own, swapped(for_core, 1))
        chip_sum = added(for_chip, swapped(for_both, 1))
        total = added(own_sum, swapped(chip_sum, 2))
        returned = exchanged(total)
        layer_outputs.append(finish(direction, carried, returned, gate, row))
    section_index = lax.axis_index("section")
    last_section = lax.axis_size("section") - 1
    from_below = passed_along(layer_outputs[0], "section", 1)
    from_above = passed_along(layer_outputs[1], "section", -1)
    new_up = jnp.where(section_index == 0, layer_outputs[1], from_below)
    new_down = jnp.where(section_index == last_section, layer_outputs[0], from_above)
    return jnp.stack([new_up, new_down])[:, None]


def solution(mesh):
    in_specs = (
        P(None, "section", "expert", None),
        P("section", None),
        P("section", None, None),
        P("section", None, "expert"),
        P("section", "expert", None),
        P("section", None, "expert", None),
    )
    out_specs = P(None, "section", "expert", None)
    return jax.shard_map(
        per_device, mesh=mesh, in_specs=in_specs, out_specs=out_specs, check_vma=False
    )
```

time: 591 us -> 240 us (0.41)
  the two profiles are of different devices: /device:TPU:24 before, /device:TPU:36 now
where the time goes in v1:
time: 240 us; the launch traced here: 239 us
  waiting for transfers between devices  133 us (55%)
  starting transfers between devices  80 us (33%)
  Pallas kernels  13.1 us (5%)
  local copies, waits for them, and re-layouts  8.27 us (3%)
  other arithmetic  4.32 us (2%)
    ppermute x12, waiting for transfers between devices, swapped(): lax.ppermute(block, 'expert', [(i, i ^ bit) for i in range(lax.axis_size(...  70.3 us
    all_to_all x4, waiting for transfers between devices, exchanged(): lax.all_to_all(packet, 'expert', split_axis=0, concat_axis=0, axis_index_...  52.4 us
    all_to_all x4, starting transfers between devices, exchanged(): lax.all_to_all(packet, 'expert', split_axis=0, concat_axis=0, axis_index_...  43.9 us
    ppermute x12, starting transfers between devices, swapped(): lax.ppermute(block, 'expert', [(i, i ^ bit) for i in range(lax.axis_size(...  27.7 us
    ppermute x2, waiting for transfers between devices, passed_along(): return lax.ppermute(block, axis, route)  10.3 us
    pallas_call x2, Pallas kernels, run_expert(): pl.pallas_call(expert_kernel, grid=(1,), out_shape=(packet,) * 4, in_spec...  10.1 us
    ppermute x2, starting transfers between devices, passed_along(): return lax.ppermute(block, axis, route)  8.36 us
    unnamed x30, local copies, waits for them, and re-layouts  8.27 us
  transfers between devices with their start and end apart: 18, of which 8 were waited for; matrix products, arithmetic and copies ran while one was open for 1% of the time, Pallas kernels for 5%

profile of v1, /device:TPU:36, one launch (start us, length us, event | category | flops | bytes accessed | tf_op | source)
XLA Modules:
  0.0 239.0 jit_solution(4529518730610056680)
XLA Ops:
  0.0 0.8 copy.8.ids_ref
  0.8 0.0 copy-start.1
  0.8 0.0 copy-start.8
  0.8 1.3 copy.7.router_ref
  2.1 0.0 copy-start
  2.1 1.1 copy-done
  3.2 0.7 copy-done.7
  3.9 1.0 prepare.2
  5.0 0.8 copy-done.4
  5.8 0.6 copy-done.9
  6.3 0.6 copy-done.11
  7.0 14.3 %all-to-all-start = ((bf16[8,16,16,128]{3,2,1,0:T(8,128)(2,1)}), bf16[8,16,16,128]{3,2,1,0:T(8,128)(2,1)}, u32[]{:S(2)}, u32[]{:S(2)}) async-start(bf16[8,16,16,128]{3,2,1,0:T(8,128)(2,1)} %copy-done.4), calls=%async_computation | async-start | bytes 1048576 | tf_op jit(solution)/shard_map/all_to_all | solution.py:236
  21.3 0.0 copy-done.8
  21.3 1.0 prepare.3
  22.3 0.0 copy-start.3
  22.3 0.8 copy-done.3
  23.1 26.2 %all-to-all-done.own_ref = bf16[8,16,16,128]{3,2,1,0:T(8,128)(2,1)} async-done(((bf16[8,16,16,128]{3,2,1,0:T(8,128)(2,1)}), bf16[8,16,16,128]{3,2,1,0:T(8,128)(2,1)}, u32[]{:S(2)}, u32[]{:S(2)}) %all-to-all-start) | async-done | bytes 524320 | tf_op jit(solution)/shard_map/all_to_all | solution.py:236
  49.3 7.4 %all-to-all-start.2 = ((bf16[8,16,16,128]{3,2,1,0:T(8,128)(2,1)}), bf16[8,16,16,128]{3,2,1,0:T(8,128)(2,1)}, u32[]{:S(2)}, u32[]{:S(2)}) async-start(bf16[8,16,16,128]{3,2,1,0:T(8,128)(2,1)} %copy-done.3), calls=%async_computation.2 | async-start | bytes 1048576 | tf_op jit(solution)/shard_map/all_to_all | solution.py:236
  56.8 2.9 %collective-permute-start.1 = (bf16[8,16,16,128]{3,2,1,0:T(8,128)(2,1)}, bf16[8,16,16,128]{3,2,1,0:T(8,128)(2,1)S(1)}, u32[]{:S(2)}, u32[]{:S(2)}) collective-permute-start(bf16[8,16,16,128]{3,2,1,0:T(8,128)(2,1)} %all-to-all-done.own_ref), channel_id=1, source_target_pairs={{0,2},{1,3},{2,0},{3,1},{4,6},{5,7},{6,4},{7,5},{8,10},{9,11},{10,... | collective-permute-start | bytes 1572872 | tf_op jit(solution)/shard_map/ppermute | solution.py:228
  59.7 1.9 collective-permute-start
  61.6 30.2 %collective-permute-done.1.chip_ref = bf16[8,16,16,128]{3,2,1,0:T(8,128)(2,1)S(1)} collective-permute-done((bf16[8,16,16,128]{3,2,1,0:T(8,128)(2,1)}, bf16[8,16,16,128]{3,2,1,0:T(8,128)(2,1)S(1)}, u32[]{:S(2)}, u32[]{:S(2)}) %collective-permute-start.1) | collective-permute-done | bytes 524320 | tf_op jit(solution)/shard_map/ppermute | solution.py:228
  91.8 1.9 collective-permute-start.2
  93.7 0.0 collective-permute-done.core_ref
  93.7 1.9 collective-permute-done.2.both_ref
  95.6 5.2 %expert.2 = (bf16[8,16,16,128]{3,2,1,0:T(8,128)(2,1)S(1)}, bf16[8,16,16,128]{3,2,1,0:T(8,128)(2,1)S(1)}, bf16[8,16,16,128]{3,2,1,0:T(8,128)(2,1)S(1)}, bf16[8,16,16,128]{3,2,1,0:T(8,128)(2,1)}) custom-call(bf16[8,16,16,128]{3,2,1,0:T(8,128)(2,1)} %all-to-all-done.own_ref, bf16[8,16,16,128]{3,2,1,0:T(8,128)(2,1)S(1)} %collective-permute-done.core_ref, ...), custom_call_target="tpu_custom_call" | custom-call | tf_op jit(solution)/shard_map/expert/pallas_call | solution.py:190
  100.8 0.8 copy-done.5
  101.6 0.8 copy-done.13
  102.4 2.0 collective-permute-start.4
  104.4 0.0 all-to-all-done.2.own_ref
  104.5 3.5 %collective-permute-start.7 = (bf16[8,16,16,128]{3,2,1,0:T(8,128)(2,1)}, bf16[8,16,16,128]{3,2,1,0:T(8,128)(2,1)}, u32[]{:S(2)}, u32[]{:S(2)}) collective-permute-start(bf16[8,16,16,128]{3,2,1,0:T(8,128)(2,1)} %all-to-all-done.2.own_ref), channel_id=1, source_target_pairs={{0,2},{1,3},{2,0},{3,1},{4,6},{5,7},{6,4},{7,5},{8,10},{9,11},{10,... | collective-permute-start | bytes 1572872 | tf_op jit(solution)/shard_map/ppermute | solution.py:228
  107.9 2.0 collective-permute-start.3
  109.9 0.0 collective-permute-done.4
  109.9 1.2 add_convert_fusion.4
  111.1 2.5 %collective-permute-start.5 = (bf16[8,16,16,128]{3,2,1,0:T(8,128)(2,1)S(1)}, bf16[8,16,16,128]{3,2,1,0:T(8,128)(2,1)S(1)}, u32[]{:S(2)}, u32[]{:S(2)}) collective-permute-start(bf16[8,16,16,128]{3,2,1,0:T(8,128)(2,1)S(1)} %add_convert_fusion.4), channel_id=1, source_target_pairs={{0,2},{1,3},{2,0},{3,1},{4,6},{5,7},{6,4},{7,5},{8,10},{9,11},{10,... | collective-permute-start | bytes 1572872 | tf_op jit(solution)/shard_map/ppermute | solution.py:228
  113.7 2.1 collective-permute-start.6
  115.7 5.8 %collective-permute-done.7.chip_ref = bf16[8,16,16,128]{3,2,1,0:T(8,128)(2,1)} collective-permute-done((bf16[8,16,16,128]{3,2,1,0:T(8,128)(2,1)}, bf16[8,16,16,128]{3,2,1,0:T(8,128)(2,1)}, u32[]{:S(2)}, u32[]{:S(2)}) %collective-permute-start.7) | collective-permute-done | bytes 524320 | tf_op jit(solution)/shard_map/ppermute | solution.py:228
  121.6 1.9 collective-permute-start.8
  123.5 0.0 collective-permute-done.3
  123.5 8.7 %collective-permute-done.5 = bf16[8,16,16,128]{3,2,1,0:T(8,128)(2,1)S(1)} collective-permute-done((bf16[8,16,16,128]{3,2,1,0:T(8,128)(2,1)S(1)}, bf16[8,16,16,128]{3,2,1,0:T(8,128)(2,1)S(1)}, u32[]{:S(2)}, u32[]{:S(2)}) %collective-permute-start.5) | collective-permute-done | bytes 524320 | tf_op jit(solution)/shard_map/ppermute | solution.py:228
  132.1 1.0 add_convert_fusion.3
  133.2 11.6 %all-to-all-start.1 = ((bf16[8,16,16,128]{3,2,1,0:T(8,128)(2,1)}), bf16[8,16,16,128]{3,2,1,0:T(8,128)(2,1)S(1)}, u32[]{:S(2)}, u32[]{:S(2)}) async-start(bf16[8,16,16,128]{3,2,1,0:T(8,128)(2,1)} %add_convert_fusion.3), calls=%async_computation.1 | async-start | bytes 1048576 | tf_op jit(solution)/shard_map/all_to_all | solution.py:236
  144.8 0.0 collective-permute-done.6.core_ref
  144.8 0.0 collective-permute-done.8.both_ref
  144.8 4.9 %expert.3 = (bf16[8,16,16,128]{3,2,1,0:T(8,128)(2,1)S(1)}, bf16[8,16,16,128]{3,2,1,0:T(8,128)(2,1)S(1)}, bf16[8,16,16,128]{3,2,1,0:T(8,128)(2,1)S(1)}, bf16[8,16,16,128]{3,2,1,0:T(8,128)(2,1)S(1)}) custom-call(bf16[8,16,16,128]{3,2,1,0:T(8,128)(2,1)} %all-to-all-done.2.own_ref, bf16[8,16,16,128]{3,2,1,0:T(8,128)(2,1)} %collective-permute-done.6.core_ref, ...), custom_call_target="tpu_custom_call" | custom-call | tf_op jit(solution)/shard_map/expert/pallas_call | solution.py:190
  149.7 1.9 collective-permute-start.10
  151.6 2.4 %collective-permute-start.9 = (bf16[8,16,16,128]{3,2,1,0:T(8,128)(2,1)S(1)}, bf16[8,16,16,128]{3,2,1,0:T(8,128)(2,1)S(1)}, u32[]{:S(2)}, u32[]{:S(2)}) collective-permute-start(bf16[8,16,16,128]{3,2,1,0:T(8,128)(2,1)S(1)} %get-tuple-element.28), channel_id=1, source_target_pairs={{0,1},{1,0},{2,3},{3,2},{4,5},{5,4},{6,7},{7,6},{8,9},{9,8},{10,11... | collective-permute-start | bytes 1572872 | tf_op jit(solution)/shard_map/ppermute | solution.py:228
  154.0 0.0 collective-permute-done.10
  154.0 0.1 add_convert_fusion.1
  154.2 0.0 copy-start.10
  154.2 0.0 copy-start.12
  154.2 2.7 %collective-permute-start.11 = (bf16[8,16,16,128]{3,2,1,0:T(8,128)(2,1)S(1)}, bf16[8,16,16,128]{3,2,1,0:T(8,128)(2,1)S(1)}, u32[]{:S(2)}, u32[]{:S(2)}) collective-permute-start(bf16[8,16,16,128]{3,2,1,0:T(8,128)(2,1)S(1)} %add_convert_fusion.1), channel_id=1, source_target_pairs={{0,2},{1,3},{2,0},{3,1},{4,6},{5,7},{6,4},{7,5},{8,10},{9,11},{10,... | collective-permute-start | bytes 1572872 | tf_op jit(solution)/shard_map/ppermute | solution.py:228
  156.9 0.0 collective-permute-done.9
  156.9 23.7 %collective-permute-done.11 = bf16[8,16,16,128]{3,2,1,0:T(8,128)(2,1)S(1)} collective-permute-done((bf16[8,16,16,128]{3,2,1,0:T(8,128)(2,1)S(1)}, bf16[8,16,16,128]{3,2,1,0:T(8,128)(2,1)S(1)}, u32[]{:S(2)}, u32[]{:S(2)}) %collective-permute-start.11) | collective-permute-done | bytes 524320 | tf_op jit(solution)/shard_map/ppermute | solution.py:228
  180.6 1.0 add_convert_fusion
  181.6 0.0 all-to-all-done.1.packet_ref
  181.6 10.5 %all-to-all-start.3 = ((bf16[8,16,16,128]{3,2,1,0:T(8,128)(2,1)}), bf16[8,16,16,128]{3,2,1,0:T(8,128)(2,1)S(1)}, u32[]{:S(2)}, u32[]{:S(2)}) async-start(bf16[8,16,16,128]{3,2,1,0:T(8,128)(2,1)} %add_convert_fusion), calls=%async_computation.3 | async-start | bytes 1048576 | tf_op jit(solution)/shard_map/all_to_all | solution.py:236
  192.1 0.5 finish.2
  192.6 4.9 %collective-permute-start.13 = (bf16[48,3584]{1,0:T(8,128)(2,1)S(1)}, bf16[48,3584]{1,0:T(8,128)(2,1)S(1)}, u32[]{:S(2)}, u32[]{:S(2)}) collective-permute-start(bf16[48,3584]{1,0:T(8,128)(2,1)S(1)} %finish.2), channel_id=1, source_target_pairs={{32,0},{64,32},{96,64},{128,96},{160,128},{192,160},{224,192},{256... | collective-permute-start | bytes 1032200 | tf_op jit(solution)/shard_map/ppermute | solution.py:224
  197.5 26.2 %all-to-all-done.3.packet_ref = bf16[8,16,16,128]{3,2,1,0:T(8,128)(2,1)S(1)} async-done(((bf16[8,16,16,128]{3,2,1,0:T(8,128)(2,1)}), bf16[8,16,16,128]{3,2,1,0:T(8,128)(2,1)S(1)}, u32[]{:S(2)}, u32[]{:S(2)}) %all-to-all-start.3) | async-done | bytes 524320 | tf_op jit(solution)/shard_map/all_to_all | solution.py:236
  223.7 0.5 finish.3
  224.2 3.5 %collective-permute-start.12 = (bf16[48,3584]{1,0:T(8,128)(2,1)S(1)}, bf16[48,3584]{1,0:T(8,128)(2,1)S(1)}, u32[]{:S(2)}, u32[]{:S(2)}) collective-permute-start(bf16[48,3584]{1,0:T(8,128)(2,1)S(1)} %finish.3), channel_id=1, source_target_pairs={{0,32},{32,64},{64,96},{96,128},{128,160},{160,192},{192,224},{224... | collective-permute-start | bytes 1032200 | tf_op jit(solution)/shard_map/ppermute | solution.py:224
  227.7 0.0 collective-permute-done.13
  227.8 10.3 %collective-permute-done.12 = bf16[48,3584]{1,0:T(8,128)(2,1)S(1)} collective-permute-done((bf16[48,3584]{1,0:T(8,128)(2,1)S(1)}, bf16[48,3584]{1,0:T(8,128)(2,1)S(1)}, u32[]{:S(2)}, u32[]{:S(2)}) %collective-permute-start.12) | collective-permute-done | bytes 344096 | tf_op jit(solution)/shard_map/ppermute | solution.py:224
  238.1 0.9 maximum_bitcast_fusion
  (15 shorter events, 0.1 us)
Async XLA Ops:
  0.8 20.5 %copy-start.1 = (bf16[2,1,48,3584]{3,2,1,0:T(8,128)(2,1)S(1)}, bf16[2,1,48,3584]{3,2,1,0:T(8,128)(2,1)}, u32[]{:S(2)}) copy-start(bf16[2,1,48,3584]{3,2,1,0:T(8,128)(2,1)} %x_ref.7) | copy-start | bytes 2064388
  0.8 20.5 %copy-start.8 = (bf16[1,3584]{1,0:T(2,128)(2,1)S(1)}, bf16[1,3584]{1,0:T(2,128)(2,1)}, u32[]{:S(2)}) copy-start(bf16[1,3584]{1,0:T(2,128)(2,1)} %gain_ref.3) | copy-start | bytes 21508
  2.1 1.1 copy-start
  3.2 0.7 copy-start.7
  5.0 0.8 copy-start.4
  5.8 0.6 copy-start.9
  6.3 0.6 copy-start.11
  7.0 88.7 %copy-start.2 = (bf16[1,3584,256]{2,1,0:T(8,128)(2,1)S(1)}, bf16[1,3584,256]{2,1,0:T(8,128)(2,1)}, u32[]{:S(2)}) copy-start(bf16[1,3584,256]{2,1,0:T(8,128)(2,1)} %up_ref.3) | copy-start | bytes 5505028
  7.0 42.4 %all-to-all-start = ((bf16[8,16,16,128]{3,2,1,0:T(8,128)(2,1)}), bf16[8,16,16,128]{3,2,1,0:T(8,128)(2,1)}, u32[]{:S(2)}, u32[]{:S(2)}) async-start(bf16[8,16,16,128]{3,2,1,0:T(8,128)(2,1)} %copy-done.4), calls=%async_computation | async-start | bytes 1048576 | tf_op jit(solution)/shard_map/all_to_all | solution.py:236
  22.3 0.8 copy-start.3
  49.3 55.1 %all-to-all-start.2 = ((bf16[8,16,16,128]{3,2,1,0:T(8,128)(2,1)}), bf16[8,16,16,128]{3,2,1,0:T(8,128)(2,1)}, u32[]{:S(2)}, u32[]{:S(2)}) async-start(bf16[8,16,16,128]{3,2,1,0:T(8,128)(2,1)} %copy-done.3), calls=%async_computation.2 | async-start | bytes 1048576 | tf_op jit(solution)/shard_map/all_to_all | solution.py:236
  56.8 35.1 %collective-permute-start.1 = (bf16[8,16,16,128]{3,2,1,0:T(8,128)(2,1)}, bf16[8,16,16,128]{3,2,1,0:T(8,128)(2,1)S(1)}, u32[]{:S(2)}, u32[]{:S(2)}) collective-permute-start(bf16[8,16,16,128]{3,2,1,0:T(8,128)(2,1)} %all-to-all-done.own_ref), channel_id=1, source_target_pairs={{0,2},{1,3},{2,0},{3,1},{4,6},{5,7},{6,4},{7,5},{8,10},{9,11},{10,... | collective-permute-start | bytes 1572872 | tf_op jit(solution)/shard_map/ppermute | solution.py:228
  59.7 34.1 %collective-permute-start = (bf16[8,16,16,128]{3,2,1,0:T(8,128)(2,1)}, bf16[8,16,16,128]{3,2,1,0:T(8,128)(2,1)S(1)}, u32[]{:S(2)}, u32[]{:S(2)}) collective-permute-start(bf16[8,16,16,128]{3,2,1,0:T(8,128)(2,1)} %all-to-all-done.own_ref), channel_id=1, source_target_pairs={{0,1},{1,0},{2,3},{3,2},{4,5},{5,4},{6,7},{7,6},{8,9},{9,8},{10,11... | collective-permute-start | bytes 1572872 | tf_op jit(solution)/shard_map/ppermute | solution.py:228
  91.8 3.8 %collective-permute-start.2 = (bf16[8,16,16,128]{3,2,1,0:T(8,128)(2,1)S(1)}, bf16[8,16,16,128]{3,2,1,0:T(8,128)(2,1)S(1)}, u32[]{:S(2)}, u32[]{:S(2)}) collective-permute-start(bf16[8,16,16,128]{3,2,1,0:T(8,128)(2,1)S(1)} %collective-permute-done.1.chip_ref), channel_id=1, source_target_pairs={{0,1},{1,0},{2,3},{3,2},{4,5},{5,4},{6,7},{7,6},{8,9},{9,8},{10,11... | collective-permute-start | bytes 1572872 | tf_op jit(solution)/shard_map/ppermute | solution.py:228
  100.8 0.8 copy-start.5
  101.6 0.8 copy-start.13
  102.4 7.5 %collective-permute-start.4 = (bf16[8,16,16,128]{3,2,1,0:T(8,128)(2,1)}, bf16[8,16,16,128]{3,2,1,0:T(8,128)(2,1)}, u32[]{:S(2)}, u32[]{:S(2)}) collective-permute-start(bf16[8,16,16,128]{3,2,1,0:T(8,128)(2,1)} %get-tuple-element.23), channel_id=1, source_target_pairs={{0,1},{1,0},{2,3},{3,2},{4,5},{5,4},{6,7},{7,6},{8,9},{9,8},{10,11... | collective-permute-start | bytes 1572872 | tf_op jit(solution)/shard_map/ppermute | solution.py:228
  104.5 27.7 %copy-start.6 = (bf16[8,16,16,128]{3,2,1,0:T(8,128)(2,1)S(1)}, bf16[8,16,16,128]{3,2,1,0:T(8,128)(2,1)}, u32[]{:S(2)}) copy-start(bf16[8,16,16,128]{3,2,1,0:T(8,128)(2,1)} %copy-done.5) | copy-start | bytes 1572868
  104.5 17.1 %collective-permute-start.7 = (bf16[8,16,16,128]{3,2,1,0:T(8,128)(2,1)}, bf16[8,16,16,128]{3,2,1,0:T(8,128)(2,1)}, u32[]{:S(2)}, u32[]{:S(2)}) collective-permute-start(bf16[8,16,16,128]{3,2,1,0:T(8,128)(2,1)} %all-to-all-done.2.own_ref), channel_id=1, source_target_pairs={{0,2},{1,3},{2,0},{3,1},{4,6},{5,7},{6,4},{7,5},{8,10},{9,11},{10,... | collective-permute-start | bytes 1572872 | tf_op jit(solution)/shard_map/ppermute | solution.py:228
  107.9 15.6 %collective-permute-start.3 = (bf16[8,16,16,128]{3,2,1,0:T(8,128)(2,1)}, bf16[8,16,16,128]{3,2,1,0:T(8,128)(2,1)S(1)}, u32[]{:S(2)}, u32[]{:S(2)}) collective-permute-start(bf16[8,16,16,128]{3,2,1,0:T(8,128)(2,1)} %copy-done.13), channel_id=1, source_target_pairs={{0,1},{1,0},{2,3},{3,2},{4,5},{5,4},{6,7},{7,6},{8,9},{9,8},{10,11... | collective-permute-start | bytes 1572872 | tf_op jit(solution)/shard_map/ppermute | solution.py:228
  111.1 21.0 %collective-permute-start.5 = (bf16[8,16,16,128]{3,2,1,0:T(8,128)(2,1)S(1)}, bf16[8,16,16,128]{3,2,1,0:T(8,128)(2,1)S(1)}, u32[]{:S(2)}, u32[]{:S(2)}) collective-permute-start(bf16[8,16,16,128]{3,2,1,0:T(8,128)(2,1)S(1)} %add_convert_fusion.4), channel_id=1, source_target_pairs={{0,2},{1,3},{2,0},{3,1},{4,6},{5,7},{6,4},{7,5},{8,10},{9,11},{10,... | collective-permute-start | bytes 1572872 | tf_op jit(solution)/shard_map/ppermute | solution.py:228
  113.7 31.1 %collective-permute-start.6 = (bf16[8,16,16,128]{3,2,1,0:T(8,128)(2,1)}, bf16[8,16,16,128]{3,2,1,0:T(8,128)(2,1)}, u32[]{:S(2)}, u32[]{:S(2)}) collective-permute-start(bf16[8,16,16,128]{3,2,1,0:T(8,128)(2,1)} %all-to-all-done.2.own_ref), channel_id=1, source_target_pairs={{0,1},{1,0},{2,3},{3,2},{4,5},{5,4},{6,7},{7,6},{8,9},{9,8},{10,11... | collective-permute-start | bytes 1572872 | tf_op jit(solution)/shard_map/ppermute | solution.py:228
  121.6 23.2 %collective-permute-start.8 = (bf16[8,16,16,128]{3,2,1,0:T(8,128)(2,1)}, bf16[8,16,16,128]{3,2,1,0:T(8,128)(2,1)}, u32[]{:S(2)}, u32[]{:S(2)}) collective-permute-start(bf16[8,16,16,128]{3,2,1,0:T(8,128)(2,1)} %collective-permute-done.7.chip_ref), channel_id=1, source_target_pairs={{0,1},{1,0},{2,3},{3,2},{4,5},{5,4},{6,7},{7,6},{8,9},{9,8},{10,11... | collective-permute-start | bytes 1572872 | tf_op jit(solution)/shard_map/ppermute | solution.py:228
  133.2 48.4 %all-to-all-start.1 = ((bf16[8,16,16,128]{3,2,1,0:T(8,128)(2,1)}), bf16[8,16,16,128]{3,2,1,0:T(8,128)(2,1)S(1)}, u32[]{:S(2)}, u32[]{:S(2)}) async-start(bf16[8,16,16,128]{3,2,1,0:T(8,128)(2,1)} %add_convert_fusion.3), calls=%async_computation.1 | async-start | bytes 1048576 | tf_op jit(solution)/shard_map/all_to_all | solution.py:236
  149.7 4.3 %collective-permute-start.10 = (bf16[8,16,16,128]{3,2,1,0:T(8,128)(2,1)S(1)}, bf16[8,16,16,128]{3,2,1,0:T(8,128)(2,1)S(1)}, u32[]{:S(2)}, u32[]{:S(2)}) collective-permute-start(bf16[8,16,16,128]{3,2,1,0:T(8,128)(2,1)S(1)} %get-tuple-element.30), channel_id=1, source_target_pairs={{0,1},{1,0},{2,3},{3,2},{4,5},{5,4},{6,7},{7,6},{8,9},{9,8},{10,11... | collective-permute-start | bytes 1572872 | tf_op jit(solution)/shard_map/ppermute | solution.py:228
  151.6 5.3 %collective-permute-start.9 = (bf16[8,16,16,128]{3,2,1,0:T(8,128)(2,1)S(1)}, bf16[8,16,16,128]{3,2,1,0:T(8,128)(2,1)S(1)}, u32[]{:S(2)}, u32[]{:S(2)}) collective-permute-start(bf16[8,16,16,128]{3,2,1,0:T(8,128)(2,1)S(1)} %get-tuple-element.28), channel_id=1, source_target_pairs={{0,1},{1,0},{2,3},{3,2},{4,5},{5,4},{6,7},{7,6},{8,9},{9,8},{10,11... | collective-permute-start | bytes 1572872 | tf_op jit(solution)/shard_map/ppermute | solution.py:228
  154.2 37.9 %copy-start.10 = (f32[48,128]{1,0:T(8,128)S(1)}, f32[48,128]{1,0:T(8,128)}, u32[]{:S(2)}) copy-start(f32[48,128]{1,0:T(8,128)} %copy-done.9) | copy-start | bytes 73732
  154.2 37.9 %copy-start.12 = (f32[48,128]{1,0:T(8,128)S(1)}, f32[48,128]{1,0:T(8,128)}, u32[]{:S(2)}) copy-start(f32[48,128]{1,0:T(8,128)} %copy-done.11) | copy-start | bytes 73732
  154.2 26.4 %collective-permute-start.11 = (bf16[8,16,16,128]{3,2,1,0:T(8,128)(2,1)S(1)}, bf16[8,16,16,128]{3,2,1,0:T(8,128)(2,1)S(1)}, u32[]{:S(2)}, u32[]{:S(2)}) collective-permute-start(bf16[8,16,16,128]{3,2,1,0:T(8,128)(2,1)S(1)} %add_convert_fusion.1), channel_id=1, source_target_pairs={{0,2},{1,3},{2,0},{3,1},{4,6},{5,7},{6,4},{7,5},{8,10},{9,11},{10,... | collective-permute-start | bytes 1572872 | tf_op jit(solution)/shard_map/ppermute | solution.py:228
  181.6 42.1 %all-to-all-start.3 = ((bf16[8,16,16,128]{3,2,1,0:T(8,128)(2,1)}), bf16[8,16,16,128]{3,2,1,0:T(8,128)(2,1)S(1)}, u32[]{:S(2)}, u32[]{:S(2)}) async-start(bf16[8,16,16,128]{3,2,1,0:T(8,128)(2,1)} %add_convert_fusion), calls=%async_computation.3 | async-start | bytes 1048576 | tf_op jit(solution)/shard_map/all_to_all | solution.py:236
  192.6 35.1 %collective-permute-start.13 = (bf16[48,3584]{1,0:T(8,128)(2,1)S(1)}, bf16[48,3584]{1,0:T(8,128)(2,1)S(1)}, u32[]{:S(2)}, u32[]{:S(2)}) collective-permute-start(bf16[48,3584]{1,0:T(8,128)(2,1)S(1)} %finish.2), channel_id=1, source_target_pairs={{32,0},{64,32},{96,64},{128,96},{160,128},{192,160},{224,192},{256... | collective-permute-start | bytes 1032200 | tf_op jit(solution)/shard_map/ppermute | solution.py:224
  224.2 13.8 %collective-permute-start.12 = (bf16[48,3584]{1,0:T(8,128)(2,1)S(1)}, bf16[48,3584]{1,0:T(8,128)(2,1)S(1)}, u32[]{:S(2)}, u32[]{:S(2)}) collective-permute-start(bf16[48,3584]{1,0:T(8,128)(2,1)S(1)} %finish.3), channel_id=1, source_target_pairs={{0,32},{32,64},{64,96},{96,128},{128,160},{160,192},{192,224},{224... | collective-permute-start | bytes 1032200 | tf_op jit(solution)/shard_map/ppermute | solution.py:224

commit v2 on v1

--- a/solution.py
+++ b/solution.py
@@ -8,6 +8,7 @@
 SPLIT = 4
 LANES = 128
 MAIN = 8
+PARTS = 2
 
 epsilon = 1e-06
 route_scale = 2.5
@@ -57,17 +58,30 @@
     return jnp.dot(gather, tail, preferred_element_type=jnp.float32)
 
 
-def prepare_kernel(x_ref, gain_ref, router_ref, ids_ref, packet_ref, gate_ref, row_ref):
+def prepare_kernel(x_ref, gain_ref, router_ref, ids_ref, packets_ref, gate_ref, row_ref):
+    for direction in range(x_ref.shape[0]):
+        prepare_direction(
+            x_ref.at[direction],
+            gain_ref,
+            router_ref,
+            ids_ref.at[0, direction],
+            packets_ref.at[:, direction],
+            gate_ref.at[direction],
+            row_ref.at[direction],
+        )
+
+
+def prepare_direction(x_ref, gain_ref, router_ref, ids_ref, packet_ref, gate_ref, row_ref):
     experts = packet_ref.shape[0]
     pairs = packet_ref.shape[1] - 2
-    tokens = x_ref.shape[2]
-    x = x_ref[0, 0].astype(jnp.float32)
+    tokens = x_ref.shape[1]
+    x = x_ref[0].astype(jnp.float32)
     mean_square = jnp.mean(x * x, axis=-1, keepdims=True)
     normed = (x * lax.rsqrt(mean_square + epsilon) * gain_ref[...].astype(jnp.float32)).astype(
         jnp.bfloat16
     )
     logits = jnp.dot(normed, router_ref[0], preferred_element_type=jnp.float32)
-    chosen = ids_ref[0, 0]
+    chosen = ids_ref[...]
     one_hot = (iota((tokens, experts), 1) == chosen).astype(jnp.float32)
     gate = route_scale * jax.nn.sigmoid(jnp.sum(logits * one_hot, axis=-1, keepdims=True))
     earlier = (iota((tokens, tokens), 1) < iota((tokens, tokens), 0)).astype(jnp.float32)
@@ -129,10 +143,21 @@
         write_tail(ref, jnp.concatenate(tail_chunks[index], axis=0).astype(jnp.bfloat16))
 
 
-def finish_kernel(x_ref, packet_ref, gate_ref, row_ref, out_ref):
+def finish_kernel(x_ref, packets_ref, gate_ref, row_ref, up_ref, down_ref):
+    for direction, out_ref in enumerate((up_ref, down_ref)):
+        finish_direction(
+            x_ref.at[direction],
+            packets_ref.at[:, direction],
+            gate_ref.at[direction],
+            row_ref.at[direction],
+            out_ref,
+        )
+
+
+def finish_direction(x_ref, packet_ref, gate_ref, row_ref, out_ref):
     experts = packet_ref.shape[0]
     pairs = packet_ref.shape[1] - 2
-    tokens = x_ref.shape[2]
+    tokens = x_ref.shape[1]
     rows = experts * (MAIN + 1)
     row = row_ref[:, :1]
     gate = gate_ref[:, :1]
@@ -149,7 +174,7 @@
         routed = jnp.dot(
             choose_main, read_pair(packet_ref, pair), preferred_element_type=jnp.float32
         ) + jnp.dot(choose_tail, tail_pair, preferred_element_type=jnp.float32)
-        x = x_ref[0, 0, :, columns].astype(jnp.float32)
+        x = x_ref[0, :, columns].astype(jnp.float32)
         out_ref[:, columns] = (x + gate * routed).astype(jnp.bfloat16)
 
 
@@ -161,22 +186,17 @@
     return pl.BlockSpec(array.shape, lambda _: (0,) * array.ndim)
 
 
-def prepare(direction, carried, gain, router, ids, experts):
-    tokens, width = carried.shape[2:]
+def prepare(carried, gain, router, ids, experts):
+    directions, _, tokens, width = carried.shape
     blocks = width // 256 + 2
-    packet = jax.ShapeDtypeStruct((experts, blocks, 16, LANES), jnp.bfloat16)
-    notes = jax.ShapeDtypeStruct((tokens, LANES), jnp.float32)
+    packets = jax.ShapeDtypeStruct((experts, directions, blocks, 16, LANES), jnp.bfloat16)
+    notes = jax.ShapeDtypeStruct((directions, tokens, LANES), jnp.float32)
     return pl.pallas_call(
         prepare_kernel,
         grid=(1,),
-        out_shape=(packet, notes, notes),
-        in_specs=[
-            pl.BlockSpec((1, 1, tokens, width), lambda _: (direction, 0, 0, 0)),
-            whole(gain),
-            whole(router),
-            pl.BlockSpec((1, 1, tokens, 1), lambda _: (0, direction, 0, 0)),
-        ],
-        out_specs=(whole(packet), whole(notes), whole(notes)),
+        out_shape=(packets, notes, notes),
+        in_specs=[whole(a) for a in (carried, gain, router, ids)],
+        out_specs=(whole(packets), whole(notes), whole(notes)),
         compiler_params=params(),
         name="prepare",
     )(carried, gain, router, ids)
@@ -199,23 +219,18 @@
     )(own, core, chip, both, up, down)
 
 
-def finish(direction, carried, packet, gate, row):
+def finish(carried, packets, gate, row):
     tokens, width = carried.shape[2:]
     out = jax.ShapeDtypeStruct((tokens, width), jnp.bfloat16)
     return pl.pallas_call(
         finish_kernel,
         grid=(1,),
-        out_shape=out,
-        in_specs=[
-            pl.BlockSpec((1, 1, tokens, width), lambda _: (direction, 0, 0, 0)),
-            whole(packet),
-            whole(gate),
-            whole(row),
-        ],
-        out_specs=whole(out),
+        out_shape=(out, out),
+        in_specs=[whole(a) for a in (carried, packets, gate, row)],
+        out_specs=(whole(out), whole(out)),
         compiler_params=params(),
         name="finish",
-    )(carried, packet, gate, row)
+    )(carried, packets, gate, row)
 
 
 def passed_along(block, axis, distance):
@@ -244,23 +259,21 @@
 
 def per_device(carried, norm_gain, router, w_up, w_down, expert_ids):
     experts = lax.axis_size("expert") // SPLIT
-    layer_outputs = []
-    prepared = [
-        prepare(direction, carried, norm_gain, router, expert_ids, experts)
-        for direction in range(2)
-    ]
-    for direction in range(2):
-        packet, gate, row = prepared[direction]
-        own = exchanged(packet)
+    packets, gate, row = prepare(carried, norm_gain, router, expert_ids, experts)
+    received = exchanged(packets)
+    peers = experts // PARTS
+    totals = []
+    for part in range(PARTS):
+        own = received[part * peers : (part + 1) * peers].reshape(-1, *packets.shape[2:])
         chip = swapped(own, 2)
         core = swapped(own, 1)
         both = swapped(chip, 1)
         for_own, for_core, for_chip, for_both = run_expert(own, core, chip, both, w_up, w_down)
         own_sum = added(for_own, swapped(for_core, 1))
         chip_sum = added(for_chip, swapped(for_both, 1))
-        total = added(own_sum, swapped(chip_sum, 2))
-        returned = exchanged(total)
-        layer_outputs.append(finish(direction, carried, returned, gate, row))
+        totals.append(added(own_sum, swapped(chip_sum, 2)).reshape(peers, *packets.shape[1:]))
+    returned = exchanged(jnp.concatenate(totals, axis=0))
+    layer_outputs = finish(carried, returned, gate, row)
     section_index = lax.axis_index("section")
     last_section = lax.axis_size("section") - 1
     from_below = passed_along(layer_outputs[0], "section", 1)

time: 240 us -> 220 us (0.917)
  the two profiles are of different devices: /device:TPU:36 before, /device:TPU:24 now
where the time goes in v2:
time: 220 us; the launch traced here: 215 us
  blocking collectives  123 us (56%)
  waiting for transfers between devices  40.2 us (18%)
  starting transfers between devices  34.8 us (16%)
  Pallas kernels  11.1 us (5%)
  local copies, waits for them, and re-layouts  4.07 us (2%)
    all_to_all x2, blocking collectives, exchanged(): lax.all_to_all(packet, 'expert', split_axis=0, concat_axis=0, axis_index_...  123 us
    ppermute x12, waiting for transfers between devices, swapped(): lax.ppermute(block, 'expert', [(i, i ^ bit) for i in range(lax.axis_size(...  31.5 us
    ppermute x12, starting transfers between devices, swapped(): lax.ppermute(block, 'expert', [(i, i ^ bit) for i in range(lax.axis_size(...  29 us
    ppermute x2, waiting for transfers between devices, passed_along(): return lax.ppermute(block, axis, route)  8.68 us
    pallas_call x2, Pallas kernels, run_expert(): pl.pallas_call(expert_kernel, grid=(1,), out_shape=(packet,) * 4, in_spec...  8.48 us
    ppermute x2, starting transfers between devices, passed_along(): return lax.ppermute(block, axis, route)  5.84 us
  transfers between devices with their start and end apart: 14, of which 6 were waited for; matrix products, arithmetic and copies ran while one was open for 0% of the time, Pallas kernels for 4%

profile of v2, /device:TPU:24, one launch (start us, length us, event | category | flops | bytes accessed | tf_op | source)
XLA Modules:
  0.0 215.5 jit_solution(5803883380496039753)
XLA Ops:
  0.0 1.2 copy.7.router_ref
  1.2 0.8 copy.8.ids_ref
  2.0 0.0 copy-start.1
  2.0 1.1 copy-done.1
  3.1 0.0 copy-start.3
  3.1 0.7 copy-done.3
  3.8 1.7 prepare.1
  5.6 0.0 copy-start
  5.6 64.7 %all_to_all.10 = bf16[8,2,16,16,128]{4,3,2,1,0:T(8,128)(2,1)S(1)} all-to-all(bf16[8,2,16,16,128]{4,3,2,1,0:T(8,128)(2,1)S(1)} %get-tuple-element.18), channel_id=1, replica_groups={{0,4,8,12,16,20,24,28},{1,5,9,13,17,21,25,29},{2,6,10,14,18,22,26,30},{..., dimensions={0} | all-to-all | bytes 2097152 | tf_op jit(solution)/shard_map/all_to_all | solution.py:251
  70.3 0.2 fusion
  70.5 4.4 %collective-permute-start.1 = (bf16[8,16,16,128]{3,2,1,0:T(8,128)(2,1)S(1)}, bf16[8,16,16,128]{3,2,1,0:T(8,128)(2,1)S(1)}, u32[]{:S(2)}, u32[]{:S(2)}) collective-permute-start(bf16[8,16,16,128]{3,2,1,0:T(8,128)(2,1)S(1)} %bitcast.15), channel_id=1, source_target_pairs={{0,2},{1,3},{2,0},{3,1},{4,6},{5,7},{6,4},{7,5},{8,10},{9,11},{10,... | collective-permute-start | bytes 1572872 | tf_op jit(solution)/shard_map/ppermute | solution.py:243
  74.9 1.9 collective-permute-start.7
  76.9 1.9 collective-permute-start
  78.8 9.0 %collective-permute-done.1.chip_ref = bf16[8,16,16,128]{3,2,1,0:T(8,128)(2,1)S(1)} collective-permute-done((bf16[8,16,16,128]{3,2,1,0:T(8,128)(2,1)S(1)}, bf16[8,16,16,128]{3,2,1,0:T(8,128)(2,1)S(1)}, u32[]{:S(2)}, u32[]{:S(2)}) %collective-permute-start.1) | collective-permute-done | bytes 524320 | tf_op jit(solution)/shard_map/ppermute | solution.py:243
  87.8 1.9 collective-permute-start.2
  89.7 2.4 %collective-permute-start.6 = (bf16[8,16,16,128]{3,2,1,0:T(8,128)(2,1)S(1)}, bf16[8,16,16,128]{3,2,1,0:T(8,128)(2,1)S(1)}, u32[]{:S(2)}, u32[]{:S(2)}) collective-permute-start(bf16[8,16,16,128]{3,2,1,0:T(8,128)(2,1)S(1)} %bitcast.13), channel_id=1, source_target_pairs={{0,1},{1,0},{2,3},{3,2},{4,5},{5,4},{6,7},{7,6},{8,9},{9,8},{10,11... | collective-permute-start | bytes 1572872 | tf_op jit(solution)/shard_map/ppermute | solution.py:243
  92.1 3.8 %collective-permute-done.7.chip_ref = bf16[8,16,16,128]{3,2,1,0:T(8,128)(2,1)S(1)} collective-permute-done((bf16[8,16,16,128]{3,2,1,0:T(8,128)(2,1)S(1)}, bf16[8,16,16,128]{3,2,1,0:T(8,128)(2,1)S(1)}, u32[]{:S(2)}, u32[]{:S(2)}) %collective-permute-start.7) | collective-permute-done | bytes 524320 | tf_op jit(solution)/shard_map/ppermute | solution.py:243
  95.9 1.9 collective-permute-start.8
  97.8 0.0 collective-permute-done.core_ref
  97.8 0.0 collective-permute-done.2.both_ref
  97.8 0.0 copy-done
  97.8 4.2 %expert.2 = (bf16[8,16,16,128]{3,2,1,0:T(8,128)(2,1)S(1)}, bf16[8,16,16,128]{3,2,1,0:T(8,128)(2,1)S(1)}, bf16[8,16,16,128]{3,2,1,0:T(8,128)(2,1)S(1)}, bf16[8,16,16,128]{3,2,1,0:T(8,128)(2,1)S(1)}) custom-call(bf16[8,16,16,128]{3,2,1,0:T(8,128)(2,1)S(1)} %bitcast.17, bf16[8,16,16,128]{3,2,1,0:T(8,128)(2,1)S(1)} %collective-permute-done.core_ref, ...), custom_call_target="tpu_custom_call" | custom-call | tf_op jit(solution)/shard_map/expert/pallas_call | solution.py:210
  102.0 2.4 %collective-permute-start.4 = (bf16[8,16,16,128]{3,2,1,0:T(8,128)(2,1)S(1)}, bf16[8,16,16,128]{3,2,1,0:T(8,128)(2,1)S(1)}, u32[]{:S(2)}, u32[]{:S(2)}) collective-permute-start(bf16[8,16,16,128]{3,2,1,0:T(8,128)(2,1)S(1)} %get-tuple-element.22), channel_id=1, source_target_pairs={{0,1},{1,0},{2,3},{3,2},{4,5},{5,4},{6,7},{7,6},{8,9},{9,8},{10,11... | collective-permute-start | bytes 1572872 | tf_op jit(solution)/shard_map/ppermute | solution.py:243
  104.5 0.0 collective-permute-done.6.core_ref
  104.5 0.0 collective-permute-done.8.both_ref
  104.5 4.2 %expert.3 = (bf16[8,16,16,128]{3,2,1,0:T(8,128)(2,1)S(1)}, bf16[8,16,16,128]{3,2,1,0:T(8,128)(2,1)S(1)}, bf16[8,16,16,128]{3,2,1,0:T(8,128)(2,1)S(1)}, bf16[8,16,16,128]{3,2,1,0:T(8,128)(2,1)S(1)}) custom-call(bf16[8,16,16,128]{3,2,1,0:T(8,128)(2,1)S(1)} %bitcast.14, bf16[8,16,16,128]{3,2,1,0:T(8,128)(2,1)S(1)} %collective-permute-done.6.core_ref, ...), custom_call_target="tpu_custom_call" | custom-call | tf_op jit(solution)/shard_map/expert/pallas_call | solution.py:210
  108.7 1.9 collective-permute-start.10
  110.7 2.4 %collective-permute-start.3 = (bf16[8,16,16,128]{3,2,1,0:T(8,128)(2,1)S(1)}, bf16[8,16,16,128]{3,2,1,0:T(8,128)(2,1)S(1)}, u32[]{:S(2)}, u32[]{:S(2)}) collective-permute-start(bf16[8,16,16,128]{3,2,1,0:T(8,128)(2,1)S(1)} %get-tuple-element.20), channel_id=1, source_target_pairs={{0,1},{1,0},{2,3},{3,2},{4,5},{5,4},{6,7},{7,6},{8,9},{9,8},{10,11... | collective-permute-start | bytes 1572872 | tf_op jit(solution)/shard_map/ppermute | solution.py:243
  113.1 0.0 collective-permute-done.4
  113.1 0.1 add_convert_fusion.4
  113.2 3.6 %collective-permute-start.5 = (bf16[8,16,16,128]{3,2,1,0:T(8,128)(2,1)S(1)}, bf16[8,16,16,128]{3,2,1,0:T(8,128)(2,1)S(1)}, u32[]{:S(2)}, u32[]{:S(2)}) collective-permute-start(bf16[8,16,16,128]{3,2,1,0:T(8,128)(2,1)S(1)} %add_convert_fusion.4), channel_id=1, source_target_pairs={{0,2},{1,3},{2,0},{3,1},{4,6},{5,7},{6,4},{7,5},{8,10},{9,11},{10,... | collective-permute-start | bytes 1572872 | tf_op jit(solution)/shard_map/ppermute | solution.py:243
  116.8 1.9 collective-permute-start.9
  118.7 0.0 collective-permute-done.10
  118.7 0.1 add_convert_fusion.1
  118.9 2.3 %collective-permute-start.11 = (bf16[8,16,16,128]{3,2,1,0:T(8,128)(2,1)S(1)}, bf16[8,16,16,128]{3,2,1,0:T(8,128)(2,1)S(1)}, u32[]{:S(2)}, u32[]{:S(2)}) collective-permute-start(bf16[8,16,16,128]{3,2,1,0:T(8,128)(2,1)S(1)} %add_convert_fusion.1), channel_id=1, source_target_pairs={{0,2},{1,3},{2,0},{3,1},{4,6},{5,7},{6,4},{7,5},{8,10},{9,11},{10,... | collective-permute-start | bytes 1572872 | tf_op jit(solution)/shard_map/ppermute | solution.py:243
  121.2 0.0 collective-permute-done.3
  121.2 8.7 %collective-permute-done.5 = bf16[8,16,16,128]{3,2,1,0:T(8,128)(2,1)S(1)} collective-permute-done((bf16[8,16,16,128]{3,2,1,0:T(8,128)(2,1)S(1)}, bf16[8,16,16,128]{3,2,1,0:T(8,128)(2,1)S(1)}, u32[]{:S(2)}, u32[]{:S(2)}) %collective-permute-start.5) | collective-permute-done | bytes 524320 | tf_op jit(solution)/shard_map/ppermute | solution.py:243
  129.9 0.2 add_convert_fusion.3
  130.1 0.0 collective-permute-done.9
  130.1 10.1 %collective-permute-done.11 = bf16[8,16,16,128]{3,2,1,0:T(8,128)(2,1)S(1)} collective-permute-done((bf16[8,16,16,128]{3,2,1,0:T(8,128)(2,1)S(1)}, bf16[8,16,16,128]{3,2,1,0:T(8,128)(2,1)S(1)}, u32[]{:S(2)}, u32[]{:S(2)}) %collective-permute-start.11) | collective-permute-done | bytes 524320 | tf_op jit(solution)/shard_map/ppermute | solution.py:243
  140.2 0.2 add_convert_fusion
  140.4 0.0 copy-start.2
  140.4 0.1 pad_maximum_fusion
  140.5 58.5 %all_to_all.11.packets_ref = bf16[8,2,16,16,128]{4,3,2,1,0:T(8,128)(2,1)S(1)} all-to-all(bf16[8,2,16,16,128]{4,3,2,1,0:T(8,128)(2,1)S(1)} %pad_maximum_fusion), channel_id=1, replica_groups={{0,4,8,12,16,20,24,28},{1,5,9,13,17,21,25,29},{2,6,10,14,18,22,26,30},{..., dimensions={0} | all-to-all | bytes 2097152 | tf_op jit(solution)/shard_map/all_to_all | solution.py:251
  199.0 0.0 copy-done.2
  199.0 0.8 finish.1
  199.9 3.1 %collective-permute-start.12 = (bf16[48,3584]{1,0:T(8,128)(2,1)S(1)}, bf16[48,3584]{1,0:T(8,128)(2,1)S(1)}, u32[]{:S(2)}, u32[]{:S(2)}) collective-permute-start(bf16[48,3584]{1,0:T(8,128)(2,1)S(1)} %get-tuple-element.30), channel_id=1, source_target_pairs={{0,32},{32,64},{64,96},{96,128},{128,160},{160,192},{192,224},{224... | collective-permute-start | bytes 1032200 | tf_op jit(solution)/shard_map/ppermute | solution.py:239
  203.0 2.8 %collective-permute-start.13 = (bf16[48,3584]{1,0:T(8,128)(2,1)S(1)}, bf16[48,3584]{1,0:T(8,128)(2,1)S(1)}, u32[]{:S(2)}, u32[]{:S(2)}) collective-permute-start(bf16[48,3584]{1,0:T(8,128)(2,1)S(1)} %get-tuple-element.29), channel_id=1, source_target_pairs={{32,0},{64,32},{96,64},{128,96},{160,128},{192,160},{224,192},{256... | collective-permute-start | bytes 1032200 | tf_op jit(solution)/shard_map/ppermute | solution.py:239
  205.8 3.8 %collective-permute-done.12 = bf16[48,3584]{1,0:T(8,128)(2,1)S(1)} collective-permute-done((bf16[48,3584]{1,0:T(8,128)(2,1)S(1)}, bf16[48,3584]{1,0:T(8,128)(2,1)S(1)}, u32[]{:S(2)}, u32[]{:S(2)}) %collective-permute-start.12) | collective-permute-done | bytes 344096 | tf_op jit(solution)/shard_map/ppermute | solution.py:239
  209.6 4.9 %collective-permute-done.13 = bf16[48,3584]{1,0:T(8,128)(2,1)S(1)} collective-permute-done((bf16[48,3584]{1,0:T(8,128)(2,1)S(1)}, bf16[48,3584]{1,0:T(8,128)(2,1)S(1)}, u32[]{:S(2)}, u32[]{:S(2)}) %collective-permute-start.13) | collective-permute-done | bytes 344096 | tf_op jit(solution)/shard_map/ppermute | solution.py:239
  214.5 0.1 select_bitcast_fusion
  214.5 0.9 maximum_bitcast_fusion
  (1 shorter events, 0.0 us)
Async XLA Ops:
  2.0 1.1 copy-start.1
  3.1 0.7 copy-start.3
  5.6 92.2 %copy-start = (bf16[1,3584,256]{2,1,0:T(8,128)(2,1)S(1)}, bf16[1,3584,256]{2,1,0:T(8,128)(2,1)}, u32[]{:S(2)}) copy-start(bf16[1,3584,256]{2,1,0:T(8,128)(2,1)} %up_ref.3) | copy-start | bytes 5505028
  70.5 17.3 %collective-permute-start.1 = (bf16[8,16,16,128]{3,2,1,0:T(8,128)(2,1)S(1)}, bf16[8,16,16,128]{3,2,1,0:T(8,128)(2,1)S(1)}, u32[]{:S(2)}, u32[]{:S(2)}) collective-permute-start(bf16[8,16,16,128]{3,2,1,0:T(8,128)(2,1)S(1)} %bitcast.15), channel_id=1, source_target_pairs={{0,2},{1,3},{2,0},{3,1},{4,6},{5,7},{6,4},{7,5},{8,10},{9,11},{10,... | collective-permute-start | bytes 1572872 | tf_op jit(solution)/shard_map/ppermute | solution.py:243
  74.9 20.9 %collective-permute-start.7 = (bf16[8,16,16,128]{3,2,1,0:T(8,128)(2,1)S(1)}, bf16[8,16,16,128]{3,2,1,0:T(8,128)(2,1)S(1)}, u32[]{:S(2)}, u32[]{:S(2)}) collective-permute-start(bf16[8,16,16,128]{3,2,1,0:T(8,128)(2,1)S(1)} %bitcast.12), channel_id=1, source_target_pairs={{0,2},{1,3},{2,0},{3,1},{4,6},{5,7},{6,4},{7,5},{8,10},{9,11},{10,... | collective-permute-start | bytes 1572872 | tf_op jit(solution)/shard_map/ppermute | solution.py:243
  76.9 20.9 %collective-permute-start = (bf16[8,16,16,128]{3,2,1,0:T(8,128)(2,1)S(1)}, bf16[8,16,16,128]{3,2,1,0:T(8,128)(2,1)S(1)}, u32[]{:S(2)}, u32[]{:S(2)}) collective-permute-start(bf16[8,16,16,128]{3,2,1,0:T(8,128)(2,1)S(1)} %bitcast.16), channel_id=1, source_target_pairs={{0,1},{1,0},{2,3},{3,2},{4,5},{5,4},{6,7},{7,6},{8,9},{9,8},{10,11... | collective-permute-start | bytes 1572872 | tf_op jit(solution)/shard_map/ppermute | solution.py:243
  87.8 10.0 %collective-permute-start.2 = (bf16[8,16,16,128]{3,2,1,0:T(8,128)(2,1)S(1)}, bf16[8,16,16,128]{3,2,1,0:T(8,128)(2,1)S(1)}, u32[]{:S(2)}, u32[]{:S(2)}) collective-permute-start(bf16[8,16,16,128]{3,2,1,0:T(8,128)(2,1)S(1)} %collective-permute-done.1.chip_ref), channel_id=1, source_target_pairs={{0,1},{1,0},{2,3},{3,2},{4,5},{5,4},{6,7},{7,6},{8,9},{9,8},{10,11... | collective-permute-start | bytes 1572872 | tf_op jit(solution)/shard_map/ppermute | solution.py:243
  89.7 14.8 %collective-permute-start.6 = (bf16[8,16,16,128]{3,2,1,0:T(8,128)(2,1)S(1)}, bf16[8,16,16,128]{3,2,1,0:T(8,128)(2,1)S(1)}, u32[]{:S(2)}, u32[]{:S(2)}) collective-permute-start(bf16[8,16,16,128]{3,2,1,0:T(8,128)(2,1)S(1)} %bitcast.13), channel_id=1, source_target_pairs={{0,1},{1,0},{2,3},{3,2},{4,5},{5,4},{6,7},{7,6},{8,9},{9,8},{10,11... | collective-permute-start | bytes 1572872 | tf_op jit(solution)/shard_map/ppermute | solution.py:243
  95.9 8.6 %collective-permute-start.8 = (bf16[8,16,16,128]{3,2,1,0:T(8,128)(2,1)S(1)}, bf16[8,16,16,128]{3,2,1,0:T(8,128)(2,1)S(1)}, u32[]{:S(2)}, u32[]{:S(2)}) collective-permute-start(bf16[8,16,16,128]{3,2,1,0:T(8,128)(2,1)S(1)} %collective-permute-done.7.chip_ref), channel_id=1, source_target_pairs={{0,1},{1,0},{2,3},{3,2},{4,5},{5,4},{6,7},{7,6},{8,9},{9,8},{10,11... | collective-permute-start | bytes 1572872 | tf_op jit(solution)/shard_map/ppermute | solution.py:243
  102.0 11.0 %collective-permute-start.4 = (bf16[8,16,16,128]{3,2,1,0:T(8,128)(2,1)S(1)}, bf16[8,16,16,128]{3,2,1,0:T(8,128)(2,1)S(1)}, u32[]{:S(2)}, u32[]{:S(2)}) collective-permute-start(bf16[8,16,16,128]{3,2,1,0:T(8,128)(2,1)S(1)} %get-tuple-element.22), channel_id=1, source_target_pairs={{0,1},{1,0},{2,3},{3,2},{4,5},{5,4},{6,7},{7,6},{8,9},{9,8},{10,11... | collective-permute-start | bytes 1572872 | tf_op jit(solution)/shard_map/ppermute | solution.py:243
  108.7 10.0 %collective-permute-start.10 = (bf16[8,16,16,128]{3,2,1,0:T(8,128)(2,1)S(1)}, bf16[8,16,16,128]{3,2,1,0:T(8,128)(2,1)S(1)}, u32[]{:S(2)}, u32[]{:S(2)}) collective-permute-start(bf16[8,16,16,128]{3,2,1,0:T(8,128)(2,1)S(1)} %get-tuple-element.26), channel_id=1, source_target_pairs={{0,1},{1,0},{2,3},{3,2},{4,5},{5,4},{6,7},{7,6},{8,9},{9,8},{10,11... | collective-permute-start | bytes 1572872 | tf_op jit(solution)/shard_map/ppermute | solution.py:243
  110.7 10.5 %collective-permute-start.3 = (bf16[8,16,16,128]{3,2,1,0:T(8,128)(2,1)S(1)}, bf16[8,16,16,128]{3,2,1,0:T(8,128)(2,1)S(1)}, u32[]{:S(2)}, u32[]{:S(2)}) collective-permute-start(bf16[8,16,16,128]{3,2,1,0:T(8,128)(2,1)S(1)} %get-tuple-element.20), channel_id=1, source_target_pairs={{0,1},{1,0},{2,3},{3,2},{4,5},{5,4},{6,7},{7,6},{8,9},{9,8},{10,11... | collective-permute-start | bytes 1572872 | tf_op jit(solution)/shard_map/ppermute | solution.py:243
  113.2 16.7 %collective-permute-start.5 = (bf16[8,16,16,128]{3,2,1,0:T(8,128)(2,1)S(1)}, bf16[8,16,16,128]{3,2,1,0:T(8,128)(2,1)S(1)}, u32[]{:S(2)}, u32[]{:S(2)}) collective-permute-start(bf16[8,16,16,128]{3,2,1,0:T(8,128)(2,1)S(1)} %add_convert_fusion.4), channel_id=1, source_target_pairs={{0,2},{1,3},{2,0},{3,1},{4,6},{5,7},{6,4},{7,5},{8,10},{9,11},{10,... | collective-permute-start | bytes 1572872 | tf_op jit(solution)/shard_map/ppermute | solution.py:243
  116.8 13.3 %collective-permute-start.9 = (bf16[8,16,16,128]{3,2,1,0:T(8,128)(2,1)S(1)}, bf16[8,16,16,128]{3,2,1,0:T(8,128)(2,1)S(1)}, u32[]{:S(2)}, u32[]{:S(2)}) collective-permute-start(bf16[8,16,16,128]{3,2,1,0:T(8,128)(2,1)S(1)} %get-tuple-element.24), channel_id=1, source_target_pairs={{0,1},{1,0},{2,3},{3,2},{4,5},{5,4},{6,7},{7,6},{8,9},{9,8},{10,11... | collective-permute-start | bytes 1572872 | tf_op jit(solution)/shard_map/ppermute | solution.py:243
  118.9 21.3 %collective-permute-start.11 = (bf16[8,16,16,128]{3,2,1,0:T(8,128)(2,1)S(1)}, bf16[8,16,16,128]{3,2,1,0:T(8,128)(2,1)S(1)}, u32[]{:S(2)}, u32[]{:S(2)}) collective-permute-start(bf16[8,16,16,128]{3,2,1,0:T(8,128)(2,1)S(1)} %add_convert_fusion.1), channel_id=1, source_target_pairs={{0,2},{1,3},{2,0},{3,1},{4,6},{5,7},{6,4},{7,5},{8,10},{9,11},{10,... | collective-permute-start | bytes 1572872 | tf_op jit(solution)/shard_map/ppermute | solution.py:243
  140.4 58.6 %copy-start.2 = (bf16[2,1,48,3584]{3,2,1,0:T(8,128)(2,1)S(1)}, bf16[2,1,48,3584]{3,2,1,0:T(8,128)(2,1)}, u32[]{:S(2)}) copy-start(bf16[2,1,48,3584]{3,2,1,0:T(8,128)(2,1)} %x_ref.3) | copy-start | bytes 2064388
  199.9 9.7 %collective-permute-start.12 = (bf16[48,3584]{1,0:T(8,128)(2,1)S(1)}, bf16[48,3584]{1,0:T(8,128)(2,1)S(1)}, u32[]{:S(2)}, u32[]{:S(2)}) collective-permute-start(bf16[48,3584]{1,0:T(8,128)(2,1)S(1)} %get-tuple-element.30), channel_id=1, source_target_pairs={{0,32},{32,64},{64,96},{96,128},{128,160},{160,192},{192,224},{224... | collective-permute-start | bytes 1032200 | tf_op jit(solution)/shard_map/ppermute | solution.py:239
  203.0 11.5 %collective-permute-start.13 = (bf16[48,3584]{1,0:T(8,128)(2,1)S(1)}, bf16[48,3584]{1,0:T(8,128)(2,1)S(1)}, u32[]{:S(2)}, u32[]{:S(2)}) collective-permute-start(bf16[48,3584]{1,0:T(8,128)(2,1)S(1)} %get-tuple-element.29), channel_id=1, source_target_pairs={{32,0},{64,32},{96,64},{128,96},{160,128},{192,160},{224,192},{256... | collective-permute-start | bytes 1032200 | tf_op jit(solution)/shard_map/ppermute | solution.py:239

commit v3 on v2

--- a/solution.py
+++ b/solution.py
@@ -8,10 +8,12 @@
 SPLIT = 4
 LANES = 128
 MAIN = 8
-PARTS = 2
 
 epsilon = 1e-06
 route_scale = 2.5
+
+HOPS = (0, 2, 4, 6, -7, -5, -3, -1)
+GROUPS = ((2, 5, 3, 4), (0, 7, 1, 6))
 
 
 def iota(shape, dimension):
@@ -58,22 +60,25 @@
     return jnp.dot(gather, tail, preferred_element_type=jnp.float32)
 
 
-def prepare_kernel(x_ref, gain_ref, router_ref, ids_ref, packets_ref, gate_ref, row_ref):
+def prepare_kernel(x_ref, gain_ref, router_ref, ids_ref, turns_ref, gate_ref, row_ref, *packet_refs):
     for direction in range(x_ref.shape[0]):
         prepare_direction(
             x_ref.at[direction],
             gain_ref,
             router_ref,
             ids_ref.at[0, direction],
-            packets_ref.at[:, direction],
+            turns_ref.at[0, direction],
             gate_ref.at[direction],
             row_ref.at[direction],
+            [ref.at[direction] for ref in packet_refs],
         )
 
 
-def prepare_direction(x_ref, gain_ref, router_ref, ids_ref, packet_ref, gate_ref, row_ref):
-    experts = packet_ref.shape[0]
-    pairs = packet_ref.shape[1] - 2
+def prepare_direction(
+    x_ref, gain_ref, router_ref, ids_ref, turns_ref, gate_ref, row_ref, packet_refs
+):
+    experts = len(packet_refs)
+    pairs = packet_refs[0].shape[0] - 2
     tokens = x_ref.shape[1]
     x = x_ref[0].astype(jnp.float32)
     mean_square = jnp.mean(x * x, axis=-1, keepdims=True)
@@ -81,9 +86,10 @@
         jnp.bfloat16
     )
     logits = jnp.dot(normed, router_ref[0], preferred_element_type=jnp.float32)
-    chosen = ids_ref[...]
-    one_hot = (iota((tokens, experts), 1) == chosen).astype(jnp.float32)
-    gate = route_scale * jax.nn.sigmoid(jnp.sum(logits * one_hot, axis=-1, keepdims=True))
+    chosen = (iota((tokens, experts), 1) == ids_ref[...]).astype(jnp.float32)
+    gate = route_scale * jax.nn.sigmoid(jnp.sum(logits * chosen, axis=-1, keepdims=True))
+    turn = turns_ref[...]
+    one_hot = (iota((tokens, experts), 1) == turn).astype(jnp.float32)
     earlier = (iota((tokens, tokens), 1) < iota((tokens, tokens), 0)).astype(jnp.float32)
     before = jnp.dot(
         earlier.astype(jnp.bfloat16),
@@ -91,8 +97,8 @@
         preferred_element_type=jnp.float32,
     )
     slot = jnp.sum(before * one_hot, axis=-1, keepdims=True)
-    expert = chosen.astype(jnp.float32)
-    row = jnp.where(slot < MAIN, expert * MAIN + slot, experts * MAIN + expert)
+    turn = turn.astype(jnp.float32)
+    row = jnp.where(slot < MAIN, turn * MAIN + slot, experts * MAIN + turn)
     gate_ref[...] = jnp.broadcast_to(gate, gate_ref.shape)
     row_ref[...] = jnp.broadcast_to(row, row_ref.shape)
     diagonal = iota((tokens, tokens), 0) == iota((tokens, tokens), 1)
@@ -100,13 +106,22 @@
     rows = experts * (MAIN + 1)
     placer = (iota((rows, tokens), 0).astype(jnp.float32) == row_along).astype(jnp.float32)
     slots = jnp.dot(placer.astype(jnp.bfloat16), normed, preferred_element_type=jnp.float32)
-    main, tail = slots[: experts * MAIN], slots[experts * MAIN :]
-    for pair in range(pairs):
-        write_packet(packet_ref, pair, main[:, pair * 256 : (pair + 1) * 256])
+    tail = slots[experts * MAIN :]
     stacked = jnp.concatenate(
         [tail[:, c * LANES : (c + 1) * LANES] for c in range(2 * pairs)], axis=0
     )
-    write_tail(packet_ref, stacked.astype(jnp.bfloat16))
+    spread = tail_spread(experts, 2 * pairs, 32, False)
+    tails = jnp.dot(spread, stacked.astype(jnp.bfloat16), preferred_element_type=jnp.float32)
+    for index, packet_ref in enumerate(packet_refs):
+        main = slots[index * MAIN : (index + 1) * MAIN]
+        for pair in range(pairs):
+            first = pair * 256
+            block = jnp.concatenate(
+                [main[:, first : first + LANES], main[:, first + LANES : first + 256]], axis=0
+            )
+            packet_ref[pair] = block.astype(jnp.bfloat16)
+        last = tails[index * 32 : (index + 1) * 32].astype(jnp.bfloat16)
+        packet_ref[pairs:] = last.reshape(2, 16, LANES)
 
 
 def expert_kernel(own_ref, core_ref, chip_ref, both_ref, up_ref, down_ref, *rest):
@@ -143,20 +158,21 @@
         write_tail(ref, jnp.concatenate(tail_chunks[index], axis=0).astype(jnp.bfloat16))
 
 
-def finish_kernel(x_ref, packets_ref, gate_ref, row_ref, up_ref, down_ref):
-    for direction, out_ref in enumerate((up_ref, down_ref)):
+def finish_kernel(x_ref, gate_ref, row_ref, *rest):
+    packet_refs, out_refs = rest[:-2], rest[-2:]
+    for direction, out_ref in enumerate(out_refs):
         finish_direction(
             x_ref.at[direction],
-            packets_ref.at[:, direction],
             gate_ref.at[direction],
             row_ref.at[direction],
+            [ref.at[direction] for ref in packet_refs],
             out_ref,
         )
 
 
-def finish_direction(x_ref, packet_ref, gate_ref, row_ref, out_ref):
-    experts = packet_ref.shape[0]
-    pairs = packet_ref.shape[1] - 2
+def finish_direction(x_ref, gate_ref, row_ref, packet_refs, out_ref):
+    experts = len(packet_refs)
+    pairs = packet_refs[0].shape[0] - 2
     tokens = x_ref.shape[1]
     rows = experts * (MAIN + 1)
     row = row_ref[:, :1]
@@ -164,15 +180,21 @@
     chooser = (iota((tokens, rows), 1).astype(jnp.float32) == row).astype(jnp.float32)
     choose_main = chooser[:, : experts * MAIN].astype(jnp.bfloat16)
     choose_tail = chooser[:, experts * MAIN :].astype(jnp.bfloat16)
-    tail = read_tail(packet_ref)
+    tails = jnp.concatenate([ref[pairs:].reshape(32, LANES) for ref in packet_refs], axis=0)
+    gather = tail_spread(experts, 2 * pairs, 32, True)
+    tail = jnp.dot(gather, tails, preferred_element_type=jnp.float32)
     for pair in range(pairs):
         columns = slice(pair * 256, (pair + 1) * 256)
+        blocks = [ref[pair].astype(jnp.float32) for ref in packet_refs]
+        low = jnp.concatenate([block[:MAIN] for block in blocks], axis=0)
+        high = jnp.concatenate([block[MAIN:] for block in blocks], axis=0)
+        main_pair = jnp.concatenate([low, high], axis=1).astype(jnp.bfloat16)
         first = 2 * pair * experts
         tail_pair = jnp.concatenate(
             [tail[first : first + experts], tail[first + experts : first + 2 * experts]], axis=1
         ).astype(jnp.bfloat16)
         routed = jnp.dot(
-            choose_main, read_pair(packet_ref, pair), preferred_element_type=jnp.float32
+            choose_main, main_pair, preferred_element_type=jnp.float32
         ) + jnp.dot(choose_tail, tail_pair, preferred_element_type=jnp.float32)
         x = x_ref[0, :, columns].astype(jnp.float32)
         out_ref[:, columns] = (x + gate * routed).astype(jnp.bfloat16)
@@ -186,20 +208,21 @@
     return pl.BlockSpec(array.shape, lambda _: (0,) * array.ndim)
 
 
-def prepare(carried, gain, router, ids, experts):
+def prepare(carried, gain, router, ids, turns, experts):
     directions, _, tokens, width = carried.shape
-    blocks = width // 256 + 2
-    packets = jax.ShapeDtypeStruct((experts, directions, blocks, 16, LANES), jnp.bfloat16)
+    packet = jax.ShapeDtypeStruct((directions, width // 256 + 2, 16, LANES), jnp.bfloat16)
     notes = jax.ShapeDtypeStruct((directions, tokens, LANES), jnp.float32)
-    return pl.pallas_call(
+    outs = (notes, notes) + (packet,) * experts
+    gate, row, *packets = pl.pallas_call(
         prepare_kernel,
         grid=(1,),
-        out_shape=(packets, notes, notes),
-        in_specs=[whole(a) for a in (carried, gain, router, ids)],
-        out_specs=(whole(packets), whole(notes), whole(notes)),
+        out_shape=outs,
+        in_specs=[whole(a) for a in (carried, gain, router, ids, turns)],
+        out_specs=tuple(whole(a) for a in outs),
         compiler_params=params(),
         name="prepare",
-    )(carried, gain, router, ids)
+    )(carried, gain, router, ids, turns)
+    return gate, row, packets
 
 
 def run_expert(own, core, chip, both, up, down):
@@ -219,18 +242,19 @@
     )(own, core, chip, both, up, down)
 
 
-def finish(carried, packets, gate, row):
+def finish(carried, gate, row, packets):
     tokens, width = carried.shape[2:]
     out = jax.ShapeDtypeStruct((tokens, width), jnp.bfloat16)
+    operands = (carried, gate, row, *packets)
     return pl.pallas_call(
         finish_kernel,
         grid=(1,),
         out_shape=(out, out),
-        in_specs=[whole(a) for a in (carried, packets, gate, row)],
+        in_specs=[whole(a) for a in operands],
         out_specs=(whole(out), whole(out)),
         compiler_params=params(),
         name="finish",
-    )(carried, packets, gate, row)
+    )(*operands)
 
 
 def passed_along(block, axis, distance):
@@ -245,12 +269,16 @@
     )
 
 
-def exchanged(packet):
-    experts = lax.axis_size("expert") // SPLIT
-    groups = [[e * SPLIT + k for e in range(experts)] for k in range(SPLIT)]
-    return lax.all_to_all(
-        packet, "expert", split_axis=0, concat_axis=0, axis_index_groups=groups, tiled=True
-    )
+def delivered(packet, turn, back):
+    if HOPS[turn] == 0:
+        return packet
+    devices = lax.axis_size("expert")
+    route = []
+    for device in range(devices):
+        chips = HOPS[turn] if device // 2 % 2 == 0 else -HOPS[turn]
+        there = (device + 2 * chips) % devices
+        route.append((there, device) if back else (device, there))
+    return lax.ppermute(packet, "expert", route)
 
 
 def added(left, right):
@@ -259,21 +287,26 @@
 
 def per_device(carried, norm_gain, router, w_up, w_down, expert_ids):
     experts = lax.axis_size("expert") // SPLIT
-    packets, gate, row = prepare(carried, norm_gain, router, expert_ids, experts)
-    received = exchanged(packets)
-    peers = experts // PARTS
-    totals = []
-    for part in range(PARTS):
-        own = received[part * peers : (part + 1) * peers].reshape(-1, *packets.shape[2:])
+    device = lax.axis_index("expert")
+    pair = device // SPLIT
+    lower = device // 2 % 2 == 0
+    turns = jnp.where(lower, expert_ids - pair, pair - expert_ids) % experts
+    gate, row, packets = prepare(carried, norm_gain, router, expert_ids, turns, experts)
+    arrived = [delivered(packet, turn, False) for turn, packet in enumerate(packets)]
+    returned = [None] * experts
+    for group in GROUPS:
+        own = jnp.concatenate([arrived[turn] for turn in group], axis=0)
         chip = swapped(own, 2)
         core = swapped(own, 1)
         both = swapped(chip, 1)
         for_own, for_core, for_chip, for_both = run_expert(own, core, chip, both, w_up, w_down)
         own_sum = added(for_own, swapped(for_core, 1))
         chip_sum = added(for_chip, swapped(for_both, 1))
-        totals.append(added(own_sum, swapped(chip_sum, 2)).reshape(peers, *packets.shape[1:]))
-    returned = exchanged(jnp.concatenate(totals, axis=0))
-    layer_outputs = finish(carried, returned, gate, row)
+        from_chip = swapped(chip_sum, 2)
+        for place, turn in enumerate(group):
+            part = slice(2 * place, 2 * place + 2)
+            returned[turn] = delivered(added(own_sum[part], from_chip[part]), turn, True)
+    layer_outputs = finish(carried, gate, row, returned)
     section_index = lax.axis_index("section")
     last_section = lax.axis_size("section") - 1
     from_below = passed_along(layer_outputs[0], "section", 1)

time: 220 us -> 197 us (0.90); the launches traced: 215 us -> 196 us
  blocking collectives: 123 us -> 0 us
  starting transfers between devices: 34.8 us -> 116 us
  waiting for transfers between devices: 40.2 us -> 62.7 us
    all_to_all x2 -> x0, blocking collectives: 123 us -> none  [exchanged(): lax.all_to_all(packet, 'expert', split_axis=0, concat_axis=0, axis_index_...]
    ppermute x0 -> x14, starting transfers between devices: none -> 77.9 us  [delivered(): return lax.ppermute(packet, 'expert', route)]
    ppermute x0 -> x14, waiting for transfers between devices: none -> 20.5 us  [delivered(): return lax.ppermute(packet, 'expert', route)]
    ppermute x12, starting transfers between devices: 29 us -> 32.3 us  [swapped(): lax.ppermute(block, 'expert', [(i, i ^ bit) for i in range(lax.axis_size(...]
  transfers between devices with their start and end apart: 14 -> 28, of which waited for: 6 -> 12; matrix products, arithmetic and copies ran while one was open for 0% -> 1% of each run, Pallas kernels for 4% -> 4%
where the time goes in v3:
time: 197 us; the launch traced here: 196 us
  starting transfers between devices  116 us (59%)
  waiting for transfers between devices  62.7 us (32%)
  Pallas kernels  11 us (6%)
  local copies, waits for them, and re-layouts  3.13 us (2%)
  other arithmetic  2.55 us (1%)
    ppermute x14, starting transfers between devices, delivered(): return lax.ppermute(packet, 'expert', route)  77.9 us
    ppermute x12, starting transfers between devices, swapped(): lax.ppermute(block, 'expert', [(i, i ^ bit) for i in range(lax.axis_size(...  32.3 us
    ppermute x12, waiting for transfers between devices, swapped(): lax.ppermute(block, 'expert', [(i, i ^ bit) for i in range(lax.axis_size(...  31.5 us
    ppermute x14, waiting for transfers between devices, delivered(): return lax.ppermute(packet, 'expert', route)  20.5 us
    ppermute x2, waiting for transfers between devices, passed_along(): return lax.ppermute(block, axis, route)  10.7 us
    pallas_call x2, Pallas kernels, run_expert(): pl.pallas_call(expert_kernel, grid=(1,), out_shape=(packet,) * 4, in_spec...  8.48 us
    ppermute x2, starting transfers between devices, passed_along(): return lax.ppermute(block, axis, route)  5.84 us
  transfers between devices with their start and end apart: 28, of which 12 were waited for; matrix products, arithmetic and copies ran while one was open for 1% of the time, Pallas kernels for 4%

profile of v3, /device:TPU:24, one launch (start us, length us, event | category | flops | bytes accessed | tf_op | source)
XLA Modules:
  0.0 196.0 jit_solution(17806994610278607002)
XLA Ops:
  0.0 0.8 copy.19.ids_ref
  0.9 0.7 fusion.1
  1.5 0.1 copy.16
  1.6 0.1 copy.17
  1.7 1.2 copy.18.router_ref
  3.0 0.0 copy-start.2
  3.1 0.7 copy-done.2
  3.8 1.7 prepare.1
  5.5 9.1 %collective-permute-start.10 = (bf16[2,16,16,128]{3,2,1,0:T(8,128)(2,1)S(1)}, bf16[2,16,16,128]{3,2,1,0:T(8,128)(2,1)S(1)}, u32[]{:S(2)}, u32[]{:S(2)}) collective-permute-start(bf16[2,16,16,128]{3,2,1,0:T(8,128)(2,1)S(1)} %get-tuple-element.35), channel_id=1, source_target_pairs={{0,8},{1,9},{2,26},{3,27},{4,12},{5,13},{6,30},{7,31},{8,16},{9,17... | collective-permute-start | bytes 393224 | tf_op jit(solution)/shard_map/ppermute | solution.py:281
  14.6 8.7 %collective-permute-start.11 = (bf16[2,16,16,128]{3,2,1,0:T(8,128)(2,1)S(1)}, bf16[2,16,16,128]{3,2,1,0:T(8,128)(2,1)S(1)}, u32[]{:S(2)}, u32[]{:S(2)}) collective-permute-start(bf16[2,16,16,128]{3,2,1,0:T(8,128)(2,1)S(1)} %get-tuple-element.36), channel_id=1, source_target_pairs={{0,22},{1,23},{2,12},{3,13},{4,26},{5,27},{6,16},{7,17},{8,30},{9,... | collective-permute-start | bytes 393224 | tf_op jit(solution)/shard_map/ppermute | solution.py:281
  23.2 6.1 %collective-permute-start.12 = (bf16[2,16,16,128]{3,2,1,0:T(8,128)(2,1)S(1)}, bf16[2,16,16,128]{3,2,1,0:T(8,128)(2,1)S(1)}, u32[]{:S(2)}, u32[]{:S(2)}) collective-permute-start(bf16[2,16,16,128]{3,2,1,0:T(8,128)(2,1)S(1)} %get-tuple-element.37), channel_id=1, source_target_pairs={{0,12},{1,13},{2,22},{3,23},{4,16},{5,17},{6,26},{7,27},{8,20},{9,... | collective-permute-start | bytes 393224 | tf_op jit(solution)/shard_map/ppermute | solution.py:281
  29.4 8.0 %collective-permute-start.13 = (bf16[2,16,16,128]{3,2,1,0:T(8,128)(2,1)S(1)}, bf16[2,16,16,128]{3,2,1,0:T(8,128)(2,1)S(1)}, u32[]{:S(2)}, u32[]{:S(2)}) collective-permute-start(bf16[2,16,16,128]{3,2,1,0:T(8,128)(2,1)S(1)} %get-tuple-element.38), channel_id=1, source_target_pairs={{0,18},{1,19},{2,16},{3,17},{4,22},{5,23},{6,20},{7,21},{8,26},{9,... | collective-permute-start | bytes 393224 | tf_op jit(solution)/shard_map/ppermute | solution.py:281
  37.4 1.9 collective-permute-start
  39.3 2.2 %collective-permute-start.1 = (bf16[2,16,16,128]{3,2,1,0:T(8,128)(2,1)S(1)}, bf16[2,16,16,128]{3,2,1,0:T(8,128)(2,1)S(1)}, u32[]{:S(2)}, u32[]{:S(2)}) collective-permute-start(bf16[2,16,16,128]{3,2,1,0:T(8,128)(2,1)S(1)} %get-tuple-element.29), channel_id=1, source_target_pairs={{0,4},{1,5},{2,30},{3,31},{4,8},{5,9},{6,2},{7,3},{8,12},{9,13},{1... | collective-permute-start | bytes 393224 | tf_op jit(solution)/shard_map/ppermute | solution.py:281
  41.5 2.3 %collective-permute-done.11 = bf16[2,16,16,128]{3,2,1,0:T(8,128)(2,1)S(1)} collective-permute-done((bf16[2,16,16,128]{3,2,1,0:T(8,128)(2,1)S(1)}, bf16[2,16,16,128]{3,2,1,0:T(8,128)(2,1)S(1)}, u32[]{:S(2)}, u32[]{:S(2)}) %collective-permute-start.11) | collective-permute-done | bytes 131104 | tf_op jit(solution)/shard_map/ppermute | solution.py:281
  43.9 6.1 %collective-permute-start.2 = (bf16[2,16,16,128]{3,2,1,0:T(8,128)(2,1)S(1)}, bf16[2,16,16,128]{3,2,1,0:T(8,128)(2,1)S(1)}, u32[]{:S(2)}, u32[]{:S(2)}) collective-permute-start(bf16[2,16,16,128]{3,2,1,0:T(8,128)(2,1)S(1)} %get-tuple-element.30), channel_id=1, source_target_pairs={{0,26},{1,27},{2,8},{3,9},{4,30},{5,31},{6,12},{7,13},{8,2},{9,3},... | collective-permute-start | bytes 393224 | tf_op jit(solution)/shard_map/ppermute | solution.py:281
  50.1 4.7 %collective-permute-done.13 = bf16[2,16,16,128]{3,2,1,0:T(8,128)(2,1)S(1)} collective-permute-done((bf16[2,16,16,128]{3,2,1,0:T(8,128)(2,1)S(1)}, bf16[2,16,16,128]{3,2,1,0:T(8,128)(2,1)S(1)}, u32[]{:S(2)}, u32[]{:S(2)}) %collective-permute-start.13) | collective-permute-done | bytes 131104 | tf_op jit(solution)/shard_map/ppermute | solution.py:281
  54.8 3.9 %collective-permute-start.15 = (bf16[8,16,16,128]{3,2,1,0:T(8,128)(2,1)S(1)}, bf16[8,16,16,128]{3,2,1,0:T(8,128)(2,1)S(1)}, u32[]{:S(2)}, u32[]{:S(2)}) collective-permute-start(bf16[8,16,16,128]{3,2,1,0:T(8,128)(2,1)S(1)} %constant_dynamic-update-slice_fusion.4.own_ref), channel_id=1, source_target_pairs={{0,2},{1,3},{2,0},{3,1},{4,6},{5,7},{6,4},{7,5},{8,10},{9,11},{10,... | collective-permute-start | bytes 1572872 | tf_op jit(solution)/shard_map/ppermute | solution.py:267
  58.7 1.1 collective-permute-done
  59.9 0.0 collective-permute-done.1
  59.9 4.3 %collective-permute-done.2 = bf16[2,16,16,128]{3,2,1,0:T(8,128)(2,1)S(1)} collective-permute-done((bf16[2,16,16,128]{3,2,1,0:T(8,128)(2,1)S(1)}, bf16[2,16,16,128]{3,2,1,0:T(8,128)(2,1)S(1)}, u32[]{:S(2)}, u32[]{:S(2)}) %collective-permute-start.2) | collective-permute-done | bytes 131104 | tf_op jit(solution)/shard_map/ppermute | solution.py:281
  64.2 5.7 %collective-permute-start.4 = (bf16[8,16,16,128]{3,2,1,0:T(8,128)(2,1)S(1)}, bf16[8,16,16,128]{3,2,1,0:T(8,128)(2,1)S(1)}, u32[]{:S(2)}, u32[]{:S(2)}) collective-permute-start(bf16[8,16,16,128]{3,2,1,0:T(8,128)(2,1)S(1)} %constant_dynamic-update-slice_fusion.own_ref), channel_id=1, source_target_pairs={{0,2},{1,3},{2,0},{3,1},{4,6},{5,7},{6,4},{7,5},{8,10},{9,11},{10,... | collective-permute-start | bytes 1572872 | tf_op jit(solution)/shard_map/ppermute | solution.py:267
  69.9 1.9 collective-permute-start.14
  71.8 1.7 collective-permute-done.15.chip_ref
  73.5 1.9 collective-permute-start.16
  75.5 2.4 %collective-permute-start.3 = (bf16[8,16,16,128]{3,2,1,0:T(8,128)(2,1)S(1)}, bf16[8,16,16,128]{3,2,1,0:T(8,128)(2,1)S(1)}, u32[]{:S(2)}, u32[]{:S(2)}) collective-permute-start(bf16[8,16,16,128]{3,2,1,0:T(8,128)(2,1)S(1)} %constant_dynamic-update-slice_fusion.own_ref), channel_id=1, source_target_pairs={{0,1},{1,0},{2,3},{3,2},{4,5},{5,4},{6,7},{7,6},{8,9},{9,8},{10,11... | collective-permute-start | bytes 1572872 | tf_op jit(solution)/shard_map/ppermute | solution.py:267
  77.9 6.5 %collective-permute-done.4.chip_ref = bf16[8,16,16,128]{3,2,1,0:T(8,128)(2,1)S(1)} collective-permute-done((bf16[8,16,16,128]{3,2,1,0:T(8,128)(2,1)S(1)}, bf16[8,16,16,128]{3,2,1,0:T(8,128)(2,1)S(1)}, u32[]{:S(2)}, u32[]{:S(2)}) %collective-permute-start.4) | collective-permute-done | bytes 524320 | tf_op jit(solution)/shard_map/ppermute | solution.py:267
  84.4 1.9 collective-permute-start.5
  86.3 0.0 collective-permute-done.14.core_ref
  86.3 4.2 %expert.3 = (bf16[8,16,16,128]{3,2,1,0:T(8,128)(2,1)S(1)}, bf16[8,16,16,128]{3,2,1,0:T(8,128)(2,1)S(1)}, bf16[8,16,16,128]{3,2,1,0:T(8,128)(2,1)S(1)}, bf16[8,16,16,128]{3,2,1,0:T(8,128)(2,1)S(1)}) custom-call(bf16[8,16,16,128]{3,2,1,0:T(8,128)(2,1)S(1)} %constant_dynamic-update-slice_fusion.4.own_ref, ...), custom_call_target="tpu_custom_call" | custom-call | tf_op jit(solution)/shard_map/expert/pallas_call | solution.py:233
  90.6 2.4 %collective-permute-start.18 = (bf16[8,16,16,128]{3,2,1,0:T(8,128)(2,1)S(1)}, bf16[8,16,16,128]{3,2,1,0:T(8,128)(2,1)S(1)}, u32[]{:S(2)}, u32[]{:S(2)}) collective-permute-start(bf16[8,16,16,128]{3,2,1,0:T(8,128)(2,1)S(1)} %get-tuple-element.42), channel_id=1, source_target_pairs={{0,1},{1,0},{2,3},{3,2},{4,5},{5,4},{6,7},{7,6},{8,9},{9,8},{10,11... | collective-permute-start | bytes 1572872 | tf_op jit(solution)/shard_map/ppermute | solution.py:267
  93.0 0.0 collective-permute-done.3.core_ref
  93.0 4.2 %expert.2 = (bf16[8,16,16,128]{3,2,1,0:T(8,128)(2,1)S(1)}, bf16[8,16,16,128]{3,2,1,0:T(8,128)(2,1)S(1)}, bf16[8,16,16,128]{3,2,1,0:T(8,128)(2,1)S(1)}, bf16[8,16,16,128]{3,2,1,0:T(8,128)(2,1)S(1)}) custom-call(bf16[8,16,16,128]{3,2,1,0:T(8,128)(2,1)S(1)} %constant_dynamic-update-slice_fusion.own_ref, ...), custom_call_target="tpu_custom_call" | custom-call | tf_op jit(solution)/shard_map/expert/pallas_call | solution.py:233
  97.3 1.9 collective-permute-start.7
  99.2 2.4 %collective-permute-start.17 = (bf16[8,16,16,128]{3,2,1,0:T(8,128)(2,1)S(1)}, bf16[8,16,16,128]{3,2,1,0:T(8,128)(2,1)S(1)}, u32[]{:S(2)}, u32[]{:S(2)}) collective-permute-start(bf16[8,16,16,128]{3,2,1,0:T(8,128)(2,1)S(1)} %get-tuple-element.40), channel_id=1, source_target_pairs={{0,1},{1,0},{2,3},{3,2},{4,5},{5,4},{6,7},{7,6},{8,9},{9,8},{10,11... | collective-permute-start | bytes 1572872 | tf_op jit(solution)/shard_map/ppermute | solution.py:267
  101.6 1.9 collective-permute-start.6
  103.5 0.1 add_convert_fusion
  103.7 3.9 %collective-permute-start.19 = (bf16[8,16,16,128]{3,2,1,0:T(8,128)(2,1)S(1)}, bf16[8,16,16,128]{3,2,1,0:T(8,128)(2,1)S(1)}, u32[]{:S(2)}, u32[]{:S(2)}) collective-permute-start(bf16[8,16,16,128]{3,2,1,0:T(8,128)(2,1)S(1)} %add_convert_fusion), channel_id=1, source_target_pairs={{0,2},{1,3},{2,0},{3,1},{4,6},{5,7},{6,4},{7,5},{8,10},{9,11},{10,... | collective-permute-start | bytes 1572872 | tf_op jit(solution)/shard_map/ppermute | solution.py:267
  107.6 0.0 collective-permute-done.7
  107.6 0.1 add_convert_fusion.2
  107.8 1.9 collective-permute-start.8
  109.7 0.1 add_convert_fusion.1
  109.9 0.0 collective-permute-done.6
  109.9 0.1 add_convert_fusion.3
  110.0 10.4 %collective-permute-done.19 = bf16[8,16,16,128]{3,2,1,0:T(8,128)(2,1)S(1)} collective-permute-done((bf16[8,16,16,128]{3,2,1,0:T(8,128)(2,1)S(1)}, bf16[8,16,16,128]{3,2,1,0:T(8,128)(2,1)S(1)}, u32[]{:S(2)}, u32[]{:S(2)}) %collective-permute-start.19) | collective-permute-done | bytes 524320 | tf_op jit(solution)/shard_map/ppermute | solution.py:267
  120.4 0.1 add_convert_fusion.6
  120.5 8.0 %collective-permute-start.20 = (bf16[2,16,16,128]{3,2,1,0:T(8,128)(2,1)S(1)}, bf16[2,16,16,128]{3,2,1,0:T(8,128)(2,1)S(1)}, u32[]{:S(2)}, u32[]{:S(2)}) collective-permute-start(bf16[2,16,16,128]{3,2,1,0:T(8,128)(2,1)S(1)} %get-tuple-element.52), channel_id=1, source_target_pairs={{8,0},{9,1},{26,2},{27,3},{12,4},{13,5},{30,6},{31,7},{16,8},{17,9... | collective-permute-start | bytes 393224 | tf_op jit(solution)/shard_map/ppermute | solution.py:281
  128.6 5.9 %collective-permute-start.21 = (bf16[2,16,16,128]{3,2,1,0:T(8,128)(2,1)S(1)}, bf16[2,16,16,128]{3,2,1,0:T(8,128)(2,1)S(1)}, u32[]{:S(2)}, u32[]{:S(2)}) collective-permute-start(bf16[2,16,16,128]{3,2,1,0:T(8,128)(2,1)S(1)} %get-tuple-element.51), channel_id=1, source_target_pairs={{12,0},{13,1},{22,2},{23,3},{16,4},{17,5},{26,6},{27,7},{20,8},{21... | collective-permute-start | bytes 393224 | tf_op jit(solution)/shard_map/ppermute | solution.py:281
  134.5 5.2 %collective-permute-start.22 = (bf16[2,16,16,128]{3,2,1,0:T(8,128)(2,1)S(1)}, bf16[2,16,16,128]{3,2,1,0:T(8,128)(2,1)S(1)}, u32[]{:S(2)}, u32[]{:S(2)}) collective-permute-start(bf16[2,16,16,128]{3,2,1,0:T(8,128)(2,1)S(1)} %get-tuple-element.50), channel_id=1, source_target_pairs={{18,0},{19,1},{16,2},{17,3},{22,4},{23,5},{20,6},{21,7},{26,8},{27... | collective-permute-start | bytes 393224 | tf_op jit(solution)/shard_map/ppermute | solution.py:281
  139.7 5.4 %collective-permute-start.23 = (bf16[2,16,16,128]{3,2,1,0:T(8,128)(2,1)S(1)}, bf16[2,16,16,128]{3,2,1,0:T(8,128)(2,1)S(1)}, u32[]{:S(2)}, u32[]{:S(2)}) collective-permute-start(bf16[2,16,16,128]{3,2,1,0:T(8,128)(2,1)S(1)} %get-tuple-element.49), channel_id=1, source_target_pairs={{22,0},{23,1},{12,2},{13,3},{26,4},{27,5},{16,6},{17,7},{30,8},{31... | collective-permute-start | bytes 393224 | tf_op jit(solution)/shard_map/ppermute | solution.py:281
  145.1 12.9 %collective-permute-done.8 = bf16[8,16,16,128]{3,2,1,0:T(8,128)(2,1)S(1)} collective-permute-done((bf16[8,16,16,128]{3,2,1,0:T(8,128)(2,1)S(1)}, bf16[8,16,16,128]{3,2,1,0:T(8,128)(2,1)S(1)}, u32[]{:S(2)}, u32[]{:S(2)}) %collective-permute-start.8) | collective-permute-done | bytes 524320 | tf_op jit(solution)/shard_map/ppermute | solution.py:267
  158.0 0.1 add_convert_fusion.4
  158.2 5.1 %collective-permute-start.24 = (bf16[2,16,16,128]{3,2,1,0:T(8,128)(2,1)S(1)}, bf16[2,16,16,128]{3,2,1,0:T(8,128)(2,1)S(1)}, u32[]{:S(2)}, u32[]{:S(2)}) collective-permute-start(bf16[2,16,16,128]{3,2,1,0:T(8,128)(2,1)S(1)} %get-tuple-element.46), channel_id=1, source_target_pairs={{26,0},{27,1},{8,2},{9,3},{30,4},{31,5},{12,6},{13,7},{2,8},{3,9},... | collective-permute-start | bytes 393224 | tf_op jit(solution)/shard_map/ppermute | solution.py:281
  163.2 2.2 %collective-permute-start.25 = (bf16[2,16,16,128]{3,2,1,0:T(8,128)(2,1)S(1)}, bf16[2,16,16,128]{3,2,1,0:T(8,128)(2,1)S(1)}, u32[]{:S(2)}, u32[]{:S(2)}) collective-permute-start(bf16[2,16,16,128]{3,2,1,0:T(8,128)(2,1)S(1)} %get-tuple-element.45), channel_id=1, source_target_pairs={{30,0},{31,1},{4,2},{5,3},{2,4},{3,5},{8,6},{9,7},{6,8},{7,9},{12,... | collective-permute-start | bytes 393224 | tf_op jit(solution)/shard_map/ppermute | solution.py:281
  165.5 4.0 %collective-permute-start.9 = (bf16[2,16,16,128]{3,2,1,0:T(8,128)(2,1)S(1)}, bf16[2,16,16,128]{3,2,1,0:T(8,128)(2,1)S(1)}, u32[]{:S(2)}, u32[]{:S(2)}) collective-permute-start(bf16[2,16,16,128]{3,2,1,0:T(8,128)(2,1)S(1)} %get-tuple-element.47), channel_id=1, source_target_pairs={{4,0},{5,1},{30,2},{31,3},{8,4},{9,5},{2,6},{3,7},{12,8},{13,9},{6... | collective-permute-start | bytes 393224 | tf_op jit(solution)/shard_map/ppermute | solution.py:281
  169.5 3.8 %collective-permute-done.24.rest_6_ = bf16[2,16,16,128]{3,2,1,0:T(8,128)(2,1)S(1)} collective-permute-done((bf16[2,16,16,128]{3,2,1,0:T(8,128)(2,1)S(1)}, bf16[2,16,16,128]{3,2,1,0:T(8,128)(2,1)S(1)}, u32[]{:S(2)}, u32[]{:S(2)}) %collective-permute-start.24) | collective-permute-done | bytes 131104 | tf_op jit(solution)/shard_map/ppermute | solution.py:281
  173.3 4.3 %collective-permute-done.9.rest_1_ = bf16[2,16,16,128]{3,2,1,0:T(8,128)(2,1)S(1)} collective-permute-done((bf16[2,16,16,128]{3,2,1,0:T(8,128)(2,1)S(1)}, bf16[2,16,16,128]{3,2,1,0:T(8,128)(2,1)S(1)}, u32[]{:S(2)}, u32[]{:S(2)}) %collective-permute-start.9) | collective-permute-done | bytes 131104 | tf_op jit(solution)/shard_map/ppermute | solution.py:281
  177.6 0.8 finish.1
  178.4 3.1 %collective-permute-start.26 = (bf16[48,3584]{1,0:T(8,128)(2,1)S(1)}, bf16[48,3584]{1,0:T(8,128)(2,1)S(1)}, u32[]{:S(2)}, u32[]{:S(2)}) collective-permute-start(bf16[48,3584]{1,0:T(8,128)(2,1)S(1)} %get-tuple-element.44), channel_id=1, source_target_pairs={{0,32},{32,64},{64,96},{96,128},{128,160},{160,192},{192,224},{224... | collective-permute-start | bytes 1032200 | tf_op jit(solution)/shard_map/ppermute | solution.py:263
  181.5 2.8 %collective-permute-start.27 = (bf16[48,3584]{1,0:T(8,128)(2,1)S(1)}, bf16[48,3584]{1,0:T(8,128)(2,1)S(1)}, u32[]{:S(2)}, u32[]{:S(2)}) collective-permute-start(bf16[48,3584]{1,0:T(8,128)(2,1)S(1)} %get-tuple-element.43), channel_id=1, source_target_pairs={{32,0},{64,32},{96,64},{128,96},{160,128},{192,160},{224,192},{256... | collective-permute-start | bytes 1032200 | tf_op jit(solution)/shard_map/ppermute | solution.py:263
  184.3 5.7 %collective-permute-done.26 = bf16[48,3584]{1,0:T(8,128)(2,1)S(1)} collective-permute-done((bf16[48,3584]{1,0:T(8,128)(2,1)S(1)}, bf16[48,3584]{1,0:T(8,128)(2,1)S(1)}, u32[]{:S(2)}, u32[]{:S(2)}) %collective-permute-start.26) | collective-permute-done | bytes 344096 | tf_op jit(solution)/shard_map/ppermute | solution.py:263
  190.0 5.0 %collective-permute-done.27 = bf16[48,3584]{1,0:T(8,128)(2,1)S(1)} collective-permute-done((bf16[48,3584]{1,0:T(8,128)(2,1)S(1)}, bf16[48,3584]{1,0:T(8,128)(2,1)S(1)}, u32[]{:S(2)}, u32[]{:S(2)}) %collective-permute-start.27) | collective-permute-done | bytes 344096 | tf_op jit(solution)/shard_map/ppermute | solution.py:263
  195.1 0.1 select_bitcast_fusion
  195.1 0.9 maximum_bitcast_fusion
  (26 shorter events, 0.2 us)
Async XLA Ops:
  0.0 3.0 %copy-start.1 = (bf16[2,1,48,3584]{3,2,1,0:T(8,128)(2,1)S(1)}, bf16[2,1,48,3584]{3,2,1,0:T(8,128)(2,1)}, u32[]{:S(2)}) copy-start(bf16[2,1,48,3584]{3,2,1,0:T(8,128)(2,1)} %x_ref.3) | copy-start | bytes 2064388
  3.0 0.7 copy-start.2
  3.8 82.6 %copy-start = (bf16[1,3584,256]{2,1,0:T(8,128)(2,1)S(1)}, bf16[1,3584,256]{2,1,0:T(8,128)(2,1)}, u32[]{:S(2)}) copy-start(bf16[1,3584,256]{2,1,0:T(8,128)(2,1)} %up_ref.3) | copy-start | bytes 5505028
  5.5 33.9 %collective-permute-start.10 = (bf16[2,16,16,128]{3,2,1,0:T(8,128)(2,1)S(1)}, bf16[2,16,16,128]{3,2,1,0:T(8,128)(2,1)S(1)}, u32[]{:S(2)}, u32[]{:S(2)}) collective-permute-start(bf16[2,16,16,128]{3,2,1,0:T(8,128)(2,1)S(1)} %get-tuple-element.35), channel_id=1, source_target_pairs={{0,8},{1,9},{2,26},{3,27},{4,12},{5,13},{6,30},{7,31},{8,16},{9,17... | collective-permute-start | bytes 393224 | tf_op jit(solution)/shard_map/ppermute | solution.py:281
  14.6 29.3 %collective-permute-start.11 = (bf16[2,16,16,128]{3,2,1,0:T(8,128)(2,1)S(1)}, bf16[2,16,16,128]{3,2,1,0:T(8,128)(2,1)S(1)}, u32[]{:S(2)}, u32[]{:S(2)}) collective-permute-start(bf16[2,16,16,128]{3,2,1,0:T(8,128)(2,1)S(1)} %get-tuple-element.36), channel_id=1, source_target_pairs={{0,22},{1,23},{2,12},{3,13},{4,26},{5,27},{6,16},{7,17},{8,30},{9,... | collective-permute-start | bytes 393224 | tf_op jit(solution)/shard_map/ppermute | solution.py:281
  23.2 26.8 %collective-permute-start.12 = (bf16[2,16,16,128]{3,2,1,0:T(8,128)(2,1)S(1)}, bf16[2,16,16,128]{3,2,1,0:T(8,128)(2,1)S(1)}, u32[]{:S(2)}, u32[]{:S(2)}) collective-permute-start(bf16[2,16,16,128]{3,2,1,0:T(8,128)(2,1)S(1)} %get-tuple-element.37), channel_id=1, source_target_pairs={{0,12},{1,13},{2,22},{3,23},{4,16},{5,17},{6,26},{7,27},{8,20},{9,... | collective-permute-start | bytes 393224 | tf_op jit(solution)/shard_map/ppermute | solution.py:281
  29.4 25.4 %collective-permute-start.13 = (bf16[2,16,16,128]{3,2,1,0:T(8,128)(2,1)S(1)}, bf16[2,16,16,128]{3,2,1,0:T(8,128)(2,1)S(1)}, u32[]{:S(2)}, u32[]{:S(2)}) collective-permute-start(bf16[2,16,16,128]{3,2,1,0:T(8,128)(2,1)S(1)} %get-tuple-element.38), channel_id=1, source_target_pairs={{0,18},{1,19},{2,16},{3,17},{4,22},{5,23},{6,20},{7,21},{8,26},{9,... | collective-permute-start | bytes 393224 | tf_op jit(solution)/shard_map/ppermute | solution.py:281
  37.4 22.5 %collective-permute-start = (bf16[2,16,16,128]{3,2,1,0:T(8,128)(2,1)S(1)}, bf16[2,16,16,128]{3,2,1,0:T(8,128)(2,1)S(1)}, u32[]{:S(2)}, u32[]{:S(2)}) collective-permute-start(bf16[2,16,16,128]{3,2,1,0:T(8,128)(2,1)S(1)} %get-tuple-element.28), channel_id=1, source_target_pairs={{0,30},{1,31},{2,4},{3,5},{4,2},{5,3},{6,8},{7,9},{8,6},{9,7},{10,... | collective-permute-start | bytes 393224 | tf_op jit(solution)/shard_map/ppermute | solution.py:281
  39.3 20.5 %collective-permute-start.1 = (bf16[2,16,16,128]{3,2,1,0:T(8,128)(2,1)S(1)}, bf16[2,16,16,128]{3,2,1,0:T(8,128)(2,1)S(1)}, u32[]{:S(2)}, u32[]{:S(2)}) collective-permute-start(bf16[2,16,16,128]{3,2,1,0:T(8,128)(2,1)S(1)} %get-tuple-element.29), channel_id=1, source_target_pairs={{0,4},{1,5},{2,30},{3,31},{4,8},{5,9},{6,2},{7,3},{8,12},{9,13},{1... | collective-permute-start | bytes 393224 | tf_op jit(solution)/shard_map/ppermute | solution.py:281
  43.9 20.3 %collective-permute-start.2 = (bf16[2,16,16,128]{3,2,1,0:T(8,128)(2,1)S(1)}, bf16[2,16,16,128]{3,2,1,0:T(8,128)(2,1)S(1)}, u32[]{:S(2)}, u32[]{:S(2)}) collective-permute-start(bf16[2,16,16,128]{3,2,1,0:T(8,128)(2,1)S(1)} %get-tuple-element.30), channel_id=1, source_target_pairs={{0,26},{1,27},{2,8},{3,9},{4,30},{5,31},{6,12},{7,13},{8,2},{9,3},... | collective-permute-start | bytes 393224 | tf_op jit(solution)/shard_map/ppermute | solution.py:281
  54.8 18.7 %collective-permute-start.15 = (bf16[8,16,16,128]{3,2,1,0:T(8,128)(2,1)S(1)}, bf16[8,16,16,128]{3,2,1,0:T(8,128)(2,1)S(1)}, u32[]{:S(2)}, u32[]{:S(2)}) collective-permute-start(bf16[8,16,16,128]{3,2,1,0:T(8,128)(2,1)S(1)} %constant_dynamic-update-slice_fusion.4.own_ref), channel_id=1, source_target_pairs={{0,2},{1,3},{2,0},{3,1},{4,6},{5,7},{6,4},{7,5},{8,10},{9,11},{10,... | collective-permute-start | bytes 1572872 | tf_op jit(solution)/shard_map/ppermute | solution.py:267
  64.2 20.2 %collective-permute-start.4 = (bf16[8,16,16,128]{3,2,1,0:T(8,128)(2,1)S(1)}, bf16[8,16,16,128]{3,2,1,0:T(8,128)(2,1)S(1)}, u32[]{:S(2)}, u32[]{:S(2)}) collective-permute-start(bf16[8,16,16,128]{3,2,1,0:T(8,128)(2,1)S(1)} %constant_dynamic-update-slice_fusion.own_ref), channel_id=1, source_target_pairs={{0,2},{1,3},{2,0},{3,1},{4,6},{5,7},{6,4},{7,5},{8,10},{9,11},{10,... | collective-permute-start | bytes 1572872 | tf_op jit(solution)/shard_map/ppermute | solution.py:267
  69.9 16.4 %collective-permute-start.14 = (bf16[8,16,16,128]{3,2,1,0:T(8,128)(2,1)S(1)}, bf16[8,16,16,128]{3,2,1,0:T(8,128)(2,1)S(1)}, u32[]{:S(2)}, u32[]{:S(2)}) collective-permute-start(bf16[8,16,16,128]{3,2,1,0:T(8,128)(2,1)S(1)} %constant_dynamic-update-slice_fusion.4.own_ref), channel_id=1, source_target_pairs={{0,1},{1,0},{2,3},{3,2},{4,5},{5,4},{6,7},{7,6},{8,9},{9,8},{10,11... | collective-permute-start | bytes 1572872 | tf_op jit(solution)/shard_map/ppermute | solution.py:267
  73.5 12.8 %collective-permute-start.16 = (bf16[8,16,16,128]{3,2,1,0:T(8,128)(2,1)S(1)}, bf16[8,16,16,128]{3,2,1,0:T(8,128)(2,1)S(1)}, u32[]{:S(2)}, u32[]{:S(2)}) collective-permute-start(bf16[8,16,16,128]{3,2,1,0:T(8,128)(2,1)S(1)} %collective-permute-done.15.chip_ref), channel_id=1, source_target_pairs={{0,1},{1,0},{2,3},{3,2},{4,5},{5,4},{6,7},{7,6},{8,9},{9,8},{10,11... | collective-permute-start | bytes 1572872 | tf_op jit(solution)/shard_map/ppermute | solution.py:267
  75.5 17.5 %collective-permute-start.3 = (bf16[8,16,16,128]{3,2,1,0:T(8,128)(2,1)S(1)}, bf16[8,16,16,128]{3,2,1,0:T(8,128)(2,1)S(1)}, u32[]{:S(2)}, u32[]{:S(2)}) collective-permute-start(bf16[8,16,16,128]{3,2,1,0:T(8,128)(2,1)S(1)} %constant_dynamic-update-slice_fusion.own_ref), channel_id=1, source_target_pairs={{0,1},{1,0},{2,3},{3,2},{4,5},{5,4},{6,7},{7,6},{8,9},{9,8},{10,11... | collective-permute-start | bytes 1572872 | tf_op jit(solution)/shard_map/ppermute | solution.py:267
  84.4 8.6 %collective-permute-start.5 = (bf16[8,16,16,128]{3,2,1,0:T(8,128)(2,1)S(1)}, bf16[8,16,16,128]{3,2,1,0:T(8,128)(2,1)S(1)}, u32[]{:S(2)}, u32[]{:S(2)}) collective-permute-start(bf16[8,16,16,128]{3,2,1,0:T(8,128)(2,1)S(1)} %collective-permute-done.4.chip_ref), channel_id=1, source_target_pairs={{0,1},{1,0},{2,3},{3,2},{4,5},{5,4},{6,7},{7,6},{8,9},{9,8},{10,11... | collective-permute-start | bytes 1572872 | tf_op jit(solution)/shard_map/ppermute | solution.py:267
  90.6 13.0 %collective-permute-start.18 = (bf16[8,16,16,128]{3,2,1,0:T(8,128)(2,1)S(1)}, bf16[8,16,16,128]{3,2,1,0:T(8,128)(2,1)S(1)}, u32[]{:S(2)}, u32[]{:S(2)}) collective-permute-start(bf16[8,16,16,128]{3,2,1,0:T(8,128)(2,1)S(1)} %get-tuple-element.42), channel_id=1, source_target_pairs={{0,1},{1,0},{2,3},{3,2},{4,5},{5,4},{6,7},{7,6},{8,9},{9,8},{10,11... | collective-permute-start | bytes 1572872 | tf_op jit(solution)/shard_map/ppermute | solution.py:267
  97.3 10.4 %collective-permute-start.7 = (bf16[8,16,16,128]{3,2,1,0:T(8,128)(2,1)S(1)}, bf16[8,16,16,128]{3,2,1,0:T(8,128)(2,1)S(1)}, u32[]{:S(2)}, u32[]{:S(2)}) collective-permute-start(bf16[8,16,16,128]{3,2,1,0:T(8,128)(2,1)S(1)} %get-tuple-element.34), channel_id=1, source_target_pairs={{0,1},{1,0},{2,3},{3,2},{4,5},{5,4},{6,7},{7,6},{8,9},{9,8},{10,11... | collective-permute-start | bytes 1572872 | tf_op jit(solution)/shard_map/ppermute | solution.py:267
  99.2 10.5 %collective-permute-start.17 = (bf16[8,16,16,128]{3,2,1,0:T(8,128)(2,1)S(1)}, bf16[8,16,16,128]{3,2,1,0:T(8,128)(2,1)S(1)}, u32[]{:S(2)}, u32[]{:S(2)}) collective-permute-start(bf16[8,16,16,128]{3,2,1,0:T(8,128)(2,1)S(1)} %get-tuple-element.40), channel_id=1, source_target_pairs={{0,1},{1,0},{2,3},{3,2},{4,5},{5,4},{6,7},{7,6},{8,9},{9,8},{10,11... | collective-permute-start | bytes 1572872 | tf_op jit(solution)/shard_map/ppermute | solution.py:267
  101.6 8.3 %collective-permute-start.6 = (bf16[8,16,16,128]{3,2,1,0:T(8,128)(2,1)S(1)}, bf16[8,16,16,128]{3,2,1,0:T(8,128)(2,1)S(1)}, u32[]{:S(2)}, u32[]{:S(2)}) collective-permute-start(bf16[8,16,16,128]{3,2,1,0:T(8,128)(2,1)S(1)} %get-tuple-element.32), channel_id=1, source_target_pairs={{0,1},{1,0},{2,3},{3,2},{4,5},{5,4},{6,7},{7,6},{8,9},{9,8},{10,11... | collective-permute-start | bytes 1572872 | tf_op jit(solution)/shard_map/ppermute | solution.py:267
  103.7 16.7 %collective-permute-start.19 = (bf16[8,16,16,128]{3,2,1,0:T(8,128)(2,1)S(1)}, bf16[8,16,16,128]{3,2,1,0:T(8,128)(2,1)S(1)}, u32[]{:S(2)}, u32[]{:S(2)}) collective-permute-start(bf16[8,16,16,128]{3,2,1,0:T(8,128)(2,1)S(1)} %add_convert_fusion), channel_id=1, source_target_pairs={{0,2},{1,3},{2,0},{3,1},{4,6},{5,7},{6,4},{7,5},{8,10},{9,11},{10,... | collective-permute-start | bytes 1572872 | tf_op jit(solution)/shard_map/ppermute | solution.py:267
  107.8 50.2 %collective-permute-start.8 = (bf16[8,16,16,128]{3,2,1,0:T(8,128)(2,1)S(1)}, bf16[8,16,16,128]{3,2,1,0:T(8,128)(2,1)S(1)}, u32[]{:S(2)}, u32[]{:S(2)}) collective-permute-start(bf16[8,16,16,128]{3,2,1,0:T(8,128)(2,1)S(1)} %add_convert_fusion.2), channel_id=1, source_target_pairs={{0,2},{1,3},{2,0},{3,1},{4,6},{5,7},{6,4},{7,5},{8,10},{9,11},{10,... | collective-permute-start | bytes 1572872 | tf_op jit(solution)/shard_map/ppermute | solution.py:267
  120.5 42.7 %collective-permute-start.20 = (bf16[2,16,16,128]{3,2,1,0:T(8,128)(2,1)S(1)}, bf16[2,16,16,128]{3,2,1,0:T(8,128)(2,1)S(1)}, u32[]{:S(2)}, u32[]{:S(2)}) collective-permute-start(bf16[2,16,16,128]{3,2,1,0:T(8,128)(2,1)S(1)} %get-tuple-element.52), channel_id=1, source_target_pairs={{8,0},{9,1},{26,2},{27,3},{12,4},{13,5},{30,6},{31,7},{16,8},{17,9... | collective-permute-start | bytes 393224 | tf_op jit(solution)/shard_map/ppermute | solution.py:281
  128.6 36.9 %collective-permute-start.21 = (bf16[2,16,16,128]{3,2,1,0:T(8,128)(2,1)S(1)}, bf16[2,16,16,128]{3,2,1,0:T(8,128)(2,1)S(1)}, u32[]{:S(2)}, u32[]{:S(2)}) collective-permute-start(bf16[2,16,16,128]{3,2,1,0:T(8,128)(2,1)S(1)} %get-tuple-element.51), channel_id=1, source_target_pairs={{12,0},{13,1},{22,2},{23,3},{16,4},{17,5},{26,6},{27,7},{20,8},{21... | collective-permute-start | bytes 393224 | tf_op jit(solution)/shard_map/ppermute | solution.py:281
  134.5 35.0 %collective-permute-start.22 = (bf16[2,16,16,128]{3,2,1,0:T(8,128)(2,1)S(1)}, bf16[2,16,16,128]{3,2,1,0:T(8,128)(2,1)S(1)}, u32[]{:S(2)}, u32[]{:S(2)}) collective-permute-start(bf16[2,16,16,128]{3,2,1,0:T(8,128)(2,1)S(1)} %get-tuple-element.50), channel_id=1, source_target_pairs={{18,0},{19,1},{16,2},{17,3},{22,4},{23,5},{20,6},{21,7},{26,8},{27... | collective-permute-start | bytes 393224 | tf_op jit(solution)/shard_map/ppermute | solution.py:281
  139.7 29.8 %collective-permute-start.23 = (bf16[2,16,16,128]{3,2,1,0:T(8,128)(2,1)S(1)}, bf16[2,16,16,128]{3,2,1,0:T(8,128)(2,1)S(1)}, u32[]{:S(2)}, u32[]{:S(2)}) collective-permute-start(bf16[2,16,16,128]{3,2,1,0:T(8,128)(2,1)S(1)} %get-tuple-element.49), channel_id=1, source_target_pairs={{22,0},{23,1},{12,2},{13,3},{26,4},{27,5},{16,6},{17,7},{30,8},{31... | collective-permute-start | bytes 393224 | tf_op jit(solution)/shard_map/ppermute | solution.py:281
  158.2 15.2 %collective-permute-start.24 = (bf16[2,16,16,128]{3,2,1,0:T(8,128)(2,1)S(1)}, bf16[2,16,16,128]{3,2,1,0:T(8,128)(2,1)S(1)}, u32[]{:S(2)}, u32[]{:S(2)}) collective-permute-start(bf16[2,16,16,128]{3,2,1,0:T(8,128)(2,1)S(1)} %get-tuple-element.46), channel_id=1, source_target_pairs={{26,0},{27,1},{8,2},{9,3},{30,4},{31,5},{12,6},{13,7},{2,8},{3,9},... | collective-permute-start | bytes 393224 | tf_op jit(solution)/shard_map/ppermute | solution.py:281
  163.2 10.1 %collective-permute-start.25 = (bf16[2,16,16,128]{3,2,1,0:T(8,128)(2,1)S(1)}, bf16[2,16,16,128]{3,2,1,0:T(8,128)(2,1)S(1)}, u32[]{:S(2)}, u32[]{:S(2)}) collective-permute-start(bf16[2,16,16,128]{3,2,1,0:T(8,128)(2,1)S(1)} %get-tuple-element.45), channel_id=1, source_target_pairs={{30,0},{31,1},{4,2},{5,3},{2,4},{3,5},{8,6},{9,7},{6,8},{7,9},{12,... | collective-permute-start | bytes 393224 | tf_op jit(solution)/shard_map/ppermute | solution.py:281
  165.5 12.1 %collective-permute-start.9 = (bf16[2,16,16,128]{3,2,1,0:T(8,128)(2,1)S(1)}, bf16[2,16,16,128]{3,2,1,0:T(8,128)(2,1)S(1)}, u32[]{:S(2)}, u32[]{:S(2)}) collective-permute-start(bf16[2,16,16,128]{3,2,1,0:T(8,128)(2,1)S(1)} %get-tuple-element.47), channel_id=1, source_target_pairs={{4,0},{5,1},{30,2},{31,3},{8,4},{9,5},{2,6},{3,7},{12,8},{13,9},{6... | collective-permute-start | bytes 393224 | tf_op jit(solution)/shard_map/ppermute | solution.py:281
  178.4 11.6 %collective-permute-start.26 = (bf16[48,3584]{1,0:T(8,128)(2,1)S(1)}, bf16[48,3584]{1,0:T(8,128)(2,1)S(1)}, u32[]{:S(2)}, u32[]{:S(2)}) collective-permute-start(bf16[48,3584]{1,0:T(8,128)(2,1)S(1)} %get-tuple-element.44), channel_id=1, source_target_pairs={{0,32},{32,64},{64,96},{96,128},{128,160},{160,192},{192,224},{224... | collective-permute-start | bytes 1032200 | tf_op jit(solution)/shard_map/ppermute | solution.py:263
  181.5 13.5 %collective-permute-start.27 = (bf16[48,3584]{1,0:T(8,128)(2,1)S(1)}, bf16[48,3584]{1,0:T(8,128)(2,1)S(1)}, u32[]{:S(2)}, u32[]{:S(2)}) collective-permute-start(bf16[48,3584]{1,0:T(8,128)(2,1)S(1)} %get-tuple-element.43), channel_id=1, source_target_pairs={{32,0},{64,32},{96,64},{128,96},{160,128},{192,160},{224,192},{256... | collective-permute-start | bytes 1032200 | tf_op jit(solution)/shard_map/ppermute | solution.py:263

commit v4 on v3

--- a/solution.py
+++ b/solution.py
@@ -124,12 +124,12 @@
         packet_ref[pairs:] = last.reshape(2, 16, LANES)
 
 
-def expert_kernel(own_ref, core_ref, chip_ref, both_ref, up_ref, down_ref, *rest):
-    outs, rows_ref = rest[:4], rest[4]
-    ins = (own_ref, core_ref, chip_ref, both_ref)
-    experts = own_ref.shape[0]
+def expert_kernel(own_ref, chip_ref, *rest):
+    ups, downs, outs, rows_ref = rest[:2], rest[2:4], rest[4:6], rest[6]
+    ins = (own_ref, chip_ref)
+    packets = own_ref.shape[0]
     pairs = own_ref.shape[1] - 2
-    main = experts * MAIN
+    main = packets * MAIN
     tails = [read_tail(ref) for ref in ins]
     for pair in range(pairs):
         columns = slice(pair * 256, (pair + 1) * 256)
@@ -138,21 +138,27 @@
         for half in range(2):
             chunk = 2 * pair + half
             block = jnp.concatenate(
-                [tail[chunk * experts : (chunk + 1) * experts] for tail in tails], axis=0
+                [tail[chunk * packets : (chunk + 1) * packets] for tail in tails], axis=0
             )
-            rows_ref[4 * main :, chunk * LANES : (chunk + 1) * LANES] = block.astype(jnp.bfloat16)
-    hidden_pre = jnp.dot(rows_ref[...], up_ref[0], preferred_element_type=jnp.float32)
-    activated = (hidden_pre / (1.0 + jnp.exp(-hidden_pre))).astype(jnp.bfloat16)
+            rows_ref[2 * main :, chunk * LANES : (chunk + 1) * LANES] = block.astype(jnp.bfloat16)
+    rows = rows_ref[...]
+    activated = []
+    for up_ref in ups:
+        hidden_pre = jnp.dot(rows, up_ref[0], preferred_element_type=jnp.float32)
+        activated.append((hidden_pre / (1.0 + jnp.exp(-hidden_pre))).astype(jnp.bfloat16))
     tail_chunks = [[] for _ in ins]
     for pair in range(pairs):
         columns = slice(pair * 256, (pair + 1) * 256)
-        partial = jnp.dot(activated, down_ref[0, :, columns], preferred_element_type=jnp.float32)
+        partial = sum(
+            jnp.dot(part, down_ref[0, :, columns], preferred_element_type=jnp.float32)
+            for part, down_ref in zip(activated, downs)
+        )
         for index, ref in enumerate(outs):
             write_packet(ref, pair, partial[index * main : (index + 1) * main])
-            first = 4 * main + index * experts
+            first = 2 * main + index * packets
             for half in range(2):
                 tail_chunks[index].append(
-                    partial[first : first + experts, half * LANES : (half + 1) * LANES]
+                    partial[first : first + packets, half * LANES : (half + 1) * LANES]
                 )
     for index, ref in enumerate(outs):
         write_tail(ref, jnp.concatenate(tail_chunks[index], axis=0).astype(jnp.bfloat16))
@@ -225,21 +231,21 @@
     return gate, row, packets
 
 
-def run_expert(own, core, chip, both, up, down):
-    experts = own.shape[0]
+def run_expert(own, chip, ups, downs):
     packet = jax.ShapeDtypeStruct(own.shape, own.dtype)
-    rows = 4 * experts * (MAIN + 1)
-    width = up.shape[1]
+    rows = 2 * own.shape[0] * (MAIN + 1)
+    width = ups[0].shape[1]
+    operands = (own, chip, *ups, *downs)
     return pl.pallas_call(
         expert_kernel,
         grid=(1,),
-        out_shape=(packet,) * 4,
-        in_specs=[whole(a) for a in (own, core, chip, both, up, down)],
-        out_specs=(whole(packet),) * 4,
+        out_shape=(packet,) * 2,
+        in_specs=[whole(a) for a in operands],
+        out_specs=(whole(packet),) * 2,
         scratch_shapes=[pltpu.VMEM((rows, width), jnp.bfloat16)],
         compiler_params=params(),
         name="expert",
-    )(own, core, chip, both, up, down)
+    )(*operands)
 
 
 def finish(carried, gate, row, packets):
@@ -294,18 +300,15 @@
     gate, row, packets = prepare(carried, norm_gain, router, expert_ids, turns, experts)
     arrived = [delivered(packet, turn, False) for turn, packet in enumerate(packets)]
     returned = [None] * experts
+    ups = (w_up, swapped(w_up, 1))
+    downs = (w_down, swapped(w_down, 1))
     for group in GROUPS:
         own = jnp.concatenate([arrived[turn] for turn in group], axis=0)
-        chip = swapped(own, 2)
-        core = swapped(own, 1)
-        both = swapped(chip, 1)
-        for_own, for_core, for_chip, for_both = run_expert(own, core, chip, both, w_up, w_down)
-        own_sum = added(for_own, swapped(for_core, 1))
-        chip_sum = added(for_chip, swapped(for_both, 1))
-        from_chip = swapped(chip_sum, 2)
+        for_own, for_chip = run_expert(own, swapped(own, 2), ups, downs)
+        from_chip = swapped(for_chip, 2)
         for place, turn in enumerate(group):
             part = slice(2 * place, 2 * place + 2)
-            returned[turn] = delivered(added(own_sum[part], from_chip[part]), turn, True)
+            returned[turn] = delivered(added(for_own[part], from_chip[part]), turn, True)
     layer_outputs = finish(carried, gate, row, returned)
     section_index = lax.axis_index("section")
     last_section = lax.axis_size("section") - 1

time: 197 us -> 180 us (0.914)
  starting transfers between devices: 116 us -> 107 us
  waiting for transfers between devices: 62.7 us -> 55.3 us
    ppermute x12 -> x6, starting transfers between devices: 32.3 us -> 12.4 us  [swapped(): lax.ppermute(block, 'expert', [(i, i ^ bit) for i in range(lax.axis_size(...]
    ppermute x14, starting transfers between devices: 77.9 us -> 88.4 us  [delivered(): return lax.ppermute(packet, 'expert', route)]
    ppermute x14, waiting for transfers between devices: 20.5 us -> 17.5 us  [delivered(): return lax.ppermute(packet, 'expert', route)]
    ppermute x12 -> x6, waiting for transfers between devices: 31.5 us -> 29.3 us  [swapped(): lax.ppermute(block, 'expert', [(i, i ^ bit) for i in range(lax.axis_size(...]
    ppermute x2, waiting for transfers between devices: 10.7 us -> 8.5 us  [passed_along(): return lax.ppermute(block, axis, route)]
  transfers between devices with their start and end apart: 28 -> 22, of which waited for: 12 -> 13; matrix products, arithmetic and copies ran while one was open for 1% -> 2% of each run, Pallas kernels for 4% -> 5%
where the time goes in v4:
time: 180 us; the launch traced here: 178 us
  starting transfers between devices  107 us (59%)
  waiting for transfers between devices  55.3 us (31%)
  Pallas kernels  10 us (6%)
  local copies, waits for them, and re-layouts  3.69 us (2%)
  other arithmetic  1.98 us (1%)
    ppermute x14, starting transfers between devices, delivered(): return lax.ppermute(packet, 'expert', route)  88.4 us
    ppermute x6, waiting for transfers between devices, swapped(): lax.ppermute(block, 'expert', [(i, i ^ bit) for i in range(lax.axis_size(...  29.3 us
    ppermute x14, waiting for transfers between devices, delivered(): return lax.ppermute(packet, 'expert', route)  17.5 us
    ppermute x6, starting transfers between devices, swapped(): lax.ppermute(block, 'expert', [(i, i ^ bit) for i in range(lax.axis_size(...  12.4 us
    ppermute x2, waiting for transfers between devices, passed_along(): return lax.ppermute(block, axis, route)  8.5 us
    pallas_call x2, Pallas kernels, run_expert(): pl.pallas_call(expert_kernel, grid=(1,), out_shape=(packet,) * 2, in_spec...  7.44 us
    ppermute x2, starting transfers between devices, passed_along(): return lax.ppermute(block, axis, route)  5.84 us
  transfers between devices with their start and end apart: 22, of which 13 were waited for; matrix products, arithmetic and copies ran while one was open for 2% of the time, Pallas kernels for 5%

profile of v4, /device:TPU:24, one launch (start us, length us, event | category | flops | bytes accessed | tf_op | source)
XLA Modules:
  0.0 178.0 jit_solution(409534302248485198)
XLA Ops:
  0.0 0.0 copy-start.1
  0.0 2.0 %collective-permute-start.4 = (bf16[1,3584,256]{2,1,0:T(8,128)(2,1)}, bf16[1,3584,256]{2,1,0:T(8,128)(2,1)S(1)}, u32[]{:S(2)}, u32[]{:S(2)}) collective-permute-start(bf16[1,3584,256]{2,1,0:T(8,128)(2,1)} %rest_0_.3), channel_id=1, source_target_pairs={{0,1},{1,0},{2,3},{3,2},{4,5},{5,4},{6,7},{7,6},{8,9},{9,8},{10,11... | collective-permute-start | bytes 5505032 | tf_op jit(solution)/shard_map/ppermute | solution.py:273
  2.1 2.4 %collective-permute-start.5 = (bf16[1,256,3584]{2,1,0:T(8,128)(2,1)}, bf16[1,256,3584]{2,1,0:T(8,128)(2,1)}, u32[]{:S(2)}, u32[]{:S(2)}) collective-permute-start(bf16[1,256,3584]{2,1,0:T(8,128)(2,1)} %rest_2_.3), channel_id=1, source_target_pairs={{0,1},{1,0},{2,3},{3,2},{4,5},{5,4},{6,7},{7,6},{8,9},{9,8},{10,11... | collective-permute-start | bytes 5505032 | tf_op jit(solution)/shard_map/ppermute | solution.py:273
  4.5 0.8 copy.19.ids_ref
  5.3 0.7 fusion.1
  6.0 0.1 copy.16
  6.1 0.7 copy.17
  6.8 1.2 copy.18.router_ref
  8.1 0.0 copy-done.1
  8.1 0.0 copy-start.2
  8.1 0.7 copy-done.2
  8.8 0.0 copy-start
  8.8 1.7 prepare.1
  10.6 9.1 %collective-permute-start.8 = (bf16[2,16,16,128]{3,2,1,0:T(8,128)(2,1)S(1)}, bf16[2,16,16,128]{3,2,1,0:T(8,128)(2,1)S(1)}, u32[]{:S(2)}, u32[]{:S(2)}) collective-permute-start(bf16[2,16,16,128]{3,2,1,0:T(8,128)(2,1)S(1)} %get-tuple-element.29), channel_id=1, source_target_pairs={{0,8},{1,9},{2,26},{3,27},{4,12},{5,13},{6,30},{7,31},{8,16},{9,17... | collective-permute-start | bytes 393224 | tf_op jit(solution)/shard_map/ppermute | solution.py:287
  19.7 9.4 %collective-permute-start.9 = (bf16[2,16,16,128]{3,2,1,0:T(8,128)(2,1)S(1)}, bf16[2,16,16,128]{3,2,1,0:T(8,128)(2,1)S(1)}, u32[]{:S(2)}, u32[]{:S(2)}) collective-permute-start(bf16[2,16,16,128]{3,2,1,0:T(8,128)(2,1)S(1)} %get-tuple-element.30), channel_id=1, source_target_pairs={{0,22},{1,23},{2,12},{3,13},{4,26},{5,27},{6,16},{7,17},{8,30},{9,... | collective-permute-start | bytes 393224 | tf_op jit(solution)/shard_map/ppermute | solution.py:287
  29.1 6.1 %collective-permute-start.10 = (bf16[2,16,16,128]{3,2,1,0:T(8,128)(2,1)S(1)}, bf16[2,16,16,128]{3,2,1,0:T(8,128)(2,1)S(1)}, u32[]{:S(2)}, u32[]{:S(2)}) collective-permute-start(bf16[2,16,16,128]{3,2,1,0:T(8,128)(2,1)S(1)} %get-tuple-element.31), channel_id=1, source_target_pairs={{0,12},{1,13},{2,22},{3,23},{4,16},{5,17},{6,26},{7,27},{8,20},{9,... | collective-permute-start | bytes 393224 | tf_op jit(solution)/shard_map/ppermute | solution.py:287
  35.2 0.0 collective-permute-done.8
  35.2 7.2 %collective-permute-start.11 = (bf16[2,16,16,128]{3,2,1,0:T(8,128)(2,1)S(1)}, bf16[2,16,16,128]{3,2,1,0:T(8,128)(2,1)S(1)}, u32[]{:S(2)}, u32[]{:S(2)}) collective-permute-start(bf16[2,16,16,128]{3,2,1,0:T(8,128)(2,1)S(1)} %get-tuple-element.32), channel_id=1, source_target_pairs={{0,18},{1,19},{2,16},{3,17},{4,22},{5,23},{6,20},{7,21},{8,26},{9,... | collective-permute-start | bytes 393224 | tf_op jit(solution)/shard_map/ppermute | solution.py:287
  42.5 7.0 %collective-permute-done.9 = bf16[2,16,16,128]{3,2,1,0:T(8,128)(2,1)S(1)} collective-permute-done((bf16[2,16,16,128]{3,2,1,0:T(8,128)(2,1)S(1)}, bf16[2,16,16,128]{3,2,1,0:T(8,128)(2,1)S(1)}, u32[]{:S(2)}, u32[]{:S(2)}) %collective-permute-start.9) | collective-permute-done | bytes 131104 | tf_op jit(solution)/shard_map/ppermute | solution.py:287
  49.5 1.9 %collective-permute-start = (bf16[2,16,16,128]{3,2,1,0:T(8,128)(2,1)S(1)}, bf16[2,16,16,128]{3,2,1,0:T(8,128)(2,1)S(1)}, u32[]{:S(2)}, u32[]{:S(2)}) collective-permute-start(bf16[2,16,16,128]{3,2,1,0:T(8,128)(2,1)S(1)} %get-tuple-element.24), channel_id=1, source_target_pairs={{0,30},{1,31},{2,4},{3,5},{4,2},{5,3},{6,8},{7,9},{8,6},{9,7},{10,... | collective-permute-start | bytes 393224 | tf_op jit(solution)/shard_map/ppermute | solution.py:287
  51.5 0.0 collective-permute-done.10
  51.5 4.1 %collective-permute-start.1 = (bf16[2,16,16,128]{3,2,1,0:T(8,128)(2,1)S(1)}, bf16[2,16,16,128]{3,2,1,0:T(8,128)(2,1)S(1)}, u32[]{:S(2)}, u32[]{:S(2)}) collective-permute-start(bf16[2,16,16,128]{3,2,1,0:T(8,128)(2,1)S(1)} %get-tuple-element.25), channel_id=1, source_target_pairs={{0,4},{1,5},{2,30},{3,31},{4,8},{5,9},{6,2},{7,3},{8,12},{9,13},{1... | collective-permute-start | bytes 393224 | tf_op jit(solution)/shard_map/ppermute | solution.py:287
  55.6 1.0 collective-permute-done.11
  56.6 14.9 %collective-permute-start.2 = (bf16[2,16,16,128]{3,2,1,0:T(8,128)(2,1)S(1)}, bf16[2,16,16,128]{3,2,1,0:T(8,128)(2,1)S(1)}, u32[]{:S(2)}, u32[]{:S(2)}) collective-permute-start(bf16[2,16,16,128]{3,2,1,0:T(8,128)(2,1)S(1)} %get-tuple-element.26), channel_id=1, source_target_pairs={{0,26},{1,27},{2,8},{3,9},{4,30},{5,31},{6,12},{7,13},{8,2},{9,3},... | collective-permute-start | bytes 393224 | tf_op jit(solution)/shard_map/ppermute | solution.py:287
  71.6 0.0 collective-permute-done
  71.6 1.9 %collective-permute-start.12 = (bf16[8,16,16,128]{3,2,1,0:T(8,128)(2,1)S(1)}, bf16[8,16,16,128]{3,2,1,0:T(8,128)(2,1)S(1)}, u32[]{:S(2)}, u32[]{:S(2)}) collective-permute-start(bf16[8,16,16,128]{3,2,1,0:T(8,128)(2,1)S(1)} %constant_dynamic-update-slice_fusion.4.own_ref), channel_id=1, source_target_pairs={{0,2},{1,3},{2,0},{3,1},{4,6},{5,7},{6,4},{7,5},{8,10},{9,11},{10,... | collective-permute-start | bytes 1572872 | tf_op jit(solution)/shard_map/ppermute | solution.py:273
  73.5 0.0 collective-permute-done.1
  73.6 1.7 collective-permute-done.2
  75.3 2.2 %collective-permute-start.3 = (bf16[8,16,16,128]{3,2,1,0:T(8,128)(2,1)S(1)}, bf16[8,16,16,128]{3,2,1,0:T(8,128)(2,1)S(1)}, u32[]{:S(2)}, u32[]{:S(2)}) collective-permute-start(bf16[8,16,16,128]{3,2,1,0:T(8,128)(2,1)S(1)} %constant_dynamic-update-slice_fusion.own_ref), channel_id=1, source_target_pairs={{0,2},{1,3},{2,0},{3,1},{4,6},{5,7},{6,4},{7,5},{8,10},{9,11},{10,... | collective-permute-start | bytes 1572872 | tf_op jit(solution)/shard_map/ppermute | solution.py:273
  77.5 10.8 %collective-permute-done.12.chip_ref = bf16[8,16,16,128]{3,2,1,0:T(8,128)(2,1)S(1)} collective-permute-done((bf16[8,16,16,128]{3,2,1,0:T(8,128)(2,1)S(1)}, bf16[8,16,16,128]{3,2,1,0:T(8,128)(2,1)S(1)}, u32[]{:S(2)}, u32[]{:S(2)}) %collective-permute-start.12) | collective-permute-done | bytes 524320 | tf_op jit(solution)/shard_map/ppermute | solution.py:273
  88.3 0.0 collective-permute-done.4.rest_1_
  88.3 0.0 collective-permute-done.5.rest_3_
  88.3 0.0 copy-done
  88.3 3.7 %expert.3 = (bf16[8,16,16,128]{3,2,1,0:T(8,128)(2,1)S(1)}, bf16[8,16,16,128]{3,2,1,0:T(8,128)(2,1)S(1)}) custom-call(bf16[8,16,16,128]{3,2,1,0:T(8,128)(2,1)S(1)} %constant_dynamic-update-slice_fusion.4.own_ref, bf16[8,16,16,128]{3,2,1,0:T(8,128)(2,1)S(1)} %collective-permute-done.12.chip_ref, bf16[1,3584,256]{2,1,0:T(8,128)(2,1)S(1)} %copy-done, ...), custom_call_target="tpu_custom_call" | custom-call | tf_op jit(solution)/shard_map/expert/pallas_call | solution.py:239
  92.1 1.9 %collective-permute-start.13 = (bf16[8,16,16,128]{3,2,1,0:T(8,128)(2,1)S(1)}, bf16[8,16,16,128]{3,2,1,0:T(8,128)(2,1)S(1)}, u32[]{:S(2)}, u32[]{:S(2)}) collective-permute-start(bf16[8,16,16,128]{3,2,1,0:T(8,128)(2,1)S(1)} %get-tuple-element.34), channel_id=1, source_target_pairs={{0,2},{1,3},{2,0},{3,1},{4,6},{5,7},{6,4},{7,5},{8,10},{9,11},{10,... | collective-permute-start | bytes 1572872 | tf_op jit(solution)/shard_map/ppermute | solution.py:273
  94.0 5.6 %collective-permute-done.3.chip_ref = bf16[8,16,16,128]{3,2,1,0:T(8,128)(2,1)S(1)} collective-permute-done((bf16[8,16,16,128]{3,2,1,0:T(8,128)(2,1)S(1)}, bf16[8,16,16,128]{3,2,1,0:T(8,128)(2,1)S(1)}, u32[]{:S(2)}, u32[]{:S(2)}) %collective-permute-start.3) | collective-permute-done | bytes 524320 | tf_op jit(solution)/shard_map/ppermute | solution.py:273
  99.6 3.7 %expert.2 = (bf16[8,16,16,128]{3,2,1,0:T(8,128)(2,1)S(1)}, bf16[8,16,16,128]{3,2,1,0:T(8,128)(2,1)S(1)}) custom-call(bf16[8,16,16,128]{3,2,1,0:T(8,128)(2,1)S(1)} %constant_dynamic-update-slice_fusion.own_ref, bf16[8,16,16,128]{3,2,1,0:T(8,128)(2,1)S(1)} %collective-permute-done.3.chip_ref, bf16[1,3584,256]{2,1,0:T(8,128)(2,1)S(1)} %copy-done, ...), custom_call_target="tpu_custom_call" | custom-call | tf_op jit(solution)/shard_map/expert/pallas_call | solution.py:239
  103.3 1.9 %collective-permute-start.6 = (bf16[8,16,16,128]{3,2,1,0:T(8,128)(2,1)S(1)}, bf16[8,16,16,128]{3,2,1,0:T(8,128)(2,1)S(1)}, u32[]{:S(2)}, u32[]{:S(2)}) collective-permute-start(bf16[8,16,16,128]{3,2,1,0:T(8,128)(2,1)S(1)} %get-tuple-element.28), channel_id=1, source_target_pairs={{0,2},{1,3},{2,0},{3,1},{4,6},{5,7},{6,4},{7,5},{8,10},{9,11},{10,... | collective-permute-start | bytes 1572872 | tf_op jit(solution)/shard_map/ppermute | solution.py:273
  105.2 5.6 %collective-permute-done.13 = bf16[8,16,16,128]{3,2,1,0:T(8,128)(2,1)S(1)} collective-permute-done((bf16[8,16,16,128]{3,2,1,0:T(8,128)(2,1)S(1)}, bf16[8,16,16,128]{3,2,1,0:T(8,128)(2,1)S(1)}, u32[]{:S(2)}, u32[]{:S(2)}) %collective-permute-start.13) | collective-permute-done | bytes 524320 | tf_op jit(solution)/shard_map/ppermute | solution.py:273
  110.8 0.1 add_convert_fusion.2
  110.9 1.9 %collective-permute-start.14 = (bf16[2,16,16,128]{3,2,1,0:T(8,128)(2,1)S(1)}, bf16[2,16,16,128]{3,2,1,0:T(8,128)(2,1)S(1)}, u32[]{:S(2)}, u32[]{:S(2)}) collective-permute-start(bf16[2,16,16,128]{3,2,1,0:T(8,128)(2,1)S(1)} %get-tuple-element.44), channel_id=1, source_target_pairs={{8,0},{9,1},{26,2},{27,3},{12,4},{13,5},{30,6},{31,7},{16,8},{17,9... | collective-permute-start | bytes 393224 | tf_op jit(solution)/shard_map/ppermute | solution.py:287
  112.9 8.7 %collective-permute-start.15 = (bf16[2,16,16,128]{3,2,1,0:T(8,128)(2,1)S(1)}, bf16[2,16,16,128]{3,2,1,0:T(8,128)(2,1)S(1)}, u32[]{:S(2)}, u32[]{:S(2)}) collective-permute-start(bf16[2,16,16,128]{3,2,1,0:T(8,128)(2,1)S(1)} %get-tuple-element.43), channel_id=1, source_target_pairs={{12,0},{13,1},{22,2},{23,3},{16,4},{17,5},{26,6},{27,7},{20,8},{21... | collective-permute-start | bytes 393224 | tf_op jit(solution)/shard_map/ppermute | solution.py:287
  121.5 6.0 %collective-permute-start.16 = (bf16[2,16,16,128]{3,2,1,0:T(8,128)(2,1)S(1)}, bf16[2,16,16,128]{3,2,1,0:T(8,128)(2,1)S(1)}, u32[]{:S(2)}, u32[]{:S(2)}) collective-permute-start(bf16[2,16,16,128]{3,2,1,0:T(8,128)(2,1)S(1)} %get-tuple-element.42), channel_id=1, source_target_pairs={{18,0},{19,1},{16,2},{17,3},{22,4},{23,5},{20,6},{21,7},{26,8},{27... | collective-permute-start | bytes 393224 | tf_op jit(solution)/shard_map/ppermute | solution.py:287
  127.5 7.5 %collective-permute-start.17 = (bf16[2,16,16,128]{3,2,1,0:T(8,128)(2,1)S(1)}, bf16[2,16,16,128]{3,2,1,0:T(8,128)(2,1)S(1)}, u32[]{:S(2)}, u32[]{:S(2)}) collective-permute-start(bf16[2,16,16,128]{3,2,1,0:T(8,128)(2,1)S(1)} %get-tuple-element.41), channel_id=1, source_target_pairs={{22,0},{23,1},{12,2},{13,3},{26,4},{27,5},{16,6},{17,7},{30,8},{31... | collective-permute-start | bytes 393224 | tf_op jit(solution)/shard_map/ppermute | solution.py:287
  135.0 7.3 %collective-permute-done.6 = bf16[8,16,16,128]{3,2,1,0:T(8,128)(2,1)S(1)} collective-permute-done((bf16[8,16,16,128]{3,2,1,0:T(8,128)(2,1)S(1)}, bf16[8,16,16,128]{3,2,1,0:T(8,128)(2,1)S(1)}, u32[]{:S(2)}, u32[]{:S(2)}) %collective-permute-start.6) | collective-permute-done | bytes 524320 | tf_op jit(solution)/shard_map/ppermute | solution.py:273
  142.3 0.1 add_convert_fusion
  142.4 1.9 %collective-permute-start.18 = (bf16[2,16,16,128]{3,2,1,0:T(8,128)(2,1)S(1)}, bf16[2,16,16,128]{3,2,1,0:T(8,128)(2,1)S(1)}, u32[]{:S(2)}, u32[]{:S(2)}) collective-permute-start(bf16[2,16,16,128]{3,2,1,0:T(8,128)(2,1)S(1)} %get-tuple-element.38), channel_id=1, source_target_pairs={{26,0},{27,1},{8,2},{9,3},{30,4},{31,5},{12,6},{13,7},{2,8},{3,9},... | collective-permute-start | bytes 393224 | tf_op jit(solution)/shard_map/ppermute | solution.py:287
  144.4 0.0 collective-permute-done.14.rest_2_
  144.4 7.8 %collective-permute-start.19 = (bf16[2,16,16,128]{3,2,1,0:T(8,128)(2,1)S(1)}, bf16[2,16,16,128]{3,2,1,0:T(8,128)(2,1)S(1)}, u32[]{:S(2)}, u32[]{:S(2)}) collective-permute-start(bf16[2,16,16,128]{3,2,1,0:T(8,128)(2,1)S(1)} %get-tuple-element.37), channel_id=1, source_target_pairs={{30,0},{31,1},{4,2},{5,3},{2,4},{3,5},{8,6},{9,7},{6,8},{7,9},{12,... | collective-permute-start | bytes 393224 | tf_op jit(solution)/shard_map/ppermute | solution.py:287
  152.2 0.0 collective-permute-done.15.rest_3_
  152.2 1.9 %collective-permute-start.7 = (bf16[2,16,16,128]{3,2,1,0:T(8,128)(2,1)S(1)}, bf16[2,16,16,128]{3,2,1,0:T(8,128)(2,1)S(1)}, u32[]{:S(2)}, u32[]{:S(2)}) collective-permute-start(bf16[2,16,16,128]{3,2,1,0:T(8,128)(2,1)S(1)} %get-tuple-element.39), channel_id=1, source_target_pairs={{4,0},{5,1},{30,2},{31,3},{8,4},{9,5},{2,6},{3,7},{12,8},{13,9},{6... | collective-permute-start | bytes 393224 | tf_op jit(solution)/shard_map/ppermute | solution.py:287
  154.1 0.0 collective-permute-done.16.rest_4_
  154.1 0.4 collective-permute-done.17.rest_5_
  154.5 0.9 collective-permute-done.18.rest_6_
  155.4 4.1 %collective-permute-done.19.rest_7_ = bf16[2,16,16,128]{3,2,1,0:T(8,128)(2,1)S(1)} collective-permute-done((bf16[2,16,16,128]{3,2,1,0:T(8,128)(2,1)S(1)}, bf16[2,16,16,128]{3,2,1,0:T(8,128)(2,1)S(1)}, u32[]{:S(2)}, u32[]{:S(2)}) %collective-permute-start.19) | collective-permute-done | bytes 131104 | tf_op jit(solution)/shard_map/ppermute | solution.py:287
  159.5 2.3 %collective-permute-done.7.rest_1_ = bf16[2,16,16,128]{3,2,1,0:T(8,128)(2,1)S(1)} collective-permute-done((bf16[2,16,16,128]{3,2,1,0:T(8,128)(2,1)S(1)}, bf16[2,16,16,128]{3,2,1,0:T(8,128)(2,1)S(1)}, u32[]{:S(2)}, u32[]{:S(2)}) %collective-permute-start.7) | collective-permute-done | bytes 131104 | tf_op jit(solution)/shard_map/ppermute | solution.py:287
  161.8 0.8 finish.1
  162.7 3.1 %collective-permute-start.20 = (bf16[48,3584]{1,0:T(8,128)(2,1)S(1)}, bf16[48,3584]{1,0:T(8,128)(2,1)S(1)}, u32[]{:S(2)}, u32[]{:S(2)}) collective-permute-start(bf16[48,3584]{1,0:T(8,128)(2,1)S(1)} %get-tuple-element.36), channel_id=1, source_target_pairs={{0,32},{32,64},{64,96},{96,128},{128,160},{160,192},{192,224},{224... | collective-permute-start | bytes 1032200 | tf_op jit(solution)/shard_map/ppermute | solution.py:269
  165.7 2.8 %collective-permute-start.21 = (bf16[48,3584]{1,0:T(8,128)(2,1)S(1)}, bf16[48,3584]{1,0:T(8,128)(2,1)S(1)}, u32[]{:S(2)}, u32[]{:S(2)}) collective-permute-start(bf16[48,3584]{1,0:T(8,128)(2,1)S(1)} %get-tuple-element.35), channel_id=1, source_target_pairs={{32,0},{64,32},{96,64},{128,96},{160,128},{192,160},{224,192},{256... | collective-permute-start | bytes 1032200 | tf_op jit(solution)/shard_map/ppermute | solution.py:269
  168.5 3.9 %collective-permute-done.20 = bf16[48,3584]{1,0:T(8,128)(2,1)S(1)} collective-permute-done((bf16[48,3584]{1,0:T(8,128)(2,1)S(1)}, bf16[48,3584]{1,0:T(8,128)(2,1)S(1)}, u32[]{:S(2)}, u32[]{:S(2)}) %collective-permute-start.20) | collective-permute-done | bytes 344096 | tf_op jit(solution)/shard_map/ppermute | solution.py:269
  172.5 4.6 %collective-permute-done.21 = bf16[48,3584]{1,0:T(8,128)(2,1)S(1)} collective-permute-done((bf16[48,3584]{1,0:T(8,128)(2,1)S(1)}, bf16[48,3584]{1,0:T(8,128)(2,1)S(1)}, u32[]{:S(2)}, u32[]{:S(2)}) %collective-permute-start.21) | collective-permute-done | bytes 344096 | tf_op jit(solution)/shard_map/ppermute | solution.py:269
  177.1 0.9 maximum_bitcast_fusion
  (12 shorter events, 0.2 us)
Async XLA Ops:
  0.0 8.1 %copy-start.1 = (bf16[2,1,48,3584]{3,2,1,0:T(8,128)(2,1)S(1)}, bf16[2,1,48,3584]{3,2,1,0:T(8,128)(2,1)}, u32[]{:S(2)}) copy-start(bf16[2,1,48,3584]{3,2,1,0:T(8,128)(2,1)} %x_ref.3) | copy-start | bytes 2064388
  0.0 88.3 %collective-permute-start.4 = (bf16[1,3584,256]{2,1,0:T(8,128)(2,1)}, bf16[1,3584,256]{2,1,0:T(8,128)(2,1)S(1)}, u32[]{:S(2)}, u32[]{:S(2)}) collective-permute-start(bf16[1,3584,256]{2,1,0:T(8,128)(2,1)} %rest_0_.3), channel_id=1, source_target_pairs={{0,1},{1,0},{2,3},{3,2},{4,5},{5,4},{6,7},{7,6},{8,9},{9,8},{10,11... | collective-permute-start | bytes 5505032 | tf_op jit(solution)/shard_map/ppermute | solution.py:273
  2.1 86.3 %collective-permute-start.5 = (bf16[1,256,3584]{2,1,0:T(8,128)(2,1)}, bf16[1,256,3584]{2,1,0:T(8,128)(2,1)}, u32[]{:S(2)}, u32[]{:S(2)}) collective-permute-start(bf16[1,256,3584]{2,1,0:T(8,128)(2,1)} %rest_2_.3), channel_id=1, source_target_pairs={{0,1},{1,0},{2,3},{3,2},{4,5},{5,4},{6,7},{7,6},{8,9},{9,8},{10,11... | collective-permute-start | bytes 5505032 | tf_op jit(solution)/shard_map/ppermute | solution.py:273
  8.1 0.7 copy-start.2
  8.8 79.5 %copy-start = (bf16[1,3584,256]{2,1,0:T(8,128)(2,1)S(1)}, bf16[1,3584,256]{2,1,0:T(8,128)(2,1)}, u32[]{:S(2)}) copy-start(bf16[1,3584,256]{2,1,0:T(8,128)(2,1)} %rest_0_.3) | copy-start | bytes 5505028
  10.6 24.7 %collective-permute-start.8 = (bf16[2,16,16,128]{3,2,1,0:T(8,128)(2,1)S(1)}, bf16[2,16,16,128]{3,2,1,0:T(8,128)(2,1)S(1)}, u32[]{:S(2)}, u32[]{:S(2)}) collective-permute-start(bf16[2,16,16,128]{3,2,1,0:T(8,128)(2,1)S(1)} %get-tuple-element.29), channel_id=1, source_target_pairs={{0,8},{1,9},{2,26},{3,27},{4,12},{5,13},{6,30},{7,31},{8,16},{9,17... | collective-permute-start | bytes 393224 | tf_op jit(solution)/shard_map/ppermute | solution.py:287
  19.7 29.8 %collective-permute-start.9 = (bf16[2,16,16,128]{3,2,1,0:T(8,128)(2,1)S(1)}, bf16[2,16,16,128]{3,2,1,0:T(8,128)(2,1)S(1)}, u32[]{:S(2)}, u32[]{:S(2)}) collective-permute-start(bf16[2,16,16,128]{3,2,1,0:T(8,128)(2,1)S(1)} %get-tuple-element.30), channel_id=1, source_target_pairs={{0,22},{1,23},{2,12},{3,13},{4,26},{5,27},{6,16},{7,17},{8,30},{9,... | collective-permute-start | bytes 393224 | tf_op jit(solution)/shard_map/ppermute | solution.py:287
  29.1 22.3 %collective-permute-start.10 = (bf16[2,16,16,128]{3,2,1,0:T(8,128)(2,1)S(1)}, bf16[2,16,16,128]{3,2,1,0:T(8,128)(2,1)S(1)}, u32[]{:S(2)}, u32[]{:S(2)}) collective-permute-start(bf16[2,16,16,128]{3,2,1,0:T(8,128)(2,1)S(1)} %get-tuple-element.31), channel_id=1, source_target_pairs={{0,12},{1,13},{2,22},{3,23},{4,16},{5,17},{6,26},{7,27},{8,20},{9,... | collective-permute-start | bytes 393224 | tf_op jit(solution)/shard_map/ppermute | solution.py:287
  35.2 21.4 %collective-permute-start.11 = (bf16[2,16,16,128]{3,2,1,0:T(8,128)(2,1)S(1)}, bf16[2,16,16,128]{3,2,1,0:T(8,128)(2,1)S(1)}, u32[]{:S(2)}, u32[]{:S(2)}) collective-permute-start(bf16[2,16,16,128]{3,2,1,0:T(8,128)(2,1)S(1)} %get-tuple-element.32), channel_id=1, source_target_pairs={{0,18},{1,19},{2,16},{3,17},{4,22},{5,23},{6,20},{7,21},{8,26},{9,... | collective-permute-start | bytes 393224 | tf_op jit(solution)/shard_map/ppermute | solution.py:287
  49.5 22.0 %collective-permute-start = (bf16[2,16,16,128]{3,2,1,0:T(8,128)(2,1)S(1)}, bf16[2,16,16,128]{3,2,1,0:T(8,128)(2,1)S(1)}, u32[]{:S(2)}, u32[]{:S(2)}) collective-permute-start(bf16[2,16,16,128]{3,2,1,0:T(8,128)(2,1)S(1)} %get-tuple-element.24), channel_id=1, source_target_pairs={{0,30},{1,31},{2,4},{3,5},{4,2},{5,3},{6,8},{7,9},{8,6},{9,7},{10,... | collective-permute-start | bytes 393224 | tf_op jit(solution)/shard_map/ppermute | solution.py:287
  51.5 22.1 %collective-permute-start.1 = (bf16[2,16,16,128]{3,2,1,0:T(8,128)(2,1)S(1)}, bf16[2,16,16,128]{3,2,1,0:T(8,128)(2,1)S(1)}, u32[]{:S(2)}, u32[]{:S(2)}) collective-permute-start(bf16[2,16,16,128]{3,2,1,0:T(8,128)(2,1)S(1)} %get-tuple-element.25), channel_id=1, source_target_pairs={{0,4},{1,5},{2,30},{3,31},{4,8},{5,9},{6,2},{7,3},{8,12},{9,13},{1... | collective-permute-start | bytes 393224 | tf_op jit(solution)/shard_map/ppermute | solution.py:287
  56.6 18.7 %collective-permute-start.2 = (bf16[2,16,16,128]{3,2,1,0:T(8,128)(2,1)S(1)}, bf16[2,16,16,128]{3,2,1,0:T(8,128)(2,1)S(1)}, u32[]{:S(2)}, u32[]{:S(2)}) collective-permute-start(bf16[2,16,16,128]{3,2,1,0:T(8,128)(2,1)S(1)} %get-tuple-element.26), channel_id=1, source_target_pairs={{0,26},{1,27},{2,8},{3,9},{4,30},{5,31},{6,12},{7,13},{8,2},{9,3},... | collective-permute-start | bytes 393224 | tf_op jit(solution)/shard_map/ppermute | solution.py:287
  71.6 16.8 %collective-permute-start.12 = (bf16[8,16,16,128]{3,2,1,0:T(8,128)(2,1)S(1)}, bf16[8,16,16,128]{3,2,1,0:T(8,128)(2,1)S(1)}, u32[]{:S(2)}, u32[]{:S(2)}) collective-permute-start(bf16[8,16,16,128]{3,2,1,0:T(8,128)(2,1)S(1)} %constant_dynamic-update-slice_fusion.4.own_ref), channel_id=1, source_target_pairs={{0,2},{1,3},{2,0},{3,1},{4,6},{5,7},{6,4},{7,5},{8,10},{9,11},{10,... | collective-permute-start | bytes 1572872 | tf_op jit(solution)/shard_map/ppermute | solution.py:273
  75.3 24.2 %collective-permute-start.3 = (bf16[8,16,16,128]{3,2,1,0:T(8,128)(2,1)S(1)}, bf16[8,16,16,128]{3,2,1,0:T(8,128)(2,1)S(1)}, u32[]{:S(2)}, u32[]{:S(2)}) collective-permute-start(bf16[8,16,16,128]{3,2,1,0:T(8,128)(2,1)S(1)} %constant_dynamic-update-slice_fusion.own_ref), channel_id=1, source_target_pairs={{0,2},{1,3},{2,0},{3,1},{4,6},{5,7},{6,4},{7,5},{8,10},{9,11},{10,... | collective-permute-start | bytes 1572872 | tf_op jit(solution)/shard_map/ppermute | solution.py:273
  92.1 18.7 %collective-permute-start.13 = (bf16[8,16,16,128]{3,2,1,0:T(8,128)(2,1)S(1)}, bf16[8,16,16,128]{3,2,1,0:T(8,128)(2,1)S(1)}, u32[]{:S(2)}, u32[]{:S(2)}) collective-permute-start(bf16[8,16,16,128]{3,2,1,0:T(8,128)(2,1)S(1)} %get-tuple-element.34), channel_id=1, source_target_pairs={{0,2},{1,3},{2,0},{3,1},{4,6},{5,7},{6,4},{7,5},{8,10},{9,11},{10,... | collective-permute-start | bytes 1572872 | tf_op jit(solution)/shard_map/ppermute | solution.py:273
  103.3 39.0 %collective-permute-start.6 = (bf16[8,16,16,128]{3,2,1,0:T(8,128)(2,1)S(1)}, bf16[8,16,16,128]{3,2,1,0:T(8,128)(2,1)S(1)}, u32[]{:S(2)}, u32[]{:S(2)}) collective-permute-start(bf16[8,16,16,128]{3,2,1,0:T(8,128)(2,1)S(1)} %get-tuple-element.28), channel_id=1, source_target_pairs={{0,2},{1,3},{2,0},{3,1},{4,6},{5,7},{6,4},{7,5},{8,10},{9,11},{10,... | collective-permute-start | bytes 1572872 | tf_op jit(solution)/shard_map/ppermute | solution.py:273
  110.9 33.4 %collective-permute-start.14 = (bf16[2,16,16,128]{3,2,1,0:T(8,128)(2,1)S(1)}, bf16[2,16,16,128]{3,2,1,0:T(8,128)(2,1)S(1)}, u32[]{:S(2)}, u32[]{:S(2)}) collective-permute-start(bf16[2,16,16,128]{3,2,1,0:T(8,128)(2,1)S(1)} %get-tuple-element.44), channel_id=1, source_target_pairs={{8,0},{9,1},{26,2},{27,3},{12,4},{13,5},{30,6},{31,7},{16,8},{17,9... | collective-permute-start | bytes 393224 | tf_op jit(solution)/shard_map/ppermute | solution.py:287
  112.9 39.3 %collective-permute-start.15 = (bf16[2,16,16,128]{3,2,1,0:T(8,128)(2,1)S(1)}, bf16[2,16,16,128]{3,2,1,0:T(8,128)(2,1)S(1)}, u32[]{:S(2)}, u32[]{:S(2)}) collective-permute-start(bf16[2,16,16,128]{3,2,1,0:T(8,128)(2,1)S(1)} %get-tuple-element.43), channel_id=1, source_target_pairs={{12,0},{13,1},{22,2},{23,3},{16,4},{17,5},{26,6},{27,7},{20,8},{21... | collective-permute-start | bytes 393224 | tf_op jit(solution)/shard_map/ppermute | solution.py:287
  121.5 32.6 %collective-permute-start.16 = (bf16[2,16,16,128]{3,2,1,0:T(8,128)(2,1)S(1)}, bf16[2,16,16,128]{3,2,1,0:T(8,128)(2,1)S(1)}, u32[]{:S(2)}, u32[]{:S(2)}) collective-permute-start(bf16[2,16,16,128]{3,2,1,0:T(8,128)(2,1)S(1)} %get-tuple-element.42), channel_id=1, source_target_pairs={{18,0},{19,1},{16,2},{17,3},{22,4},{23,5},{20,6},{21,7},{26,8},{27... | collective-permute-start | bytes 393224 | tf_op jit(solution)/shard_map/ppermute | solution.py:287
  127.5 27.0 %collective-permute-start.17 = (bf16[2,16,16,128]{3,2,1,0:T(8,128)(2,1)S(1)}, bf16[2,16,16,128]{3,2,1,0:T(8,128)(2,1)S(1)}, u32[]{:S(2)}, u32[]{:S(2)}) collective-permute-start(bf16[2,16,16,128]{3,2,1,0:T(8,128)(2,1)S(1)} %get-tuple-element.41), channel_id=1, source_target_pairs={{22,0},{23,1},{12,2},{13,3},{26,4},{27,5},{16,6},{17,7},{30,8},{31... | collective-permute-start | bytes 393224 | tf_op jit(solution)/shard_map/ppermute | solution.py:287
  142.4 13.0 %collective-permute-start.18 = (bf16[2,16,16,128]{3,2,1,0:T(8,128)(2,1)S(1)}, bf16[2,16,16,128]{3,2,1,0:T(8,128)(2,1)S(1)}, u32[]{:S(2)}, u32[]{:S(2)}) collective-permute-start(bf16[2,16,16,128]{3,2,1,0:T(8,128)(2,1)S(1)} %get-tuple-element.38), channel_id=1, source_target_pairs={{26,0},{27,1},{8,2},{9,3},{30,4},{31,5},{12,6},{13,7},{2,8},{3,9},... | collective-permute-start | bytes 393224 | tf_op jit(solution)/shard_map/ppermute | solution.py:287
  144.4 15.1 %collective-permute-start.19 = (bf16[2,16,16,128]{3,2,1,0:T(8,128)(2,1)S(1)}, bf16[2,16,16,128]{3,2,1,0:T(8,128)(2,1)S(1)}, u32[]{:S(2)}, u32[]{:S(2)}) collective-permute-start(bf16[2,16,16,128]{3,2,1,0:T(8,128)(2,1)S(1)} %get-tuple-element.37), channel_id=1, source_target_pairs={{30,0},{31,1},{4,2},{5,3},{2,4},{3,5},{8,6},{9,7},{6,8},{7,9},{12,... | collective-permute-start | bytes 393224 | tf_op jit(solution)/shard_map/ppermute | solution.py:287
  152.2 9.7 %collective-permute-start.7 = (bf16[2,16,16,128]{3,2,1,0:T(8,128)(2,1)S(1)}, bf16[2,16,16,128]{3,2,1,0:T(8,128)(2,1)S(1)}, u32[]{:S(2)}, u32[]{:S(2)}) collective-permute-start(bf16[2,16,16,128]{3,2,1,0:T(8,128)(2,1)S(1)} %get-tuple-element.39), channel_id=1, source_target_pairs={{4,0},{5,1},{30,2},{31,3},{8,4},{9,5},{2,6},{3,7},{12,8},{13,9},{6... | collective-permute-start | bytes 393224 | tf_op jit(solution)/shard_map/ppermute | solution.py:287
  162.7 9.8 %collective-permute-start.20 = (bf16[48,3584]{1,0:T(8,128)(2,1)S(1)}, bf16[48,3584]{1,0:T(8,128)(2,1)S(1)}, u32[]{:S(2)}, u32[]{:S(2)}) collective-permute-start(bf16[48,3584]{1,0:T(8,128)(2,1)S(1)} %get-tuple-element.36), channel_id=1, source_target_pairs={{0,32},{32,64},{64,96},{96,128},{128,160},{160,192},{192,224},{224... | collective-permute-start | bytes 1032200 | tf_op jit(solution)/shard_map/ppermute | solution.py:269
  165.7 11.3 %collective-permute-start.21 = (bf16[48,3584]{1,0:T(8,128)(2,1)S(1)}, bf16[48,3584]{1,0:T(8,128)(2,1)S(1)}, u32[]{:S(2)}, u32[]{:S(2)}) collective-permute-start(bf16[48,3584]{1,0:T(8,128)(2,1)S(1)} %get-tuple-element.35), channel_id=1, source_target_pairs={{32,0},{64,32},{96,64},{128,96},{160,128},{192,160},{224,192},{256... | collective-permute-start | bytes 1032200 | tf_op jit(solution)/shard_map/ppermute | solution.py:269

commit v5 on v4

--- a/solution.py
+++ b/solution.py
@@ -60,36 +60,46 @@
     return jnp.dot(gather, tail, preferred_element_type=jnp.float32)
 
 
-def prepare_kernel(x_ref, gain_ref, router_ref, ids_ref, turns_ref, gate_ref, row_ref, *packet_refs):
+def column(along):
+    count = along.shape[1]
+    diagonal = iota((count, count), 0) == iota((count, count), 1)
+    return jnp.sum(jnp.where(diagonal, along, 0.0), axis=1, keepdims=True)
+
+
+def prepare_kernel(x_ref, gain_ref, router_ref, ids_ref, gate_ref, row_ref, *packet_refs):
     for direction in range(x_ref.shape[0]):
         prepare_direction(
-            x_ref.at[direction],
+            x_ref.at[direction, 0],
             gain_ref,
             router_ref,
             ids_ref.at[0, direction],
-            turns_ref.at[0, direction],
             gate_ref.at[direction],
             row_ref.at[direction],
             [ref.at[direction] for ref in packet_refs],
         )
 
 
-def prepare_direction(
-    x_ref, gain_ref, router_ref, ids_ref, turns_ref, gate_ref, row_ref, packet_refs
-):
+def prepare_direction(x_ref, gain_ref, router_ref, ids_ref, gate_ref, row_ref, packet_refs):
     experts = len(packet_refs)
     pairs = packet_refs[0].shape[0] - 2
-    tokens = x_ref.shape[1]
-    x = x_ref[0].astype(jnp.float32)
+    tokens = x_ref.shape[0]
+    x = x_ref[...].astype(jnp.float32)
     mean_square = jnp.mean(x * x, axis=-1, keepdims=True)
     normed = (x * lax.rsqrt(mean_square + epsilon) * gain_ref[...].astype(jnp.float32)).astype(
         jnp.bfloat16
     )
-    logits = jnp.dot(normed, router_ref[0], preferred_element_type=jnp.float32)
-    chosen = (iota((tokens, experts), 1) == ids_ref[...]).astype(jnp.float32)
+    logits = lax.dot_general(
+        normed, router_ref[0], (((1,), (1,)), ((), ())), preferred_element_type=jnp.float32
+    )
+    expert = column(ids_ref[...].astype(jnp.float32))
+    by_expert = iota((tokens, experts), 1).astype(jnp.float32)
+    chosen = (by_expert == expert).astype(jnp.float32)
     gate = route_scale * jax.nn.sigmoid(jnp.sum(logits * chosen, axis=-1, keepdims=True))
-    turn = turns_ref[...]
-    one_hot = (iota((tokens, experts), 1) == turn).astype(jnp.float32)
+    device = lax.axis_index("expert")
+    home = (device // SPLIT).astype(jnp.float32)
+    turn = jnp.where(device // 2 % 2 == 0, expert - home, home - expert)
+    turn = jnp.where(turn < 0.0, turn + experts, turn)
+    one_hot = (by_expert == turn).astype(jnp.float32)
     earlier = (iota((tokens, tokens), 1) < iota((tokens, tokens), 0)).astype(jnp.float32)
     before = jnp.dot(
         earlier.astype(jnp.bfloat16),
@@ -97,7 +107,6 @@
         preferred_element_type=jnp.float32,
     )
     slot = jnp.sum(before * one_hot, axis=-1, keepdims=True)
-    turn = turn.astype(jnp.float32)
     row = jnp.where(slot < MAIN, turn * MAIN + slot, experts * MAIN + turn)
     gate_ref[...] = jnp.broadcast_to(gate, gate_ref.shape)
     row_ref[...] = jnp.broadcast_to(row, row_ref.shape)
@@ -214,20 +223,21 @@
     return pl.BlockSpec(array.shape, lambda _: (0,) * array.ndim)
 
 
-def prepare(carried, gain, router, ids, turns, experts):
+def prepare(carried, gain, router, ids, experts):
     directions, _, tokens, width = carried.shape
     packet = jax.ShapeDtypeStruct((directions, width // 256 + 2, 16, LANES), jnp.bfloat16)
     notes = jax.ShapeDtypeStruct((directions, tokens, LANES), jnp.float32)
     outs = (notes, notes) + (packet,) * experts
+    operands = (carried, gain, jnp.swapaxes(router, 1, 2), jnp.swapaxes(ids, 2, 3))
     gate, row, *packets = pl.pallas_call(
         prepare_kernel,
         grid=(1,),
         out_shape=outs,
-        in_specs=[whole(a) for a in (carried, gain, router, ids, turns)],
+        in_specs=[whole(a) for a in operands],
         out_specs=tuple(whole(a) for a in outs),
         compiler_params=params(),
         name="prepare",
-    )(carried, gain, router, ids, turns)
+    )(*operands)
     return gate, row, packets
 
 
@@ -291,17 +301,18 @@
     return (left.astype(jnp.float32) + right.astype(jnp.float32)).astype(jnp.bfloat16)
 
 
+def after(value, *earlier):
+    return lax.optimization_barrier((value, *earlier))[0]
+
+
 def per_device(carried, norm_gain, router, w_up, w_down, expert_ids):
     experts = lax.axis_size("expert") // SPLIT
-    device = lax.axis_index("expert")
-    pair = device // SPLIT
-    lower = device // 2 % 2 == 0
-    turns = jnp.where(lower, expert_ids - pair, pair - expert_ids) % experts
-    gate, row, packets = prepare(carried, norm_gain, router, expert_ids, turns, experts)
+    ups = (w_up, swapped(w_up, 1))
+    downs = (w_down, swapped(w_down, 1))
+    gate, row, packets = prepare(carried, norm_gain, router, expert_ids, experts)
+    packets = [after(packet, ups[1], downs[1]) for packet in packets]
     arrived = [delivered(packet, turn, False) for turn, packet in enumerate(packets)]
     returned = [None] * experts
-    ups = (w_up, swapped(w_up, 1))
-    downs = (w_down, swapped(w_down, 1))
     for group in GROUPS:
         own = jnp.concatenate([arrived[turn] for turn in group], axis=0)
         for_own, for_chip = run_expert(own, swapped(own, 2), ups, downs)

time: 180 us -> 174 us (0.967)
  waiting for transfers between devices: 55.3 us -> 50 us
    ppermute x6, starting transfers between devices: 12.4 us -> 21.9 us  [swapped(): lax.ppermute(block, 'expert', [(i, i ^ bit) for i in range(lax.axis_size(...]
    ppermute x14, starting transfers between devices: 88.4 us -> 79.3 us  [delivered(): return lax.ppermute(packet, 'expert', route)]
    ppermute x6, waiting for transfers between devices: 29.3 us -> 23.3 us  [swapped(): lax.ppermute(block, 'expert', [(i, i ^ bit) for i in range(lax.axis_size(...]
  transfers between devices with their start and end apart: 22 -> 22, of which waited for: 13 -> 13; matrix products, arithmetic and copies ran while one was open for 2% -> 0% of each run, Pallas kernels for 5% -> 5%
where the time goes in v5:
time: 174 us; the launch traced here: 172 us
  starting transfers between devices  107 us (61%)
  waiting for transfers between devices  50 us (29%)
  Pallas kernels  9.74 us (6%)
  local copies, waits for them, and re-layouts  3.45 us (2%)
    ppermute x14, starting transfers between devices, delivered(): return lax.ppermute(packet, 'expert', route)  79.3 us
    ppermute x6, waiting for transfers between devices, swapped(): lax.ppermute(block, 'expert', [(i, i ^ bit) for i in range(lax.axis_size(...  23.3 us
    ppermute x6, starting transfers between devices, swapped(): lax.ppermute(block, 'expert', [(i, i ^ bit) for i in range(lax.axis_size(...  21.9 us
    ppermute x14, waiting for transfers between devices, delivered(): return lax.ppermute(packet, 'expert', route)  17.6 us
    ppermute x2, waiting for transfers between devices, passed_along(): return lax.ppermute(block, axis, route)  9.14 us
    pallas_call x2, Pallas kernels, run_expert(): pl.pallas_call(expert_kernel, grid=(1,), out_shape=(packet,) * 2, in_spec...  7.43 us
    ppermute x2, starting transfers between devices, passed_along(): return lax.ppermute(block, axis, route)  5.84 us
  transfers between devices with their start and end apart: 22, of which 13 were waited for; matrix products, arithmetic and copies ran while one was open for 0% of the time, Pallas kernels for 5%

profile of v5, /device:TPU:24, one launch (start us, length us, event | category | flops | bytes accessed | tf_op | source)
XLA Modules:
  0.0 171.9 jit_solution(3730657414843982458)
XLA Ops:
  0.0 0.0 copy-start
  0.0 2.0 %collective-permute-start = (bf16[1,3584,256]{2,1,0:T(8,128)(2,1)}, bf16[1,3584,256]{2,1,0:T(8,128)(2,1)S(1)}, u32[]{:S(2)}, u32[]{:S(2)}) collective-permute-start(bf16[1,3584,256]{2,1,0:T(8,128)(2,1)} %rest_0_.3), channel_id=1, source_target_pairs={{0,1},{1,0},{2,3},{3,2},{4,5},{5,4},{6,7},{7,6},{8,9},{9,8},{10,11... | collective-permute-start | bytes 5505032 | tf_op jit(solution)/shard_map/ppermute | solution.py:283
  2.0 2.4 %collective-permute-start.1 = (bf16[1,256,3584]{2,1,0:T(8,128)(2,1)}, bf16[1,256,3584]{2,1,0:T(8,128)(2,1)S(1)}, u32[]{:S(2)}, u32[]{:S(2)}) collective-permute-start(bf16[1,256,3584]{2,1,0:T(8,128)(2,1)} %rest_2_.3), channel_id=1, source_target_pairs={{0,1},{1,0},{2,3},{3,2},{4,5},{5,4},{6,7},{7,6},{8,9},{9,8},{10,11... | collective-permute-start | bytes 5505032 | tf_op jit(solution)/shard_map/ppermute | solution.py:283
  4.5 0.0 copy-start.1
  4.5 1.1 copy-done.1
  5.6 0.8 copy-done.3
  6.4 0.0 copy-start.4
  6.4 0.7 copy-done.4
  7.1 0.7 copy-done.5
  7.8 1.5 prepare.1
  9.3 0.0 collective-permute-done.rest_1_
  9.3 0.0 collective-permute-done.1.rest_3_
  9.3 0.0 copy-start.6
  9.3 9.1 %collective-permute-start.8 = (bf16[2,16,16,128]{3,2,1,0:T(8,128)(2,1)S(1)}, bf16[2,16,16,128]{3,2,1,0:T(8,128)(2,1)S(1)}, u32[]{:S(2)}, u32[]{:S(2)}) collective-permute-start(bf16[2,16,16,128]{3,2,1,0:T(8,128)(2,1)S(1)} %get-tuple-element.42), channel_id=1, source_target_pairs={{0,8},{1,9},{2,26},{3,27},{4,12},{5,13},{6,30},{7,31},{8,16},{9,17... | collective-permute-start | bytes 393224 | tf_op jit(solution)/shard_map/ppermute | solution.py:297
  18.4 8.6 %collective-permute-start.9 = (bf16[2,16,16,128]{3,2,1,0:T(8,128)(2,1)S(1)}, bf16[2,16,16,128]{3,2,1,0:T(8,128)(2,1)S(1)}, u32[]{:S(2)}, u32[]{:S(2)}) collective-permute-start(bf16[2,16,16,128]{3,2,1,0:T(8,128)(2,1)S(1)} %get-tuple-element.44), channel_id=1, source_target_pairs={{0,22},{1,23},{2,12},{3,13},{4,26},{5,27},{6,16},{7,17},{8,30},{9,... | collective-permute-start | bytes 393224 | tf_op jit(solution)/shard_map/ppermute | solution.py:297
  27.0 6.1 %collective-permute-start.10 = (bf16[2,16,16,128]{3,2,1,0:T(8,128)(2,1)S(1)}, bf16[2,16,16,128]{3,2,1,0:T(8,128)(2,1)S(1)}, u32[]{:S(2)}, u32[]{:S(2)}) collective-permute-start(bf16[2,16,16,128]{3,2,1,0:T(8,128)(2,1)S(1)} %get-tuple-element.46), channel_id=1, source_target_pairs={{0,12},{1,13},{2,22},{3,23},{4,16},{5,17},{6,26},{7,27},{8,20},{9,... | collective-permute-start | bytes 393224 | tf_op jit(solution)/shard_map/ppermute | solution.py:297
  33.1 8.0 %collective-permute-start.11 = (bf16[2,16,16,128]{3,2,1,0:T(8,128)(2,1)S(1)}, bf16[2,16,16,128]{3,2,1,0:T(8,128)(2,1)S(1)}, u32[]{:S(2)}, u32[]{:S(2)}) collective-permute-start(bf16[2,16,16,128]{3,2,1,0:T(8,128)(2,1)S(1)} %get-tuple-element.48), channel_id=1, source_target_pairs={{0,18},{1,19},{2,16},{3,17},{4,22},{5,23},{6,20},{7,21},{8,26},{9,... | collective-permute-start | bytes 393224 | tf_op jit(solution)/shard_map/ppermute | solution.py:297
  41.2 1.9 %collective-permute-start.2 = (bf16[2,16,16,128]{3,2,1,0:T(8,128)(2,1)S(1)}, bf16[2,16,16,128]{3,2,1,0:T(8,128)(2,1)S(1)}, u32[]{:S(2)}, u32[]{:S(2)}) collective-permute-start(bf16[2,16,16,128]{3,2,1,0:T(8,128)(2,1)S(1)} %get-tuple-element.34), channel_id=1, source_target_pairs={{0,30},{1,31},{2,4},{3,5},{4,2},{5,3},{6,8},{7,9},{8,6},{9,7},{10,... | collective-permute-start | bytes 393224 | tf_op jit(solution)/shard_map/ppermute | solution.py:297
  43.1 0.0 collective-permute-done.8
  43.1 2.2 %collective-permute-start.3 = (bf16[2,16,16,128]{3,2,1,0:T(8,128)(2,1)S(1)}, bf16[2,16,16,128]{3,2,1,0:T(8,128)(2,1)S(1)}, u32[]{:S(2)}, u32[]{:S(2)}) collective-permute-start(bf16[2,16,16,128]{3,2,1,0:T(8,128)(2,1)S(1)} %get-tuple-element.36), channel_id=1, source_target_pairs={{0,4},{1,5},{2,30},{3,31},{4,8},{5,9},{6,2},{7,3},{8,12},{9,13},{1... | collective-permute-start | bytes 393224 | tf_op jit(solution)/shard_map/ppermute | solution.py:297
  45.3 2.5 %collective-permute-done.9 = bf16[2,16,16,128]{3,2,1,0:T(8,128)(2,1)S(1)} collective-permute-done((bf16[2,16,16,128]{3,2,1,0:T(8,128)(2,1)S(1)}, bf16[2,16,16,128]{3,2,1,0:T(8,128)(2,1)S(1)}, u32[]{:S(2)}, u32[]{:S(2)}) %collective-permute-start.9) | collective-permute-done | bytes 131104 | tf_op jit(solution)/shard_map/ppermute | solution.py:297
  47.9 5.9 %collective-permute-start.4 = (bf16[2,16,16,128]{3,2,1,0:T(8,128)(2,1)S(1)}, bf16[2,16,16,128]{3,2,1,0:T(8,128)(2,1)S(1)}, u32[]{:S(2)}, u32[]{:S(2)}) collective-permute-start(bf16[2,16,16,128]{3,2,1,0:T(8,128)(2,1)S(1)} %get-tuple-element.38), channel_id=1, source_target_pairs={{0,26},{1,27},{2,8},{3,9},{4,30},{5,31},{6,12},{7,13},{8,2},{9,3},... | collective-permute-start | bytes 393224 | tf_op jit(solution)/shard_map/ppermute | solution.py:297
  53.8 0.0 collective-permute-done.10
  53.9 4.7 %collective-permute-done.11 = bf16[2,16,16,128]{3,2,1,0:T(8,128)(2,1)S(1)} collective-permute-done((bf16[2,16,16,128]{3,2,1,0:T(8,128)(2,1)S(1)}, bf16[2,16,16,128]{3,2,1,0:T(8,128)(2,1)S(1)}, u32[]{:S(2)}, u32[]{:S(2)}) %collective-permute-start.11) | collective-permute-done | bytes 131104 | tf_op jit(solution)/shard_map/ppermute | solution.py:297
  58.6 3.9 %collective-permute-start.12 = (bf16[8,16,16,128]{3,2,1,0:T(8,128)(2,1)S(1)}, bf16[8,16,16,128]{3,2,1,0:T(8,128)(2,1)S(1)}, u32[]{:S(2)}, u32[]{:S(2)}) collective-permute-start(bf16[8,16,16,128]{3,2,1,0:T(8,128)(2,1)S(1)} %constant_dynamic-update-slice_fusion.4.own_ref), channel_id=1, source_target_pairs={{0,2},{1,3},{2,0},{3,1},{4,6},{5,7},{6,4},{7,5},{8,10},{9,11},{10,... | collective-permute-start | bytes 1572872 | tf_op jit(solution)/shard_map/ppermute | solution.py:283
  62.5 1.4 collective-permute-done.2
  63.9 0.0 collective-permute-done.3
  63.9 4.2 %collective-permute-done.4 = bf16[2,16,16,128]{3,2,1,0:T(8,128)(2,1)S(1)} collective-permute-done((bf16[2,16,16,128]{3,2,1,0:T(8,128)(2,1)S(1)}, bf16[2,16,16,128]{3,2,1,0:T(8,128)(2,1)S(1)}, u32[]{:S(2)}, u32[]{:S(2)}) %collective-permute-start.4) | collective-permute-done | bytes 131104 | tf_op jit(solution)/shard_map/ppermute | solution.py:297
  68.1 5.7 %collective-permute-start.5 = (bf16[8,16,16,128]{3,2,1,0:T(8,128)(2,1)S(1)}, bf16[8,16,16,128]{3,2,1,0:T(8,128)(2,1)S(1)}, u32[]{:S(2)}, u32[]{:S(2)}) collective-permute-start(bf16[8,16,16,128]{3,2,1,0:T(8,128)(2,1)S(1)} %constant_dynamic-update-slice_fusion.own_ref), channel_id=1, source_target_pairs={{0,2},{1,3},{2,0},{3,1},{4,6},{5,7},{6,4},{7,5},{8,10},{9,11},{10,... | collective-permute-start | bytes 1572872 | tf_op jit(solution)/shard_map/ppermute | solution.py:283
  73.9 3.6 %collective-permute-done.12.chip_ref = bf16[8,16,16,128]{3,2,1,0:T(8,128)(2,1)S(1)} collective-permute-done((bf16[8,16,16,128]{3,2,1,0:T(8,128)(2,1)S(1)}, bf16[8,16,16,128]{3,2,1,0:T(8,128)(2,1)S(1)}, u32[]{:S(2)}, u32[]{:S(2)}) %collective-permute-start.12) | collective-permute-done | bytes 524320 | tf_op jit(solution)/shard_map/ppermute | solution.py:283
  77.5 0.0 copy-done.6
  77.5 0.0 copy-done
  77.5 3.7 %expert.3 = (bf16[8,16,16,128]{3,2,1,0:T(8,128)(2,1)S(1)}, bf16[8,16,16,128]{3,2,1,0:T(8,128)(2,1)S(1)}) custom-call(bf16[8,16,16,128]{3,2,1,0:T(8,128)(2,1)S(1)} %constant_dynamic-update-slice_fusion.4.own_ref, bf16[8,16,16,128]{3,2,1,0:T(8,128)(2,1)S(1)} %collective-permute-done.12.chip_ref, bf16[1,3584,256]{2,1,0:T(8,128)(2,1)S(1)} %copy-done, ...), custom_call_target="tpu_custom_call" | custom-call | tf_op jit(solution)/shard_map/expert/pallas_call | solution.py:249
  81.2 3.9 %collective-permute-start.13 = (bf16[8,16,16,128]{3,2,1,0:T(8,128)(2,1)S(1)}, bf16[8,16,16,128]{3,2,1,0:T(8,128)(2,1)S(1)}, u32[]{:S(2)}, u32[]{:S(2)}) collective-permute-start(bf16[8,16,16,128]{3,2,1,0:T(8,128)(2,1)S(1)} %get-tuple-element.50), channel_id=1, source_target_pairs={{0,2},{1,3},{2,0},{3,1},{4,6},{5,7},{6,4},{7,5},{8,10},{9,11},{10,... | collective-permute-start | bytes 1572872 | tf_op jit(solution)/shard_map/ppermute | solution.py:283
  85.1 3.6 %collective-permute-done.5.chip_ref = bf16[8,16,16,128]{3,2,1,0:T(8,128)(2,1)S(1)} collective-permute-done((bf16[8,16,16,128]{3,2,1,0:T(8,128)(2,1)S(1)}, bf16[8,16,16,128]{3,2,1,0:T(8,128)(2,1)S(1)}, u32[]{:S(2)}, u32[]{:S(2)}) %collective-permute-start.5) | collective-permute-done | bytes 524320 | tf_op jit(solution)/shard_map/ppermute | solution.py:283
  88.8 3.7 %expert.2 = (bf16[8,16,16,128]{3,2,1,0:T(8,128)(2,1)S(1)}, bf16[8,16,16,128]{3,2,1,0:T(8,128)(2,1)S(1)}) custom-call(bf16[8,16,16,128]{3,2,1,0:T(8,128)(2,1)S(1)} %constant_dynamic-update-slice_fusion.own_ref, bf16[8,16,16,128]{3,2,1,0:T(8,128)(2,1)S(1)} %collective-permute-done.5.chip_ref, bf16[1,3584,256]{2,1,0:T(8,128)(2,1)S(1)} %copy-done, ...), custom_call_target="tpu_custom_call" | custom-call | tf_op jit(solution)/shard_map/expert/pallas_call | solution.py:249
  92.5 0.0 copy-start.2
  92.5 4.0 %collective-permute-start.6 = (bf16[8,16,16,128]{3,2,1,0:T(8,128)(2,1)S(1)}, bf16[8,16,16,128]{3,2,1,0:T(8,128)(2,1)S(1)}, u32[]{:S(2)}, u32[]{:S(2)}) collective-permute-start(bf16[8,16,16,128]{3,2,1,0:T(8,128)(2,1)S(1)} %get-tuple-element.40), channel_id=1, source_target_pairs={{0,2},{1,3},{2,0},{3,1},{4,6},{5,7},{6,4},{7,5},{8,10},{9,11},{10,... | collective-permute-start | bytes 1572872 | tf_op jit(solution)/shard_map/ppermute | solution.py:283
  96.5 3.5 %collective-permute-done.13 = bf16[8,16,16,128]{3,2,1,0:T(8,128)(2,1)S(1)} collective-permute-done((bf16[8,16,16,128]{3,2,1,0:T(8,128)(2,1)S(1)}, bf16[8,16,16,128]{3,2,1,0:T(8,128)(2,1)S(1)}, u32[]{:S(2)}, u32[]{:S(2)}) %collective-permute-start.13) | collective-permute-done | bytes 524320 | tf_op jit(solution)/shard_map/ppermute | solution.py:283
  100.0 0.1 add_convert_fusion.2
  100.1 8.1 %collective-permute-start.14 = (bf16[2,16,16,128]{3,2,1,0:T(8,128)(2,1)S(1)}, bf16[2,16,16,128]{3,2,1,0:T(8,128)(2,1)S(1)}, u32[]{:S(2)}, u32[]{:S(2)}) collective-permute-start(bf16[2,16,16,128]{3,2,1,0:T(8,128)(2,1)S(1)} %get-tuple-element.60), channel_id=1, source_target_pairs={{8,0},{9,1},{26,2},{27,3},{12,4},{13,5},{30,6},{31,7},{16,8},{17,9... | collective-permute-start | bytes 393224 | tf_op jit(solution)/shard_map/ppermute | solution.py:297
  108.2 5.8 %collective-permute-start.15 = (bf16[2,16,16,128]{3,2,1,0:T(8,128)(2,1)S(1)}, bf16[2,16,16,128]{3,2,1,0:T(8,128)(2,1)S(1)}, u32[]{:S(2)}, u32[]{:S(2)}) collective-permute-start(bf16[2,16,16,128]{3,2,1,0:T(8,128)(2,1)S(1)} %get-tuple-element.59), channel_id=1, source_target_pairs={{12,0},{13,1},{22,2},{23,3},{16,4},{17,5},{26,6},{27,7},{20,8},{21... | collective-permute-start | bytes 393224 | tf_op jit(solution)/shard_map/ppermute | solution.py:297
  114.0 5.3 %collective-permute-start.16 = (bf16[2,16,16,128]{3,2,1,0:T(8,128)(2,1)S(1)}, bf16[2,16,16,128]{3,2,1,0:T(8,128)(2,1)S(1)}, u32[]{:S(2)}, u32[]{:S(2)}) collective-permute-start(bf16[2,16,16,128]{3,2,1,0:T(8,128)(2,1)S(1)} %get-tuple-element.58), channel_id=1, source_target_pairs={{18,0},{19,1},{16,2},{17,3},{22,4},{23,5},{20,6},{21,7},{26,8},{27... | collective-permute-start | bytes 393224 | tf_op jit(solution)/shard_map/ppermute | solution.py:297
  119.3 5.1 %collective-permute-start.17 = (bf16[2,16,16,128]{3,2,1,0:T(8,128)(2,1)S(1)}, bf16[2,16,16,128]{3,2,1,0:T(8,128)(2,1)S(1)}, u32[]{:S(2)}, u32[]{:S(2)}) collective-permute-start(bf16[2,16,16,128]{3,2,1,0:T(8,128)(2,1)S(1)} %get-tuple-element.57), channel_id=1, source_target_pairs={{22,0},{23,1},{12,2},{13,3},{26,4},{27,5},{16,6},{17,7},{30,8},{31... | collective-permute-start | bytes 393224 | tf_op jit(solution)/shard_map/ppermute | solution.py:297
  124.4 12.5 %collective-permute-done.6 = bf16[8,16,16,128]{3,2,1,0:T(8,128)(2,1)S(1)} collective-permute-done((bf16[8,16,16,128]{3,2,1,0:T(8,128)(2,1)S(1)}, bf16[8,16,16,128]{3,2,1,0:T(8,128)(2,1)S(1)}, u32[]{:S(2)}, u32[]{:S(2)}) %collective-permute-start.6) | collective-permute-done | bytes 524320 | tf_op jit(solution)/shard_map/ppermute | solution.py:283
  136.9 0.1 add_convert_fusion
  137.1 2.1 %collective-permute-start.18 = (bf16[2,16,16,128]{3,2,1,0:T(8,128)(2,1)S(1)}, bf16[2,16,16,128]{3,2,1,0:T(8,128)(2,1)S(1)}, u32[]{:S(2)}, u32[]{:S(2)}) collective-permute-start(bf16[2,16,16,128]{3,2,1,0:T(8,128)(2,1)S(1)} %get-tuple-element.54), channel_id=1, source_target_pairs={{26,0},{27,1},{8,2},{9,3},{30,4},{31,5},{12,6},{13,7},{2,8},{3,9},... | collective-permute-start | bytes 393224 | tf_op jit(solution)/shard_map/ppermute | solution.py:297
  139.2 0.0 collective-permute-done.14.rest_2_
  139.2 5.7 %collective-permute-start.19 = (bf16[2,16,16,128]{3,2,1,0:T(8,128)(2,1)S(1)}, bf16[2,16,16,128]{3,2,1,0:T(8,128)(2,1)S(1)}, u32[]{:S(2)}, u32[]{:S(2)}) collective-permute-start(bf16[2,16,16,128]{3,2,1,0:T(8,128)(2,1)S(1)} %get-tuple-element.53), channel_id=1, source_target_pairs={{30,0},{31,1},{4,2},{5,3},{2,4},{3,5},{8,6},{9,7},{6,8},{7,9},{12,... | collective-permute-start | bytes 393224 | tf_op jit(solution)/shard_map/ppermute | solution.py:297
  144.9 0.0 collective-permute-done.15.rest_3_
  144.9 5.3 %collective-permute-start.7 = (bf16[2,16,16,128]{3,2,1,0:T(8,128)(2,1)S(1)}, bf16[2,16,16,128]{3,2,1,0:T(8,128)(2,1)S(1)}, u32[]{:S(2)}, u32[]{:S(2)}) collective-permute-start(bf16[2,16,16,128]{3,2,1,0:T(8,128)(2,1)S(1)} %get-tuple-element.55), channel_id=1, source_target_pairs={{4,0},{5,1},{30,2},{31,3},{8,4},{9,5},{2,6},{3,7},{12,8},{13,9},{6... | collective-permute-start | bytes 393224 | tf_op jit(solution)/shard_map/ppermute | solution.py:297
  150.2 0.0 collective-permute-done.16.rest_4_
  150.3 0.0 collective-permute-done.17.rest_5_
  150.3 0.1 collective-permute-done.18.rest_6_
  150.3 2.8 %collective-permute-done.19.rest_7_ = bf16[2,16,16,128]{3,2,1,0:T(8,128)(2,1)S(1)} collective-permute-done((bf16[2,16,16,128]{3,2,1,0:T(8,128)(2,1)S(1)}, bf16[2,16,16,128]{3,2,1,0:T(8,128)(2,1)S(1)}, u32[]{:S(2)}, u32[]{:S(2)}) %collective-permute-start.19) | collective-permute-done | bytes 131104 | tf_op jit(solution)/shard_map/ppermute | solution.py:297
  153.2 1.8 %collective-permute-done.7.rest_1_ = bf16[2,16,16,128]{3,2,1,0:T(8,128)(2,1)S(1)} collective-permute-done((bf16[2,16,16,128]{3,2,1,0:T(8,128)(2,1)S(1)}, bf16[2,16,16,128]{3,2,1,0:T(8,128)(2,1)S(1)}, u32[]{:S(2)}, u32[]{:S(2)}) %collective-permute-start.7) | collective-permute-done | bytes 131104 | tf_op jit(solution)/shard_map/ppermute | solution.py:297
  155.0 0.0 copy-done.2
  155.0 0.8 finish.1
  155.8 3.1 %collective-permute-start.20 = (bf16[48,3584]{1,0:T(8,128)(2,1)S(1)}, bf16[48,3584]{1,0:T(8,128)(2,1)S(1)}, u32[]{:S(2)}, u32[]{:S(2)}) collective-permute-start(bf16[48,3584]{1,0:T(8,128)(2,1)S(1)} %get-tuple-element.52), channel_id=1, source_target_pairs={{0,32},{32,64},{64,96},{96,128},{128,160},{160,192},{192,224},{224... | collective-permute-start | bytes 1032200 | tf_op jit(solution)/shard_map/ppermute | solution.py:279
  159.0 2.7 %collective-permute-start.21 = (bf16[48,3584]{1,0:T(8,128)(2,1)S(1)}, bf16[48,3584]{1,0:T(8,128)(2,1)S(1)}, u32[]{:S(2)}, u32[]{:S(2)}) collective-permute-start(bf16[48,3584]{1,0:T(8,128)(2,1)S(1)} %get-tuple-element.51), channel_id=1, source_target_pairs={{32,0},{64,32},{96,64},{128,96},{160,128},{192,160},{224,192},{256... | collective-permute-start | bytes 1032200 | tf_op jit(solution)/shard_map/ppermute | solution.py:279
  161.7 4.2 %collective-permute-done.20 = bf16[48,3584]{1,0:T(8,128)(2,1)S(1)} collective-permute-done((bf16[48,3584]{1,0:T(8,128)(2,1)S(1)}, bf16[48,3584]{1,0:T(8,128)(2,1)S(1)}, u32[]{:S(2)}, u32[]{:S(2)}) %collective-permute-start.20) | collective-permute-done | bytes 344096 | tf_op jit(solution)/shard_map/ppermute | solution.py:279
  166.0 4.9 %collective-permute-done.21 = bf16[48,3584]{1,0:T(8,128)(2,1)S(1)} collective-permute-done((bf16[48,3584]{1,0:T(8,128)(2,1)S(1)}, bf16[48,3584]{1,0:T(8,128)(2,1)S(1)}, u32[]{:S(2)}, u32[]{:S(2)}) %collective-permute-start.21) | collective-permute-done | bytes 344096 | tf_op jit(solution)/shard_map/ppermute | solution.py:279
  170.9 0.1 select_bitcast_fusion
  170.9 0.9 maximum_bitcast_fusion
  (11 shorter events, 0.2 us)
Async XLA Ops:
  0.0 77.5 %copy-start = (bf16[1,3584,256]{2,1,0:T(8,128)(2,1)S(1)}, bf16[1,3584,256]{2,1,0:T(8,128)(2,1)}, u32[]{:S(2)}) copy-start(bf16[1,3584,256]{2,1,0:T(8,128)(2,1)} %rest_0_.3) | copy-start | bytes 5505028
  0.0 9.3 %collective-permute-start = (bf16[1,3584,256]{2,1,0:T(8,128)(2,1)}, bf16[1,3584,256]{2,1,0:T(8,128)(2,1)S(1)}, u32[]{:S(2)}, u32[]{:S(2)}) collective-permute-start(bf16[1,3584,256]{2,1,0:T(8,128)(2,1)} %rest_0_.3), channel_id=1, source_target_pairs={{0,1},{1,0},{2,3},{3,2},{4,5},{5,4},{6,7},{7,6},{8,9},{9,8},{10,11... | collective-permute-start | bytes 5505032 | tf_op jit(solution)/shard_map/ppermute | solution.py:283
  2.0 7.2 %collective-permute-start.1 = (bf16[1,256,3584]{2,1,0:T(8,128)(2,1)}, bf16[1,256,3584]{2,1,0:T(8,128)(2,1)S(1)}, u32[]{:S(2)}, u32[]{:S(2)}) collective-permute-start(bf16[1,256,3584]{2,1,0:T(8,128)(2,1)} %rest_2_.3), channel_id=1, source_target_pairs={{0,1},{1,0},{2,3},{3,2},{4,5},{5,4},{6,7},{7,6},{8,9},{9,8},{10,11... | collective-permute-start | bytes 5505032 | tf_op jit(solution)/shard_map/ppermute | solution.py:283
  4.5 1.1 copy-start.1
  5.6 0.8 copy-start.3
  6.4 0.7 copy-start.4
  7.1 0.7 copy-start.5
  9.3 68.2 %copy-start.6 = (bf16[1,256,3584]{2,1,0:T(8,128)(2,1)}, bf16[1,256,3584]{2,1,0:T(8,128)(2,1)S(1)}, u32[]{:S(2)}) copy-start(bf16[1,256,3584]{2,1,0:T(8,128)(2,1)S(1)} %collective-permute-done.1.rest_3_) | copy-start | bytes 5505028
  9.3 33.8 %collective-permute-start.8 = (bf16[2,16,16,128]{3,2,1,0:T(8,128)(2,1)S(1)}, bf16[2,16,16,128]{3,2,1,0:T(8,128)(2,1)S(1)}, u32[]{:S(2)}, u32[]{:S(2)}) collective-permute-start(bf16[2,16,16,128]{3,2,1,0:T(8,128)(2,1)S(1)} %get-tuple-element.42), channel_id=1, source_target_pairs={{0,8},{1,9},{2,26},{3,27},{4,12},{5,13},{6,30},{7,31},{8,16},{9,17... | collective-permute-start | bytes 393224 | tf_op jit(solution)/shard_map/ppermute | solution.py:297
  18.4 29.5 %collective-permute-start.9 = (bf16[2,16,16,128]{3,2,1,0:T(8,128)(2,1)S(1)}, bf16[2,16,16,128]{3,2,1,0:T(8,128)(2,1)S(1)}, u32[]{:S(2)}, u32[]{:S(2)}) collective-permute-start(bf16[2,16,16,128]{3,2,1,0:T(8,128)(2,1)S(1)} %get-tuple-element.44), channel_id=1, source_target_pairs={{0,22},{1,23},{2,12},{3,13},{4,26},{5,27},{6,16},{7,17},{8,30},{9,... | collective-permute-start | bytes 393224 | tf_op jit(solution)/shard_map/ppermute | solution.py:297
  27.0 26.8 %collective-permute-start.10 = (bf16[2,16,16,128]{3,2,1,0:T(8,128)(2,1)S(1)}, bf16[2,16,16,128]{3,2,1,0:T(8,128)(2,1)S(1)}, u32[]{:S(2)}, u32[]{:S(2)}) collective-permute-start(bf16[2,16,16,128]{3,2,1,0:T(8,128)(2,1)S(1)} %get-tuple-element.46), channel_id=1, source_target_pairs={{0,12},{1,13},{2,22},{3,23},{4,16},{5,17},{6,26},{7,27},{8,20},{9,... | collective-permute-start | bytes 393224 | tf_op jit(solution)/shard_map/ppermute | solution.py:297
  33.1 25.4 %collective-permute-start.11 = (bf16[2,16,16,128]{3,2,1,0:T(8,128)(2,1)S(1)}, bf16[2,16,16,128]{3,2,1,0:T(8,128)(2,1)S(1)}, u32[]{:S(2)}, u32[]{:S(2)}) collective-permute-start(bf16[2,16,16,128]{3,2,1,0:T(8,128)(2,1)S(1)} %get-tuple-element.48), channel_id=1, source_target_pairs={{0,18},{1,19},{2,16},{3,17},{4,22},{5,23},{6,20},{7,21},{8,26},{9,... | collective-permute-start | bytes 393224 | tf_op jit(solution)/shard_map/ppermute | solution.py:297
  41.2 22.6 %collective-permute-start.2 = (bf16[2,16,16,128]{3,2,1,0:T(8,128)(2,1)S(1)}, bf16[2,16,16,128]{3,2,1,0:T(8,128)(2,1)S(1)}, u32[]{:S(2)}, u32[]{:S(2)}) collective-permute-start(bf16[2,16,16,128]{3,2,1,0:T(8,128)(2,1)S(1)} %get-tuple-element.34), channel_id=1, source_target_pairs={{0,30},{1,31},{2,4},{3,5},{4,2},{5,3},{6,8},{7,9},{8,6},{9,7},{10,... | collective-permute-start | bytes 393224 | tf_op jit(solution)/shard_map/ppermute | solution.py:297
  43.1 20.7 %collective-permute-start.3 = (bf16[2,16,16,128]{3,2,1,0:T(8,128)(2,1)S(1)}, bf16[2,16,16,128]{3,2,1,0:T(8,128)(2,1)S(1)}, u32[]{:S(2)}, u32[]{:S(2)}) collective-permute-start(bf16[2,16,16,128]{3,2,1,0:T(8,128)(2,1)S(1)} %get-tuple-element.36), channel_id=1, source_target_pairs={{0,4},{1,5},{2,30},{3,31},{4,8},{5,9},{6,2},{7,3},{8,12},{9,13},{1... | collective-permute-start | bytes 393224 | tf_op jit(solution)/shard_map/ppermute | solution.py:297
  47.9 20.3 %collective-permute-start.4 = (bf16[2,16,16,128]{3,2,1,0:T(8,128)(2,1)S(1)}, bf16[2,16,16,128]{3,2,1,0:T(8,128)(2,1)S(1)}, u32[]{:S(2)}, u32[]{:S(2)}) collective-permute-start(bf16[2,16,16,128]{3,2,1,0:T(8,128)(2,1)S(1)} %get-tuple-element.38), channel_id=1, source_target_pairs={{0,26},{1,27},{2,8},{3,9},{4,30},{5,31},{6,12},{7,13},{8,2},{9,3},... | collective-permute-start | bytes 393224 | tf_op jit(solution)/shard_map/ppermute | solution.py:297
  58.6 18.9 %collective-permute-start.12 = (bf16[8,16,16,128]{3,2,1,0:T(8,128)(2,1)S(1)}, bf16[8,16,16,128]{3,2,1,0:T(8,128)(2,1)S(1)}, u32[]{:S(2)}, u32[]{:S(2)}) collective-permute-start(bf16[8,16,16,128]{3,2,1,0:T(8,128)(2,1)S(1)} %constant_dynamic-update-slice_fusion.4.own_ref), channel_id=1, source_target_pairs={{0,2},{1,3},{2,0},{3,1},{4,6},{5,7},{6,4},{7,5},{8,10},{9,11},{10,... | collective-permute-start | bytes 1572872 | tf_op jit(solution)/shard_map/ppermute | solution.py:283
  68.1 20.6 %collective-permute-start.5 = (bf16[8,16,16,128]{3,2,1,0:T(8,128)(2,1)S(1)}, bf16[8,16,16,128]{3,2,1,0:T(8,128)(2,1)S(1)}, u32[]{:S(2)}, u32[]{:S(2)}) collective-permute-start(bf16[8,16,16,128]{3,2,1,0:T(8,128)(2,1)S(1)} %constant_dynamic-update-slice_fusion.own_ref), channel_id=1, source_target_pairs={{0,2},{1,3},{2,0},{3,1},{4,6},{5,7},{6,4},{7,5},{8,10},{9,11},{10,... | collective-permute-start | bytes 1572872 | tf_op jit(solution)/shard_map/ppermute | solution.py:283
  81.2 18.7 %collective-permute-start.13 = (bf16[8,16,16,128]{3,2,1,0:T(8,128)(2,1)S(1)}, bf16[8,16,16,128]{3,2,1,0:T(8,128)(2,1)S(1)}, u32[]{:S(2)}, u32[]{:S(2)}) collective-permute-start(bf16[8,16,16,128]{3,2,1,0:T(8,128)(2,1)S(1)} %get-tuple-element.50), channel_id=1, source_target_pairs={{0,2},{1,3},{2,0},{3,1},{4,6},{5,7},{6,4},{7,5},{8,10},{9,11},{10,... | collective-permute-start | bytes 1572872 | tf_op jit(solution)/shard_map/ppermute | solution.py:283
  92.5 62.5 %copy-start.2 = (bf16[2,1,48,3584]{3,2,1,0:T(8,128)(2,1)S(1)}, bf16[2,1,48,3584]{3,2,1,0:T(8,128)(2,1)}, u32[]{:S(2)}) copy-start(bf16[2,1,48,3584]{3,2,1,0:T(8,128)(2,1)} %x_ref.3) | copy-start | bytes 2064388
  92.5 44.5 %collective-permute-start.6 = (bf16[8,16,16,128]{3,2,1,0:T(8,128)(2,1)S(1)}, bf16[8,16,16,128]{3,2,1,0:T(8,128)(2,1)S(1)}, u32[]{:S(2)}, u32[]{:S(2)}) collective-permute-start(bf16[8,16,16,128]{3,2,1,0:T(8,128)(2,1)S(1)} %get-tuple-element.40), channel_id=1, source_target_pairs={{0,2},{1,3},{2,0},{3,1},{4,6},{5,7},{6,4},{7,5},{8,10},{9,11},{10,... | collective-permute-start | bytes 1572872 | tf_op jit(solution)/shard_map/ppermute | solution.py:283
  100.1 39.0 %collective-permute-start.14 = (bf16[2,16,16,128]{3,2,1,0:T(8,128)(2,1)S(1)}, bf16[2,16,16,128]{3,2,1,0:T(8,128)(2,1)S(1)}, u32[]{:S(2)}, u32[]{:S(2)}) collective-permute-start(bf16[2,16,16,128]{3,2,1,0:T(8,128)(2,1)S(1)} %get-tuple-element.60), channel_id=1, source_target_pairs={{8,0},{9,1},{26,2},{27,3},{12,4},{13,5},{30,6},{31,7},{16,8},{17,9... | collective-permute-start | bytes 393224 | tf_op jit(solution)/shard_map/ppermute | solution.py:297
  108.2 36.7 %collective-permute-start.15 = (bf16[2,16,16,128]{3,2,1,0:T(8,128)(2,1)S(1)}, bf16[2,16,16,128]{3,2,1,0:T(8,128)(2,1)S(1)}, u32[]{:S(2)}, u32[]{:S(2)}) collective-permute-start(bf16[2,16,16,128]{3,2,1,0:T(8,128)(2,1)S(1)} %get-tuple-element.59), channel_id=1, source_target_pairs={{12,0},{13,1},{22,2},{23,3},{16,4},{17,5},{26,6},{27,7},{20,8},{21... | collective-permute-start | bytes 393224 | tf_op jit(solution)/shard_map/ppermute | solution.py:297
  114.0 36.2 %collective-permute-start.16 = (bf16[2,16,16,128]{3,2,1,0:T(8,128)(2,1)S(1)}, bf16[2,16,16,128]{3,2,1,0:T(8,128)(2,1)S(1)}, u32[]{:S(2)}, u32[]{:S(2)}) collective-permute-start(bf16[2,16,16,128]{3,2,1,0:T(8,128)(2,1)S(1)} %get-tuple-element.58), channel_id=1, source_target_pairs={{18,0},{19,1},{16,2},{17,3},{22,4},{23,5},{20,6},{21,7},{26,8},{27... | collective-permute-start | bytes 393224 | tf_op jit(solution)/shard_map/ppermute | solution.py:297
  119.3 30.9 %collective-permute-start.17 = (bf16[2,16,16,128]{3,2,1,0:T(8,128)(2,1)S(1)}, bf16[2,16,16,128]{3,2,1,0:T(8,128)(2,1)S(1)}, u32[]{:S(2)}, u32[]{:S(2)}) collective-permute-start(bf16[2,16,16,128]{3,2,1,0:T(8,128)(2,1)S(1)} %get-tuple-element.57), channel_id=1, source_target_pairs={{22,0},{23,1},{12,2},{13,3},{26,4},{27,5},{16,6},{17,7},{30,8},{31... | collective-permute-start | bytes 393224 | tf_op jit(solution)/shard_map/ppermute | solution.py:297
  137.1 13.3 %collective-permute-start.18 = (bf16[2,16,16,128]{3,2,1,0:T(8,128)(2,1)S(1)}, bf16[2,16,16,128]{3,2,1,0:T(8,128)(2,1)S(1)}, u32[]{:S(2)}, u32[]{:S(2)}) collective-permute-start(bf16[2,16,16,128]{3,2,1,0:T(8,128)(2,1)S(1)} %get-tuple-element.54), channel_id=1, source_target_pairs={{26,0},{27,1},{8,2},{9,3},{30,4},{31,5},{12,6},{13,7},{2,8},{3,9},... | collective-permute-start | bytes 393224 | tf_op jit(solution)/shard_map/ppermute | solution.py:297
  139.2 14.0 %collective-permute-start.19 = (bf16[2,16,16,128]{3,2,1,0:T(8,128)(2,1)S(1)}, bf16[2,16,16,128]{3,2,1,0:T(8,128)(2,1)S(1)}, u32[]{:S(2)}, u32[]{:S(2)}) collective-permute-start(bf16[2,16,16,128]{3,2,1,0:T(8,128)(2,1)S(1)} %get-tuple-element.53), channel_id=1, source_target_pairs={{30,0},{31,1},{4,2},{5,3},{2,4},{3,5},{8,6},{9,7},{6,8},{7,9},{12,... | collective-permute-start | bytes 393224 | tf_op jit(solution)/shard_map/ppermute | solution.py:297
  144.9 10.1 %collective-permute-start.7 = (bf16[2,16,16,128]{3,2,1,0:T(8,128)(2,1)S(1)}, bf16[2,16,16,128]{3,2,1,0:T(8,128)(2,1)S(1)}, u32[]{:S(2)}, u32[]{:S(2)}) collective-permute-start(bf16[2,16,16,128]{3,2,1,0:T(8,128)(2,1)S(1)} %get-tuple-element.55), channel_id=1, source_target_pairs={{4,0},{5,1},{30,2},{31,3},{8,4},{9,5},{2,6},{3,7},{12,8},{13,9},{6... | collective-permute-start | bytes 393224 | tf_op jit(solution)/shard_map/ppermute | solution.py:297
  155.8 10.1 %collective-permute-start.20 = (bf16[48,3584]{1,0:T(8,128)(2,1)S(1)}, bf16[48,3584]{1,0:T(8,128)(2,1)S(1)}, u32[]{:S(2)}, u32[]{:S(2)}) collective-permute-start(bf16[48,3584]{1,0:T(8,128)(2,1)S(1)} %get-tuple-element.52), channel_id=1, source_target_pairs={{0,32},{32,64},{64,96},{96,128},{128,160},{160,192},{192,224},{224... | collective-permute-start | bytes 1032200 | tf_op jit(solution)/shard_map/ppermute | solution.py:279
  159.0 11.9 %collective-permute-start.21 = (bf16[48,3584]{1,0:T(8,128)(2,1)S(1)}, bf16[48,3584]{1,0:T(8,128)(2,1)S(1)}, u32[]{:S(2)}, u32[]{:S(2)}) collective-permute-start(bf16[48,3584]{1,0:T(8,128)(2,1)S(1)} %get-tuple-element.51), channel_id=1, source_target_pairs={{32,0},{64,32},{96,64},{128,96},{160,128},{192,160},{224,192},{256... | collective-permute-start | bytes 1032200 | tf_op jit(solution)/shard_map/ppermute | solution.py:279

commit v6 on v5

--- a/solution.py
+++ b/solution.py
@@ -134,27 +134,38 @@
 
 
 def expert_kernel(own_ref, chip_ref, *rest):
-    ups, downs, outs, rows_ref = rest[:2], rest[2:4], rest[4:6], rest[6]
+    ups, down_sources, outs, downs, arrived = rest[:2], rest[2:4], rest[4:6], rest[6:8], rest[8]
+    copies = [
+        pltpu.make_async_copy(source, down_ref, arrived.at[core])
+        for core, (source, down_ref) in enumerate(zip(down_sources, downs))
+    ]
+    for copy in copies:
+        copy.start()
     ins = (own_ref, chip_ref)
     packets = own_ref.shape[0]
     pairs = own_ref.shape[1] - 2
     main = packets * MAIN
     tails = [read_tail(ref) for ref in ins]
+    hidden_pre = [0.0, 0.0]
     for pair in range(pairs):
-        columns = slice(pair * 256, (pair + 1) * 256)
-        for index, ref in enumerate(ins):
-            rows_ref[index * main : (index + 1) * main, columns] = read_pair(ref, pair)
-        for half in range(2):
-            chunk = 2 * pair + half
-            block = jnp.concatenate(
-                [tail[chunk * packets : (chunk + 1) * packets] for tail in tails], axis=0
+        first = 2 * pair * packets
+        low = [tail[first : first + packets] for tail in tails]
+        high = [tail[first + packets : first + 2 * packets] for tail in tails]
+        last = jnp.concatenate(
+            [jnp.concatenate(low, axis=0), jnp.concatenate(high, axis=0)], axis=1
+        )
+        rows = jnp.concatenate(
+            [read_pair(ref, pair) for ref in ins] + [last.astype(jnp.bfloat16)], axis=0
+        )
+        for core, up_ref in enumerate(ups):
+            hidden_pre[core] = hidden_pre[core] + jnp.dot(
+                rows, up_ref[0, pair * 256 : (pair + 1) * 256], preferred_element_type=jnp.float32
             )
-            rows_ref[2 * main :, chunk * LANES : (chunk + 1) * LANES] = block.astype(jnp.bfloat16)
-    rows = rows_ref[...]
-    activated = []
-    for up_ref in ups:
-        hidden_pre = jnp.dot(rows, up_ref[0], preferred_element_type=jnp.float32)
-        activated.append((hidden_pre / (1.0 + jnp.exp(-hidden_pre))).astype(jnp.bfloat16))
+    activated = [
+        (hidden / (1.0 + jnp.exp(-hidden))).astype(jnp.bfloat16) for hidden in hidden_pre
+    ]
+    for copy in copies:
+        copy.wait()
     tail_chunks = [[] for _ in ins]
     for pair in range(pairs):
         columns = slice(pair * 256, (pair + 1) * 256)
@@ -243,16 +254,16 @@
 
 def run_expert(own, chip, ups, downs):
     packet = jax.ShapeDtypeStruct(own.shape, own.dtype)
-    rows = 2 * own.shape[0] * (MAIN + 1)
-    width = ups[0].shape[1]
     operands = (own, chip, *ups, *downs)
     return pl.pallas_call(
         expert_kernel,
         grid=(1,),
         out_shape=(packet,) * 2,
-        in_specs=[whole(a) for a in operands],
+        in_specs=[whole(a) for a in (own, chip, *ups)]
+        + [pl.BlockSpec(memory_space=pl.ANY) for _ in downs],
         out_specs=(whole(packet),) * 2,
-        scratch_shapes=[pltpu.VMEM((rows, width), jnp.bfloat16)],
+        scratch_shapes=[pltpu.VMEM(a.shape, a.dtype) for a in downs]
+        + [pltpu.SemaphoreType.DMA((len(downs),))],
         compiler_params=params(),
         name="expert",
     )(*operands)

time: 174 us -> 174 us (level)
  no operation moved by 1% of the time
where the time goes in v6:
time: 174 us; the launch traced here: 172 us
  starting transfers between devices  107 us (61%)
  waiting for transfers between devices  50.2 us (29%)
  Pallas kernels  9.55 us (5%)
  local copies, waits for them, and re-layouts  3.45 us (2%)
    ppermute x14, starting transfers between devices, delivered(): return lax.ppermute(packet, 'expert', route)  79.3 us
    ppermute x6, waiting for transfers between devices, swapped(): lax.ppermute(block, 'expert', [(i, i ^ bit) for i in range(lax.axis_size(...  23.5 us
    ppermute x6, starting transfers between devices, swapped(): lax.ppermute(block, 'expert', [(i, i ^ bit) for i in range(lax.axis_size(...  21.9 us
    ppermute x14, waiting for transfers between devices, delivered(): return lax.ppermute(packet, 'expert', route)  17.6 us
    ppermute x2, waiting for transfers between devices, passed_along(): return lax.ppermute(block, axis, route)  9.14 us
    pallas_call x2, Pallas kernels, run_expert(): pl.pallas_call(expert_kernel, grid=(1,), out_shape=(packet,) * 2, in_spec...  7.24 us
    ppermute x2, starting transfers between devices, passed_along(): return lax.ppermute(block, axis, route)  5.84 us
  transfers between devices with their start and end apart: 22, of which 13 were waited for; matrix products, arithmetic and copies ran while one was open for 0% of the time, Pallas kernels for 5%

profile of v6, /device:TPU:24, one launch (start us, length us, event | category | flops | bytes accessed | tf_op | source)
XLA Modules:
  0.0 171.9 jit_solution(10625143668040336449)
XLA Ops:
  0.0 0.0 copy-start
  0.0 2.0 %collective-permute-start = (bf16[1,3584,256]{2,1,0:T(8,128)(2,1)}, bf16[1,3584,256]{2,1,0:T(8,128)(2,1)S(1)}, u32[]{:S(2)}, u32[]{:S(2)}) collective-permute-start(bf16[1,3584,256]{2,1,0:T(8,128)(2,1)} %rest_0_.3), channel_id=1, source_target_pairs={{0,1},{1,0},{2,3},{3,2},{4,5},{5,4},{6,7},{7,6},{8,9},{9,8},{10,11... | collective-permute-start | bytes 5505032 | tf_op jit(solution)/shard_map/ppermute | solution.py:294
  2.0 2.4 %collective-permute-start.1 = (bf16[1,256,3584]{2,1,0:T(8,128)(2,1)}, bf16[1,256,3584]{2,1,0:T(8,128)(2,1)S(1)}, u32[]{:S(2)}, u32[]{:S(2)}) collective-permute-start(bf16[1,256,3584]{2,1,0:T(8,128)(2,1)} %rest_2_.3), channel_id=1, source_target_pairs={{0,1},{1,0},{2,3},{3,2},{4,5},{5,4},{6,7},{7,6},{8,9},{9,8},{10,11... | collective-permute-start | bytes 5505032 | tf_op jit(solution)/shard_map/ppermute | solution.py:294
  4.5 0.0 copy-start.1
  4.5 1.1 copy-done.1
  5.6 0.8 copy-done.3
  6.4 0.0 copy-start.4
  6.4 0.7 copy-done.4
  7.1 0.7 copy-done.5
  7.8 1.5 prepare.1
  9.3 0.0 collective-permute-done.rest_1_
  9.3 0.0 collective-permute-done.1.rest_3_
  9.3 0.0 copy-start.6
  9.3 9.1 %collective-permute-start.8 = (bf16[2,16,16,128]{3,2,1,0:T(8,128)(2,1)S(1)}, bf16[2,16,16,128]{3,2,1,0:T(8,128)(2,1)S(1)}, u32[]{:S(2)}, u32[]{:S(2)}) collective-permute-start(bf16[2,16,16,128]{3,2,1,0:T(8,128)(2,1)S(1)} %get-tuple-element.42), channel_id=1, source_target_pairs={{0,8},{1,9},{2,26},{3,27},{4,12},{5,13},{6,30},{7,31},{8,16},{9,17... | collective-permute-start | bytes 393224 | tf_op jit(solution)/shard_map/ppermute | solution.py:308
  18.4 8.6 %collective-permute-start.9 = (bf16[2,16,16,128]{3,2,1,0:T(8,128)(2,1)S(1)}, bf16[2,16,16,128]{3,2,1,0:T(8,128)(2,1)S(1)}, u32[]{:S(2)}, u32[]{:S(2)}) collective-permute-start(bf16[2,16,16,128]{3,2,1,0:T(8,128)(2,1)S(1)} %get-tuple-element.44), channel_id=1, source_target_pairs={{0,22},{1,23},{2,12},{3,13},{4,26},{5,27},{6,16},{7,17},{8,30},{9,... | collective-permute-start | bytes 393224 | tf_op jit(solution)/shard_map/ppermute | solution.py:308
  27.0 6.1 %collective-permute-start.10 = (bf16[2,16,16,128]{3,2,1,0:T(8,128)(2,1)S(1)}, bf16[2,16,16,128]{3,2,1,0:T(8,128)(2,1)S(1)}, u32[]{:S(2)}, u32[]{:S(2)}) collective-permute-start(bf16[2,16,16,128]{3,2,1,0:T(8,128)(2,1)S(1)} %get-tuple-element.46), channel_id=1, source_target_pairs={{0,12},{1,13},{2,22},{3,23},{4,16},{5,17},{6,26},{7,27},{8,20},{9,... | collective-permute-start | bytes 393224 | tf_op jit(solution)/shard_map/ppermute | solution.py:308
  33.1 8.0 %collective-permute-start.11 = (bf16[2,16,16,128]{3,2,1,0:T(8,128)(2,1)S(1)}, bf16[2,16,16,128]{3,2,1,0:T(8,128)(2,1)S(1)}, u32[]{:S(2)}, u32[]{:S(2)}) collective-permute-start(bf16[2,16,16,128]{3,2,1,0:T(8,128)(2,1)S(1)} %get-tuple-element.48), channel_id=1, source_target_pairs={{0,18},{1,19},{2,16},{3,17},{4,22},{5,23},{6,20},{7,21},{8,26},{9,... | collective-permute-start | bytes 393224 | tf_op jit(solution)/shard_map/ppermute | solution.py:308
  41.2 1.9 %collective-permute-start.2 = (bf16[2,16,16,128]{3,2,1,0:T(8,128)(2,1)S(1)}, bf16[2,16,16,128]{3,2,1,0:T(8,128)(2,1)S(1)}, u32[]{:S(2)}, u32[]{:S(2)}) collective-permute-start(bf16[2,16,16,128]{3,2,1,0:T(8,128)(2,1)S(1)} %get-tuple-element.34), channel_id=1, source_target_pairs={{0,30},{1,31},{2,4},{3,5},{4,2},{5,3},{6,8},{7,9},{8,6},{9,7},{10,... | collective-permute-start | bytes 393224 | tf_op jit(solution)/shard_map/ppermute | solution.py:308
  43.1 0.0 collective-permute-done.8
  43.1 2.2 %collective-permute-start.3 = (bf16[2,16,16,128]{3,2,1,0:T(8,128)(2,1)S(1)}, bf16[2,16,16,128]{3,2,1,0:T(8,128)(2,1)S(1)}, u32[]{:S(2)}, u32[]{:S(2)}) collective-permute-start(bf16[2,16,16,128]{3,2,1,0:T(8,128)(2,1)S(1)} %get-tuple-element.36), channel_id=1, source_target_pairs={{0,4},{1,5},{2,30},{3,31},{4,8},{5,9},{6,2},{7,3},{8,12},{9,13},{1... | collective-permute-start | bytes 393224 | tf_op jit(solution)/shard_map/ppermute | solution.py:308
  45.3 2.5 %collective-permute-done.9 = bf16[2,16,16,128]{3,2,1,0:T(8,128)(2,1)S(1)} collective-permute-done((bf16[2,16,16,128]{3,2,1,0:T(8,128)(2,1)S(1)}, bf16[2,16,16,128]{3,2,1,0:T(8,128)(2,1)S(1)}, u32[]{:S(2)}, u32[]{:S(2)}) %collective-permute-start.9) | collective-permute-done | bytes 131104 | tf_op jit(solution)/shard_map/ppermute | solution.py:308
  47.9 5.9 %collective-permute-start.4 = (bf16[2,16,16,128]{3,2,1,0:T(8,128)(2,1)S(1)}, bf16[2,16,16,128]{3,2,1,0:T(8,128)(2,1)S(1)}, u32[]{:S(2)}, u32[]{:S(2)}) collective-permute-start(bf16[2,16,16,128]{3,2,1,0:T(8,128)(2,1)S(1)} %get-tuple-element.38), channel_id=1, source_target_pairs={{0,26},{1,27},{2,8},{3,9},{4,30},{5,31},{6,12},{7,13},{8,2},{9,3},... | collective-permute-start | bytes 393224 | tf_op jit(solution)/shard_map/ppermute | solution.py:308
  53.8 0.0 collective-permute-done.10
  53.9 4.7 %collective-permute-done.11 = bf16[2,16,16,128]{3,2,1,0:T(8,128)(2,1)S(1)} collective-permute-done((bf16[2,16,16,128]{3,2,1,0:T(8,128)(2,1)S(1)}, bf16[2,16,16,128]{3,2,1,0:T(8,128)(2,1)S(1)}, u32[]{:S(2)}, u32[]{:S(2)}) %collective-permute-start.11) | collective-permute-done | bytes 131104 | tf_op jit(solution)/shard_map/ppermute | solution.py:308
  58.6 3.9 %collective-permute-start.12 = (bf16[8,16,16,128]{3,2,1,0:T(8,128)(2,1)S(1)}, bf16[8,16,16,128]{3,2,1,0:T(8,128)(2,1)S(1)}, u32[]{:S(2)}, u32[]{:S(2)}) collective-permute-start(bf16[8,16,16,128]{3,2,1,0:T(8,128)(2,1)S(1)} %constant_dynamic-update-slice_fusion.4.own_ref), channel_id=1, source_target_pairs={{0,2},{1,3},{2,0},{3,1},{4,6},{5,7},{6,4},{7,5},{8,10},{9,11},{10,... | collective-permute-start | bytes 1572872 | tf_op jit(solution)/shard_map/ppermute | solution.py:294
  62.5 1.4 collective-permute-done.2
  63.9 0.0 collective-permute-done.3
  63.9 4.2 %collective-permute-done.4 = bf16[2,16,16,128]{3,2,1,0:T(8,128)(2,1)S(1)} collective-permute-done((bf16[2,16,16,128]{3,2,1,0:T(8,128)(2,1)S(1)}, bf16[2,16,16,128]{3,2,1,0:T(8,128)(2,1)S(1)}, u32[]{:S(2)}, u32[]{:S(2)}) %collective-permute-start.4) | collective-permute-done | bytes 131104 | tf_op jit(solution)/shard_map/ppermute | solution.py:308
  68.1 5.7 %collective-permute-start.5 = (bf16[8,16,16,128]{3,2,1,0:T(8,128)(2,1)S(1)}, bf16[8,16,16,128]{3,2,1,0:T(8,128)(2,1)S(1)}, u32[]{:S(2)}, u32[]{:S(2)}) collective-permute-start(bf16[8,16,16,128]{3,2,1,0:T(8,128)(2,1)S(1)} %constant_dynamic-update-slice_fusion.own_ref), channel_id=1, source_target_pairs={{0,2},{1,3},{2,0},{3,1},{4,6},{5,7},{6,4},{7,5},{8,10},{9,11},{10,... | collective-permute-start | bytes 1572872 | tf_op jit(solution)/shard_map/ppermute | solution.py:294
  73.9 3.6 %collective-permute-done.12.chip_ref = bf16[8,16,16,128]{3,2,1,0:T(8,128)(2,1)S(1)} collective-permute-done((bf16[8,16,16,128]{3,2,1,0:T(8,128)(2,1)S(1)}, bf16[8,16,16,128]{3,2,1,0:T(8,128)(2,1)S(1)}, u32[]{:S(2)}, u32[]{:S(2)}) %collective-permute-start.12) | collective-permute-done | bytes 524320 | tf_op jit(solution)/shard_map/ppermute | solution.py:294
  77.5 0.0 copy-done.6
  77.5 0.0 copy-done
  77.5 3.6 %expert.3 = (bf16[8,16,16,128]{3,2,1,0:T(8,128)(2,1)S(1)}, bf16[8,16,16,128]{3,2,1,0:T(8,128)(2,1)S(1)}) custom-call(bf16[8,16,16,128]{3,2,1,0:T(8,128)(2,1)S(1)} %constant_dynamic-update-slice_fusion.4.own_ref, bf16[8,16,16,128]{3,2,1,0:T(8,128)(2,1)S(1)} %collective-permute-done.12.chip_ref, bf16[1,3584,256]{2,1,0:T(8,128)(2,1)S(1)} %copy-done, ...), custom_call_target="tpu_custom_call" | custom-call | tf_op jit(solution)/shard_map/expert/pallas_call | solution.py:258
  81.1 3.9 %collective-permute-start.13 = (bf16[8,16,16,128]{3,2,1,0:T(8,128)(2,1)S(1)}, bf16[8,16,16,128]{3,2,1,0:T(8,128)(2,1)S(1)}, u32[]{:S(2)}, u32[]{:S(2)}) collective-permute-start(bf16[8,16,16,128]{3,2,1,0:T(8,128)(2,1)S(1)} %get-tuple-element.50), channel_id=1, source_target_pairs={{0,2},{1,3},{2,0},{3,1},{4,6},{5,7},{6,4},{7,5},{8,10},{9,11},{10,... | collective-permute-start | bytes 1572872 | tf_op jit(solution)/shard_map/ppermute | solution.py:294
  85.0 3.7 %collective-permute-done.5.chip_ref = bf16[8,16,16,128]{3,2,1,0:T(8,128)(2,1)S(1)} collective-permute-done((bf16[8,16,16,128]{3,2,1,0:T(8,128)(2,1)S(1)}, bf16[8,16,16,128]{3,2,1,0:T(8,128)(2,1)S(1)}, u32[]{:S(2)}, u32[]{:S(2)}) %collective-permute-start.5) | collective-permute-done | bytes 524320 | tf_op jit(solution)/shard_map/ppermute | solution.py:294
  88.8 3.6 %expert.2 = (bf16[8,16,16,128]{3,2,1,0:T(8,128)(2,1)S(1)}, bf16[8,16,16,128]{3,2,1,0:T(8,128)(2,1)S(1)}) custom-call(bf16[8,16,16,128]{3,2,1,0:T(8,128)(2,1)S(1)} %constant_dynamic-update-slice_fusion.own_ref, bf16[8,16,16,128]{3,2,1,0:T(8,128)(2,1)S(1)} %collective-permute-done.5.chip_ref, bf16[1,3584,256]{2,1,0:T(8,128)(2,1)S(1)} %copy-done, ...), custom_call_target="tpu_custom_call" | custom-call | tf_op jit(solution)/shard_map/expert/pallas_call | solution.py:258
  92.4 0.0 copy-start.2
  92.4 4.0 %collective-permute-start.6 = (bf16[8,16,16,128]{3,2,1,0:T(8,128)(2,1)S(1)}, bf16[8,16,16,128]{3,2,1,0:T(8,128)(2,1)S(1)}, u32[]{:S(2)}, u32[]{:S(2)}) collective-permute-start(bf16[8,16,16,128]{3,2,1,0:T(8,128)(2,1)S(1)} %get-tuple-element.40), channel_id=1, source_target_pairs={{0,2},{1,3},{2,0},{3,1},{4,6},{5,7},{6,4},{7,5},{8,10},{9,11},{10,... | collective-permute-start | bytes 1572872 | tf_op jit(solution)/shard_map/ppermute | solution.py:294
  96.4 3.6 %collective-permute-done.13 = bf16[8,16,16,128]{3,2,1,0:T(8,128)(2,1)S(1)} collective-permute-done((bf16[8,16,16,128]{3,2,1,0:T(8,128)(2,1)S(1)}, bf16[8,16,16,128]{3,2,1,0:T(8,128)(2,1)S(1)}, u32[]{:S(2)}, u32[]{:S(2)}) %collective-permute-start.13) | collective-permute-done | bytes 524320 | tf_op jit(solution)/shard_map/ppermute | solution.py:294
  100.0 0.1 add_convert_fusion.2
  100.1 8.1 %collective-permute-start.14 = (bf16[2,16,16,128]{3,2,1,0:T(8,128)(2,1)S(1)}, bf16[2,16,16,128]{3,2,1,0:T(8,128)(2,1)S(1)}, u32[]{:S(2)}, u32[]{:S(2)}) collective-permute-start(bf16[2,16,16,128]{3,2,1,0:T(8,128)(2,1)S(1)} %get-tuple-element.60), channel_id=1, source_target_pairs={{8,0},{9,1},{26,2},{27,3},{12,4},{13,5},{30,6},{31,7},{16,8},{17,9... | collective-permute-start | bytes 393224 | tf_op jit(solution)/shard_map/ppermute | solution.py:308
  108.2 5.8 %collective-permute-start.15 = (bf16[2,16,16,128]{3,2,1,0:T(8,128)(2,1)S(1)}, bf16[2,16,16,128]{3,2,1,0:T(8,128)(2,1)S(1)}, u32[]{:S(2)}, u32[]{:S(2)}) collective-permute-start(bf16[2,16,16,128]{3,2,1,0:T(8,128)(2,1)S(1)} %get-tuple-element.59), channel_id=1, source_target_pairs={{12,0},{13,1},{22,2},{23,3},{16,4},{17,5},{26,6},{27,7},{20,8},{21... | collective-permute-start | bytes 393224 | tf_op jit(solution)/shard_map/ppermute | solution.py:308
  114.0 5.3 %collective-permute-start.16 = (bf16[2,16,16,128]{3,2,1,0:T(8,128)(2,1)S(1)}, bf16[2,16,16,128]{3,2,1,0:T(8,128)(2,1)S(1)}, u32[]{:S(2)}, u32[]{:S(2)}) collective-permute-start(bf16[2,16,16,128]{3,2,1,0:T(8,128)(2,1)S(1)} %get-tuple-element.58), channel_id=1, source_target_pairs={{18,0},{19,1},{16,2},{17,3},{22,4},{23,5},{20,6},{21,7},{26,8},{27... | collective-permute-start | bytes 393224 | tf_op jit(solution)/shard_map/ppermute | solution.py:308
  119.3 5.1 %collective-permute-start.17 = (bf16[2,16,16,128]{3,2,1,0:T(8,128)(2,1)S(1)}, bf16[2,16,16,128]{3,2,1,0:T(8,128)(2,1)S(1)}, u32[]{:S(2)}, u32[]{:S(2)}) collective-permute-start(bf16[2,16,16,128]{3,2,1,0:T(8,128)(2,1)S(1)} %get-tuple-element.57), channel_id=1, source_target_pairs={{22,0},{23,1},{12,2},{13,3},{26,4},{27,5},{16,6},{17,7},{30,8},{31... | collective-permute-start | bytes 393224 | tf_op jit(solution)/shard_map/ppermute | solution.py:308
  124.4 12.5 %collective-permute-done.6 = bf16[8,16,16,128]{3,2,1,0:T(8,128)(2,1)S(1)} collective-permute-done((bf16[8,16,16,128]{3,2,1,0:T(8,128)(2,1)S(1)}, bf16[8,16,16,128]{3,2,1,0:T(8,128)(2,1)S(1)}, u32[]{:S(2)}, u32[]{:S(2)}) %collective-permute-start.6) | collective-permute-done | bytes 524320 | tf_op jit(solution)/shard_map/ppermute | solution.py:294
  136.9 0.1 add_convert_fusion
  137.1 2.1 %collective-permute-start.18 = (bf16[2,16,16,128]{3,2,1,0:T(8,128)(2,1)S(1)}, bf16[2,16,16,128]{3,2,1,0:T(8,128)(2,1)S(1)}, u32[]{:S(2)}, u32[]{:S(2)}) collective-permute-start(bf16[2,16,16,128]{3,2,1,0:T(8,128)(2,1)S(1)} %get-tuple-element.54), channel_id=1, source_target_pairs={{26,0},{27,1},{8,2},{9,3},{30,4},{31,5},{12,6},{13,7},{2,8},{3,9},... | collective-permute-start | bytes 393224 | tf_op jit(solution)/shard_map/ppermute | solution.py:308
  139.2 0.0 collective-permute-done.14.rest_2_
  139.2 5.7 %collective-permute-start.19 = (bf16[2,16,16,128]{3,2,1,0:T(8,128)(2,1)S(1)}, bf16[2,16,16,128]{3,2,1,0:T(8,128)(2,1)S(1)}, u32[]{:S(2)}, u32[]{:S(2)}) collective-permute-start(bf16[2,16,16,128]{3,2,1,0:T(8,128)(2,1)S(1)} %get-tuple-element.53), channel_id=1, source_target_pairs={{30,0},{31,1},{4,2},{5,3},{2,4},{3,5},{8,6},{9,7},{6,8},{7,9},{12,... | collective-permute-start | bytes 393224 | tf_op jit(solution)/shard_map/ppermute | solution.py:308
  144.9 0.0 collective-permute-done.15.rest_3_
  144.9 5.3 %collective-permute-start.7 = (bf16[2,16,16,128]{3,2,1,0:T(8,128)(2,1)S(1)}, bf16[2,16,16,128]{3,2,1,0:T(8,128)(2,1)S(1)}, u32[]{:S(2)}, u32[]{:S(2)}) collective-permute-start(bf16[2,16,16,128]{3,2,1,0:T(8,128)(2,1)S(1)} %get-tuple-element.55), channel_id=1, source_target_pairs={{4,0},{5,1},{30,2},{31,3},{8,4},{9,5},{2,6},{3,7},{12,8},{13,9},{6... | collective-permute-start | bytes 393224 | tf_op jit(solution)/shard_map/ppermute | solution.py:308
  150.2 0.0 collective-permute-done.16.rest_4_
  150.3 0.0 collective-permute-done.17.rest_5_
  150.3 0.1 collective-permute-done.18.rest_6_
  150.3 2.8 %collective-permute-done.19.rest_7_ = bf16[2,16,16,128]{3,2,1,0:T(8,128)(2,1)S(1)} collective-permute-done((bf16[2,16,16,128]{3,2,1,0:T(8,128)(2,1)S(1)}, bf16[2,16,16,128]{3,2,1,0:T(8,128)(2,1)S(1)}, u32[]{:S(2)}, u32[]{:S(2)}) %collective-permute-start.19) | collective-permute-done | bytes 131104 | tf_op jit(solution)/shard_map/ppermute | solution.py:308
  153.2 1.8 %collective-permute-done.7.rest_1_ = bf16[2,16,16,128]{3,2,1,0:T(8,128)(2,1)S(1)} collective-permute-done((bf16[2,16,16,128]{3,2,1,0:T(8,128)(2,1)S(1)}, bf16[2,16,16,128]{3,2,1,0:T(8,128)(2,1)S(1)}, u32[]{:S(2)}, u32[]{:S(2)}) %collective-permute-start.7) | collective-permute-done | bytes 131104 | tf_op jit(solution)/shard_map/ppermute | solution.py:308
  155.0 0.0 copy-done.2
  155.0 0.8 finish.1
  155.8 3.1 %collective-permute-start.20 = (bf16[48,3584]{1,0:T(8,128)(2,1)S(1)}, bf16[48,3584]{1,0:T(8,128)(2,1)S(1)}, u32[]{:S(2)}, u32[]{:S(2)}) collective-permute-start(bf16[48,3584]{1,0:T(8,128)(2,1)S(1)} %get-tuple-element.52), channel_id=1, source_target_pairs={{0,32},{32,64},{64,96},{96,128},{128,160},{160,192},{192,224},{224... | collective-permute-start | bytes 1032200 | tf_op jit(solution)/shard_map/ppermute | solution.py:290
  159.0 2.7 %collective-permute-start.21 = (bf16[48,3584]{1,0:T(8,128)(2,1)S(1)}, bf16[48,3584]{1,0:T(8,128)(2,1)S(1)}, u32[]{:S(2)}, u32[]{:S(2)}) collective-permute-start(bf16[48,3584]{1,0:T(8,128)(2,1)S(1)} %get-tuple-element.51), channel_id=1, source_target_pairs={{32,0},{64,32},{96,64},{128,96},{160,128},{192,160},{224,192},{256... | collective-permute-start | bytes 1032200 | tf_op jit(solution)/shard_map/ppermute | solution.py:290
  161.7 4.2 %collective-permute-done.20 = bf16[48,3584]{1,0:T(8,128)(2,1)S(1)} collective-permute-done((bf16[48,3584]{1,0:T(8,128)(2,1)S(1)}, bf16[48,3584]{1,0:T(8,128)(2,1)S(1)}, u32[]{:S(2)}, u32[]{:S(2)}) %collective-permute-start.20) | collective-permute-done | bytes 344096 | tf_op jit(solution)/shard_map/ppermute | solution.py:290
  166.0 4.9 %collective-permute-done.21 = bf16[48,3584]{1,0:T(8,128)(2,1)S(1)} collective-permute-done((bf16[48,3584]{1,0:T(8,128)(2,1)S(1)}, bf16[48,3584]{1,0:T(8,128)(2,1)S(1)}, u32[]{:S(2)}, u32[]{:S(2)}) %collective-permute-start.21) | collective-permute-done | bytes 344096 | tf_op jit(solution)/shard_map/ppermute | solution.py:290
  170.9 0.1 select_bitcast_fusion
  170.9 0.9 maximum_bitcast_fusion
  (11 shorter events, 0.2 us)
Async XLA Ops:
  0.0 77.5 %copy-start = (bf16[1,3584,256]{2,1,0:T(8,128)(2,1)S(1)}, bf16[1,3584,256]{2,1,0:T(8,128)(2,1)}, u32[]{:S(2)}) copy-start(bf16[1,3584,256]{2,1,0:T(8,128)(2,1)} %rest_0_.3) | copy-start | bytes 5505028
  0.0 9.3 %collective-permute-start = (bf16[1,3584,256]{2,1,0:T(8,128)(2,1)}, bf16[1,3584,256]{2,1,0:T(8,128)(2,1)S(1)}, u32[]{:S(2)}, u32[]{:S(2)}) collective-permute-start(bf16[1,3584,256]{2,1,0:T(8,128)(2,1)} %rest_0_.3), channel_id=1, source_target_pairs={{0,1},{1,0},{2,3},{3,2},{4,5},{5,4},{6,7},{7,6},{8,9},{9,8},{10,11... | collective-permute-start | bytes 5505032 | tf_op jit(solution)/shard_map/ppermute | solution.py:294
  2.0 7.2 %collective-permute-start.1 = (bf16[1,256,3584]{2,1,0:T(8,128)(2,1)}, bf16[1,256,3584]{2,1,0:T(8,128)(2,1)S(1)}, u32[]{:S(2)}, u32[]{:S(2)}) collective-permute-start(bf16[1,256,3584]{2,1,0:T(8,128)(2,1)} %rest_2_.3), channel_id=1, source_target_pairs={{0,1},{1,0},{2,3},{3,2},{4,5},{5,4},{6,7},{7,6},{8,9},{9,8},{10,11... | collective-permute-start | bytes 5505032 | tf_op jit(solution)/shard_map/ppermute | solution.py:294
  4.5 1.1 copy-start.1
  5.6 0.8 copy-start.3
  6.4 0.7 copy-start.4
  7.1 0.7 copy-start.5
  9.3 68.2 %copy-start.6 = (bf16[1,256,3584]{2,1,0:T(8,128)(2,1)}, bf16[1,256,3584]{2,1,0:T(8,128)(2,1)S(1)}, u32[]{:S(2)}) copy-start(bf16[1,256,3584]{2,1,0:T(8,128)(2,1)S(1)} %collective-permute-done.1.rest_3_) | copy-start | bytes 5505028
  9.3 33.8 %collective-permute-start.8 = (bf16[2,16,16,128]{3,2,1,0:T(8,128)(2,1)S(1)}, bf16[2,16,16,128]{3,2,1,0:T(8,128)(2,1)S(1)}, u32[]{:S(2)}, u32[]{:S(2)}) collective-permute-start(bf16[2,16,16,128]{3,2,1,0:T(8,128)(2,1)S(1)} %get-tuple-element.42), channel_id=1, source_target_pairs={{0,8},{1,9},{2,26},{3,27},{4,12},{5,13},{6,30},{7,31},{8,16},{9,17... | collective-permute-start | bytes 393224 | tf_op jit(solution)/shard_map/ppermute | solution.py:308
  18.4 29.5 %collective-permute-start.9 = (bf16[2,16,16,128]{3,2,1,0:T(8,128)(2,1)S(1)}, bf16[2,16,16,128]{3,2,1,0:T(8,128)(2,1)S(1)}, u32[]{:S(2)}, u32[]{:S(2)}) collective-permute-start(bf16[2,16,16,128]{3,2,1,0:T(8,128)(2,1)S(1)} %get-tuple-element.44), channel_id=1, source_target_pairs={{0,22},{1,23},{2,12},{3,13},{4,26},{5,27},{6,16},{7,17},{8,30},{9,... | collective-permute-start | bytes 393224 | tf_op jit(solution)/shard_map/ppermute | solution.py:308
  27.0 26.8 %collective-permute-start.10 = (bf16[2,16,16,128]{3,2,1,0:T(8,128)(2,1)S(1)}, bf16[2,16,16,128]{3,2,1,0:T(8,128)(2,1)S(1)}, u32[]{:S(2)}, u32[]{:S(2)}) collective-permute-start(bf16[2,16,16,128]{3,2,1,0:T(8,128)(2,1)S(1)} %get-tuple-element.46), channel_id=1, source_target_pairs={{0,12},{1,13},{2,22},{3,23},{4,16},{5,17},{6,26},{7,27},{8,20},{9,... | collective-permute-start | bytes 393224 | tf_op jit(solution)/shard_map/ppermute | solution.py:308
  33.1 25.4 %collective-permute-start.11 = (bf16[2,16,16,128]{3,2,1,0:T(8,128)(2,1)S(1)}, bf16[2,16,16,128]{3,2,1,0:T(8,128)(2,1)S(1)}, u32[]{:S(2)}, u32[]{:S(2)}) collective-permute-start(bf16[2,16,16,128]{3,2,1,0:T(8,128)(2,1)S(1)} %get-tuple-element.48), channel_id=1, source_target_pairs={{0,18},{1,19},{2,16},{3,17},{4,22},{5,23},{6,20},{7,21},{8,26},{9,... | collective-permute-start | bytes 393224 | tf_op jit(solution)/shard_map/ppermute | solution.py:308
  41.2 22.6 %collective-permute-start.2 = (bf16[2,16,16,128]{3,2,1,0:T(8,128)(2,1)S(1)}, bf16[2,16,16,128]{3,2,1,0:T(8,128)(2,1)S(1)}, u32[]{:S(2)}, u32[]{:S(2)}) collective-permute-start(bf16[2,16,16,128]{3,2,1,0:T(8,128)(2,1)S(1)} %get-tuple-element.34), channel_id=1, source_target_pairs={{0,30},{1,31},{2,4},{3,5},{4,2},{5,3},{6,8},{7,9},{8,6},{9,7},{10,... | collective-permute-start | bytes 393224 | tf_op jit(solution)/shard_map/ppermute | solution.py:308
  43.1 20.7 %collective-permute-start.3 = (bf16[2,16,16,128]{3,2,1,0:T(8,128)(2,1)S(1)}, bf16[2,16,16,128]{3,2,1,0:T(8,128)(2,1)S(1)}, u32[]{:S(2)}, u32[]{:S(2)}) collective-permute-start(bf16[2,16,16,128]{3,2,1,0:T(8,128)(2,1)S(1)} %get-tuple-element.36), channel_id=1, source_target_pairs={{0,4},{1,5},{2,30},{3,31},{4,8},{5,9},{6,2},{7,3},{8,12},{9,13},{1... | collective-permute-start | bytes 393224 | tf_op jit(solution)/shard_map/ppermute | solution.py:308
  47.9 20.3 %collective-permute-start.4 = (bf16[2,16,16,128]{3,2,1,0:T(8,128)(2,1)S(1)}, bf16[2,16,16,128]{3,2,1,0:T(8,128)(2,1)S(1)}, u32[]{:S(2)}, u32[]{:S(2)}) collective-permute-start(bf16[2,16,16,128]{3,2,1,0:T(8,128)(2,1)S(1)} %get-tuple-element.38), channel_id=1, source_target_pairs={{0,26},{1,27},{2,8},{3,9},{4,30},{5,31},{6,12},{7,13},{8,2},{9,3},... | collective-permute-start | bytes 393224 | tf_op jit(solution)/shard_map/ppermute | solution.py:308
  58.6 18.9 %collective-permute-start.12 = (bf16[8,16,16,128]{3,2,1,0:T(8,128)(2,1)S(1)}, bf16[8,16,16,128]{3,2,1,0:T(8,128)(2,1)S(1)}, u32[]{:S(2)}, u32[]{:S(2)}) collective-permute-start(bf16[8,16,16,128]{3,2,1,0:T(8,128)(2,1)S(1)} %constant_dynamic-update-slice_fusion.4.own_ref), channel_id=1, source_target_pairs={{0,2},{1,3},{2,0},{3,1},{4,6},{5,7},{6,4},{7,5},{8,10},{9,11},{10,... | collective-permute-start | bytes 1572872 | tf_op jit(solution)/shard_map/ppermute | solution.py:294
  68.1 20.6 %collective-permute-start.5 = (bf16[8,16,16,128]{3,2,1,0:T(8,128)(2,1)S(1)}, bf16[8,16,16,128]{3,2,1,0:T(8,128)(2,1)S(1)}, u32[]{:S(2)}, u32[]{:S(2)}) collective-permute-start(bf16[8,16,16,128]{3,2,1,0:T(8,128)(2,1)S(1)} %constant_dynamic-update-slice_fusion.own_ref), channel_id=1, source_target_pairs={{0,2},{1,3},{2,0},{3,1},{4,6},{5,7},{6,4},{7,5},{8,10},{9,11},{10,... | collective-permute-start | bytes 1572872 | tf_op jit(solution)/shard_map/ppermute | solution.py:294
  81.1 18.8 %collective-permute-start.13 = (bf16[8,16,16,128]{3,2,1,0:T(8,128)(2,1)S(1)}, bf16[8,16,16,128]{3,2,1,0:T(8,128)(2,1)S(1)}, u32[]{:S(2)}, u32[]{:S(2)}) collective-permute-start(bf16[8,16,16,128]{3,2,1,0:T(8,128)(2,1)S(1)} %get-tuple-element.50), channel_id=1, source_target_pairs={{0,2},{1,3},{2,0},{3,1},{4,6},{5,7},{6,4},{7,5},{8,10},{9,11},{10,... | collective-permute-start | bytes 1572872 | tf_op jit(solution)/shard_map/ppermute | solution.py:294
  92.4 62.6 %copy-start.2 = (bf16[2,1,48,3584]{3,2,1,0:T(8,128)(2,1)S(1)}, bf16[2,1,48,3584]{3,2,1,0:T(8,128)(2,1)}, u32[]{:S(2)}) copy-start(bf16[2,1,48,3584]{3,2,1,0:T(8,128)(2,1)} %x_ref.3) | copy-start | bytes 2064388
  92.4 44.5 %collective-permute-start.6 = (bf16[8,16,16,128]{3,2,1,0:T(8,128)(2,1)S(1)}, bf16[8,16,16,128]{3,2,1,0:T(8,128)(2,1)S(1)}, u32[]{:S(2)}, u32[]{:S(2)}) collective-permute-start(bf16[8,16,16,128]{3,2,1,0:T(8,128)(2,1)S(1)} %get-tuple-element.40), channel_id=1, source_target_pairs={{0,2},{1,3},{2,0},{3,1},{4,6},{5,7},{6,4},{7,5},{8,10},{9,11},{10,... | collective-permute-start | bytes 1572872 | tf_op jit(solution)/shard_map/ppermute | solution.py:294
  100.1 39.0 %collective-permute-start.14 = (bf16[2,16,16,128]{3,2,1,0:T(8,128)(2,1)S(1)}, bf16[2,16,16,128]{3,2,1,0:T(8,128)(2,1)S(1)}, u32[]{:S(2)}, u32[]{:S(2)}) collective-permute-start(bf16[2,16,16,128]{3,2,1,0:T(8,128)(2,1)S(1)} %get-tuple-element.60), channel_id=1, source_target_pairs={{8,0},{9,1},{26,2},{27,3},{12,4},{13,5},{30,6},{31,7},{16,8},{17,9... | collective-permute-start | bytes 393224 | tf_op jit(solution)/shard_map/ppermute | solution.py:308
  108.2 36.7 %collective-permute-start.15 = (bf16[2,16,16,128]{3,2,1,0:T(8,128)(2,1)S(1)}, bf16[2,16,16,128]{3,2,1,0:T(8,128)(2,1)S(1)}, u32[]{:S(2)}, u32[]{:S(2)}) collective-permute-start(bf16[2,16,16,128]{3,2,1,0:T(8,128)(2,1)S(1)} %get-tuple-element.59), channel_id=1, source_target_pairs={{12,0},{13,1},{22,2},{23,3},{16,4},{17,5},{26,6},{27,7},{20,8},{21... | collective-permute-start | bytes 393224 | tf_op jit(solution)/shard_map/ppermute | solution.py:308
  114.0 36.2 %collective-permute-start.16 = (bf16[2,16,16,128]{3,2,1,0:T(8,128)(2,1)S(1)}, bf16[2,16,16,128]{3,2,1,0:T(8,128)(2,1)S(1)}, u32[]{:S(2)}, u32[]{:S(2)}) collective-permute-start(bf16[2,16,16,128]{3,2,1,0:T(8,128)(2,1)S(1)} %get-tuple-element.58), channel_id=1, source_target_pairs={{18,0},{19,1},{16,2},{17,3},{22,4},{23,5},{20,6},{21,7},{26,8},{27... | collective-permute-start | bytes 393224 | tf_op jit(solution)/shard_map/ppermute | solution.py:308
  119.3 30.9 %collective-permute-start.17 = (bf16[2,16,16,128]{3,2,1,0:T(8,128)(2,1)S(1)}, bf16[2,16,16,128]{3,2,1,0:T(8,128)(2,1)S(1)}, u32[]{:S(2)}, u32[]{:S(2)}) collective-permute-start(bf16[2,16,16,128]{3,2,1,0:T(8,128)(2,1)S(1)} %get-tuple-element.57), channel_id=1, source_target_pairs={{22,0},{23,1},{12,2},{13,3},{26,4},{27,5},{16,6},{17,7},{30,8},{31... | collective-permute-start | bytes 393224 | tf_op jit(solution)/shard_map/ppermute | solution.py:308
  137.1 13.3 %collective-permute-start.18 = (bf16[2,16,16,128]{3,2,1,0:T(8,128)(2,1)S(1)}, bf16[2,16,16,128]{3,2,1,0:T(8,128)(2,1)S(1)}, u32[]{:S(2)}, u32[]{:S(2)}) collective-permute-start(bf16[2,16,16,128]{3,2,1,0:T(8,128)(2,1)S(1)} %get-tuple-element.54), channel_id=1, source_target_pairs={{26,0},{27,1},{8,2},{9,3},{30,4},{31,5},{12,6},{13,7},{2,8},{3,9},... | collective-permute-start | bytes 393224 | tf_op jit(solution)/shard_map/ppermute | solution.py:308
  139.2 14.0 %collective-permute-start.19 = (bf16[2,16,16,128]{3,2,1,0:T(8,128)(2,1)S(1)}, bf16[2,16,16,128]{3,2,1,0:T(8,128)(2,1)S(1)}, u32[]{:S(2)}, u32[]{:S(2)}) collective-permute-start(bf16[2,16,16,128]{3,2,1,0:T(8,128)(2,1)S(1)} %get-tuple-element.53), channel_id=1, source_target_pairs={{30,0},{31,1},{4,2},{5,3},{2,4},{3,5},{8,6},{9,7},{6,8},{7,9},{12,... | collective-permute-start | bytes 393224 | tf_op jit(solution)/shard_map/ppermute | solution.py:308
  144.9 10.1 %collective-permute-start.7 = (bf16[2,16,16,128]{3,2,1,0:T(8,128)(2,1)S(1)}, bf16[2,16,16,128]{3,2,1,0:T(8,128)(2,1)S(1)}, u32[]{:S(2)}, u32[]{:S(2)}) collective-permute-start(bf16[2,16,16,128]{3,2,1,0:T(8,128)(2,1)S(1)} %get-tuple-element.55), channel_id=1, source_target_pairs={{4,0},{5,1},{30,2},{31,3},{8,4},{9,5},{2,6},{3,7},{12,8},{13,9},{6... | collective-permute-start | bytes 393224 | tf_op jit(solution)/shard_map/ppermute | solution.py:308
  155.8 10.1 %collective-permute-start.20 = (bf16[48,3584]{1,0:T(8,128)(2,1)S(1)}, bf16[48,3584]{1,0:T(8,128)(2,1)S(1)}, u32[]{:S(2)}, u32[]{:S(2)}) collective-permute-start(bf16[48,3584]{1,0:T(8,128)(2,1)S(1)} %get-tuple-element.52), channel_id=1, source_target_pairs={{0,32},{32,64},{64,96},{96,128},{128,160},{160,192},{192,224},{224... | collective-permute-start | bytes 1032200 | tf_op jit(solution)/shard_map/ppermute | solution.py:290
  159.0 11.9 %collective-permute-start.21 = (bf16[48,3584]{1,0:T(8,128)(2,1)S(1)}, bf16[48,3584]{1,0:T(8,128)(2,1)S(1)}, u32[]{:S(2)}, u32[]{:S(2)}) collective-permute-start(bf16[48,3584]{1,0:T(8,128)(2,1)S(1)} %get-tuple-element.51), channel_id=1, source_target_pairs={{32,0},{64,32},{96,64},{128,96},{160,128},{192,160},{224,192},{256... | collective-permute-start | bytes 1032200 | tf_op jit(solution)/shard_map/ppermute | solution.py:290

commit v7 on v6

--- a/solution.py
+++ b/solution.py
@@ -1,3 +1,5 @@
+import functools
+
 import jax
 import jax.numpy as jnp
 from jax import lax
@@ -184,16 +186,14 @@
         write_tail(ref, jnp.concatenate(tail_chunks[index], axis=0).astype(jnp.bfloat16))
 
 
-def finish_kernel(x_ref, gate_ref, row_ref, *rest):
-    packet_refs, out_refs = rest[:-2], rest[-2:]
-    for direction, out_ref in enumerate(out_refs):
-        finish_direction(
-            x_ref.at[direction],
-            gate_ref.at[direction],
-            row_ref.at[direction],
-            [ref.at[direction] for ref in packet_refs],
-            out_ref,
-        )
+def finish_kernel(direction, x_ref, gate_ref, row_ref, *rest):
+    finish_direction(
+        x_ref.at[direction],
+        gate_ref.at[direction],
+        row_ref.at[direction],
+        [ref.at[direction] for ref in rest[:-1]],
+        rest[-1],
+    )
 
 
 def finish_direction(x_ref, gate_ref, row_ref, packet_refs, out_ref):
@@ -269,16 +269,16 @@
     )(*operands)
 
 
-def finish(carried, gate, row, packets):
+def finish(direction, carried, gate, row, packets):
     tokens, width = carried.shape[2:]
     out = jax.ShapeDtypeStruct((tokens, width), jnp.bfloat16)
     operands = (carried, gate, row, *packets)
     return pl.pallas_call(
-        finish_kernel,
+        functools.partial(finish_kernel, direction),
         grid=(1,),
-        out_shape=(out, out),
+        out_shape=out,
         in_specs=[whole(a) for a in operands],
-        out_specs=(whole(out), whole(out)),
+        out_specs=whole(out),
         compiler_params=params(),
         name="finish",
     )(*operands)
@@ -331,7 +331,7 @@
         for place, turn in enumerate(group):
             part = slice(2 * place, 2 * place + 2)
             returned[turn] = delivered(added(for_own[part], from_chip[part]), turn, True)
-    layer_outputs = finish(carried, gate, row, returned)
+    layer_outputs = [finish(d, carried, gate, row, returned) for d in range(2)]
     section_index = lax.axis_index("section")
     last_section = lax.axis_size("section") - 1
     from_below = passed_along(layer_outputs[0], "section", 1)

time: 174 us -> 174 us (level)
  no operation moved by 1% of the time
where the time goes in v7:
time: 174 us; the launch traced here: 172 us
  starting transfers between devices  107 us (61%)
  waiting for transfers between devices  50.2 us (29%)
  Pallas kernels  9.67 us (6%)
  local copies, waits for them, and re-layouts  3.45 us (2%)
    ppermute x14, starting transfers between devices, delivered(): return lax.ppermute(packet, 'expert', route)  79.3 us
    ppermute x6, waiting for transfers between devices, swapped(): lax.ppermute(block, 'expert', [(i, i ^ bit) for i in range(lax.axis_size(...  23.5 us
    ppermute x6, starting transfers between devices, swapped(): lax.ppermute(block, 'expert', [(i, i ^ bit) for i in range(lax.axis_size(...  21.9 us
    ppermute x14, waiting for transfers between devices, delivered(): return lax.ppermute(packet, 'expert', route)  17.6 us
    ppermute x2, waiting for transfers between devices, passed_along(): return lax.ppermute(block, axis, route)  9.13 us
    pallas_call x2, Pallas kernels, run_expert(): pl.pallas_call(expert_kernel, grid=(1,), out_shape=(packet,) * 2, in_spec...  7.24 us
    ppermute x2, starting transfers between devices, passed_along(): return lax.ppermute(block, axis, route)  5.84 us
  transfers between devices with their start and end apart: 22, of which 13 were waited for; matrix products, arithmetic and copies ran while one was open for 0% of the time, Pallas kernels for 5%

profile of v7, /device:TPU:24, one launch (start us, length us, event | category | flops | bytes accessed | tf_op | source)
XLA Modules:
  0.0 172.0 jit_solution(2663380905484194958)
XLA Ops:
  0.0 0.0 copy-start
  0.0 2.0 %collective-permute-start = (bf16[1,3584,256]{2,1,0:T(8,128)(2,1)}, bf16[1,3584,256]{2,1,0:T(8,128)(2,1)S(1)}, u32[]{:S(2)}, u32[]{:S(2)}) collective-permute-start(bf16[1,3584,256]{2,1,0:T(8,128)(2,1)} %rest_0_.3), channel_id=1, source_target_pairs={{0,1},{1,0},{2,3},{3,2},{4,5},{5,4},{6,7},{7,6},{8,9},{9,8},{10,11... | collective-permute-start | bytes 5505032 | tf_op jit(solution)/shard_map/ppermute | solution.py:294
  2.0 2.4 %collective-permute-start.1 = (bf16[1,256,3584]{2,1,0:T(8,128)(2,1)}, bf16[1,256,3584]{2,1,0:T(8,128)(2,1)S(1)}, u32[]{:S(2)}, u32[]{:S(2)}) collective-permute-start(bf16[1,256,3584]{2,1,0:T(8,128)(2,1)} %rest_2_.3), channel_id=1, source_target_pairs={{0,1},{1,0},{2,3},{3,2},{4,5},{5,4},{6,7},{7,6},{8,9},{9,8},{10,11... | collective-permute-start | bytes 5505032 | tf_op jit(solution)/shard_map/ppermute | solution.py:294
  4.5 0.0 copy-start.1
  4.5 1.1 copy-done.1
  5.6 0.0 copy-start.3
  5.6 0.8 copy-done.3
  6.4 0.7 copy-done.4
  7.1 0.7 copy-done.5
  7.8 1.5 prepare.1
  9.3 0.0 collective-permute-done.rest_1_
  9.3 0.0 collective-permute-done.1.rest_3_
  9.3 0.0 copy-start.6
  9.3 9.1 %collective-permute-start.8 = (bf16[2,16,16,128]{3,2,1,0:T(8,128)(2,1)S(1)}, bf16[2,16,16,128]{3,2,1,0:T(8,128)(2,1)S(1)}, u32[]{:S(2)}, u32[]{:S(2)}) collective-permute-start(bf16[2,16,16,128]{3,2,1,0:T(8,128)(2,1)S(1)} %get-tuple-element.40), channel_id=1, source_target_pairs={{0,8},{1,9},{2,26},{3,27},{4,12},{5,13},{6,30},{7,31},{8,16},{9,17... | collective-permute-start | bytes 393224 | tf_op jit(solution)/shard_map/ppermute | solution.py:308
  18.4 8.6 %collective-permute-start.9 = (bf16[2,16,16,128]{3,2,1,0:T(8,128)(2,1)S(1)}, bf16[2,16,16,128]{3,2,1,0:T(8,128)(2,1)S(1)}, u32[]{:S(2)}, u32[]{:S(2)}) collective-permute-start(bf16[2,16,16,128]{3,2,1,0:T(8,128)(2,1)S(1)} %get-tuple-element.42), channel_id=1, source_target_pairs={{0,22},{1,23},{2,12},{3,13},{4,26},{5,27},{6,16},{7,17},{8,30},{9,... | collective-permute-start | bytes 393224 | tf_op jit(solution)/shard_map/ppermute | solution.py:308
  27.0 6.1 %collective-permute-start.10 = (bf16[2,16,16,128]{3,2,1,0:T(8,128)(2,1)S(1)}, bf16[2,16,16,128]{3,2,1,0:T(8,128)(2,1)S(1)}, u32[]{:S(2)}, u32[]{:S(2)}) collective-permute-start(bf16[2,16,16,128]{3,2,1,0:T(8,128)(2,1)S(1)} %get-tuple-element.44), channel_id=1, source_target_pairs={{0,12},{1,13},{2,22},{3,23},{4,16},{5,17},{6,26},{7,27},{8,20},{9,... | collective-permute-start | bytes 393224 | tf_op jit(solution)/shard_map/ppermute | solution.py:308
  33.1 8.0 %collective-permute-start.11 = (bf16[2,16,16,128]{3,2,1,0:T(8,128)(2,1)S(1)}, bf16[2,16,16,128]{3,2,1,0:T(8,128)(2,1)S(1)}, u32[]{:S(2)}, u32[]{:S(2)}) collective-permute-start(bf16[2,16,16,128]{3,2,1,0:T(8,128)(2,1)S(1)} %get-tuple-element.46), channel_id=1, source_target_pairs={{0,18},{1,19},{2,16},{3,17},{4,22},{5,23},{6,20},{7,21},{8,26},{9,... | collective-permute-start | bytes 393224 | tf_op jit(solution)/shard_map/ppermute | solution.py:308
  41.2 1.9 %collective-permute-start.2 = (bf16[2,16,16,128]{3,2,1,0:T(8,128)(2,1)S(1)}, bf16[2,16,16,128]{3,2,1,0:T(8,128)(2,1)S(1)}, u32[]{:S(2)}, u32[]{:S(2)}) collective-permute-start(bf16[2,16,16,128]{3,2,1,0:T(8,128)(2,1)S(1)} %get-tuple-element.32), channel_id=1, source_target_pairs={{0,30},{1,31},{2,4},{3,5},{4,2},{5,3},{6,8},{7,9},{8,6},{9,7},{10,... | collective-permute-start | bytes 393224 | tf_op jit(solution)/shard_map/ppermute | solution.py:308
  43.1 0.0 collective-permute-done.8
  43.1 2.2 %collective-permute-start.3 = (bf16[2,16,16,128]{3,2,1,0:T(8,128)(2,1)S(1)}, bf16[2,16,16,128]{3,2,1,0:T(8,128)(2,1)S(1)}, u32[]{:S(2)}, u32[]{:S(2)}) collective-permute-start(bf16[2,16,16,128]{3,2,1,0:T(8,128)(2,1)S(1)} %get-tuple-element.34), channel_id=1, source_target_pairs={{0,4},{1,5},{2,30},{3,31},{4,8},{5,9},{6,2},{7,3},{8,12},{9,13},{1... | collective-permute-start | bytes 393224 | tf_op jit(solution)/shard_map/ppermute | solution.py:308
  45.3 2.5 %collective-permute-done.9 = bf16[2,16,16,128]{3,2,1,0:T(8,128)(2,1)S(1)} collective-permute-done((bf16[2,16,16,128]{3,2,1,0:T(8,128)(2,1)S(1)}, bf16[2,16,16,128]{3,2,1,0:T(8,128)(2,1)S(1)}, u32[]{:S(2)}, u32[]{:S(2)}) %collective-permute-start.9) | collective-permute-done | bytes 131104 | tf_op jit(solution)/shard_map/ppermute | solution.py:308
  47.9 5.9 %collective-permute-start.4 = (bf16[2,16,16,128]{3,2,1,0:T(8,128)(2,1)S(1)}, bf16[2,16,16,128]{3,2,1,0:T(8,128)(2,1)S(1)}, u32[]{:S(2)}, u32[]{:S(2)}) collective-permute-start(bf16[2,16,16,128]{3,2,1,0:T(8,128)(2,1)S(1)} %get-tuple-element.36), channel_id=1, source_target_pairs={{0,26},{1,27},{2,8},{3,9},{4,30},{5,31},{6,12},{7,13},{8,2},{9,3},... | collective-permute-start | bytes 393224 | tf_op jit(solution)/shard_map/ppermute | solution.py:308
  53.8 0.0 collective-permute-done.10
  53.9 4.7 %collective-permute-done.11 = bf16[2,16,16,128]{3,2,1,0:T(8,128)(2,1)S(1)} collective-permute-done((bf16[2,16,16,128]{3,2,1,0:T(8,128)(2,1)S(1)}, bf16[2,16,16,128]{3,2,1,0:T(8,128)(2,1)S(1)}, u32[]{:S(2)}, u32[]{:S(2)}) %collective-permute-start.11) | collective-permute-done | bytes 131104 | tf_op jit(solution)/shard_map/ppermute | solution.py:308
  58.6 3.9 %collective-permute-start.12 = (bf16[8,16,16,128]{3,2,1,0:T(8,128)(2,1)S(1)}, bf16[8,16,16,128]{3,2,1,0:T(8,128)(2,1)S(1)}, u32[]{:S(2)}, u32[]{:S(2)}) collective-permute-start(bf16[8,16,16,128]{3,2,1,0:T(8,128)(2,1)S(1)} %constant_dynamic-update-slice_fusion.4.own_ref), channel_id=1, source_target_pairs={{0,2},{1,3},{2,0},{3,1},{4,6},{5,7},{6,4},{7,5},{8,10},{9,11},{10,... | collective-permute-start | bytes 1572872 | tf_op jit(solution)/shard_map/ppermute | solution.py:294
  62.5 1.4 collective-permute-done.2
  63.9 0.0 collective-permute-done.3
  63.9 4.2 %collective-permute-done.4 = bf16[2,16,16,128]{3,2,1,0:T(8,128)(2,1)S(1)} collective-permute-done((bf16[2,16,16,128]{3,2,1,0:T(8,128)(2,1)S(1)}, bf16[2,16,16,128]{3,2,1,0:T(8,128)(2,1)S(1)}, u32[]{:S(2)}, u32[]{:S(2)}) %collective-permute-start.4) | collective-permute-done | bytes 131104 | tf_op jit(solution)/shard_map/ppermute | solution.py:308
  68.1 5.7 %collective-permute-start.5 = (bf16[8,16,16,128]{3,2,1,0:T(8,128)(2,1)S(1)}, bf16[8,16,16,128]{3,2,1,0:T(8,128)(2,1)S(1)}, u32[]{:S(2)}, u32[]{:S(2)}) collective-permute-start(bf16[8,16,16,128]{3,2,1,0:T(8,128)(2,1)S(1)} %constant_dynamic-update-slice_fusion.own_ref), channel_id=1, source_target_pairs={{0,2},{1,3},{2,0},{3,1},{4,6},{5,7},{6,4},{7,5},{8,10},{9,11},{10,... | collective-permute-start | bytes 1572872 | tf_op jit(solution)/shard_map/ppermute | solution.py:294
  73.9 3.6 %collective-permute-done.12.chip_ref = bf16[8,16,16,128]{3,2,1,0:T(8,128)(2,1)S(1)} collective-permute-done((bf16[8,16,16,128]{3,2,1,0:T(8,128)(2,1)S(1)}, bf16[8,16,16,128]{3,2,1,0:T(8,128)(2,1)S(1)}, u32[]{:S(2)}, u32[]{:S(2)}) %collective-permute-start.12) | collective-permute-done | bytes 524320 | tf_op jit(solution)/shard_map/ppermute | solution.py:294
  77.5 0.0 copy-done.6
  77.5 0.0 copy-done
  77.5 3.6 %expert.3 = (bf16[8,16,16,128]{3,2,1,0:T(8,128)(2,1)S(1)}, bf16[8,16,16,128]{3,2,1,0:T(8,128)(2,1)S(1)}) custom-call(bf16[8,16,16,128]{3,2,1,0:T(8,128)(2,1)S(1)} %constant_dynamic-update-slice_fusion.4.own_ref, bf16[8,16,16,128]{3,2,1,0:T(8,128)(2,1)S(1)} %collective-permute-done.12.chip_ref, bf16[1,3584,256]{2,1,0:T(8,128)(2,1)S(1)} %copy-done, ...), custom_call_target="tpu_custom_call" | custom-call | tf_op jit(solution)/shard_map/expert/pallas_call | solution.py:258
  81.1 3.9 %collective-permute-start.13 = (bf16[8,16,16,128]{3,2,1,0:T(8,128)(2,1)S(1)}, bf16[8,16,16,128]{3,2,1,0:T(8,128)(2,1)S(1)}, u32[]{:S(2)}, u32[]{:S(2)}) collective-permute-start(bf16[8,16,16,128]{3,2,1,0:T(8,128)(2,1)S(1)} %get-tuple-element.48), channel_id=1, source_target_pairs={{0,2},{1,3},{2,0},{3,1},{4,6},{5,7},{6,4},{7,5},{8,10},{9,11},{10,... | collective-permute-start | bytes 1572872 | tf_op jit(solution)/shard_map/ppermute | solution.py:294
  85.0 3.7 %collective-permute-done.5.chip_ref = bf16[8,16,16,128]{3,2,1,0:T(8,128)(2,1)S(1)} collective-permute-done((bf16[8,16,16,128]{3,2,1,0:T(8,128)(2,1)S(1)}, bf16[8,16,16,128]{3,2,1,0:T(8,128)(2,1)S(1)}, u32[]{:S(2)}, u32[]{:S(2)}) %collective-permute-start.5) | collective-permute-done | bytes 524320 | tf_op jit(solution)/shard_map/ppermute | solution.py:294
  88.8 3.6 %expert.2 = (bf16[8,16,16,128]{3,2,1,0:T(8,128)(2,1)S(1)}, bf16[8,16,16,128]{3,2,1,0:T(8,128)(2,1)S(1)}) custom-call(bf16[8,16,16,128]{3,2,1,0:T(8,128)(2,1)S(1)} %constant_dynamic-update-slice_fusion.own_ref, bf16[8,16,16,128]{3,2,1,0:T(8,128)(2,1)S(1)} %collective-permute-done.5.chip_ref, bf16[1,3584,256]{2,1,0:T(8,128)(2,1)S(1)} %copy-done, ...), custom_call_target="tpu_custom_call" | custom-call | tf_op jit(solution)/shard_map/expert/pallas_call | solution.py:258
  92.4 0.0 copy-start.2
  92.4 4.0 %collective-permute-start.6 = (bf16[8,16,16,128]{3,2,1,0:T(8,128)(2,1)S(1)}, bf16[8,16,16,128]{3,2,1,0:T(8,128)(2,1)S(1)}, u32[]{:S(2)}, u32[]{:S(2)}) collective-permute-start(bf16[8,16,16,128]{3,2,1,0:T(8,128)(2,1)S(1)} %get-tuple-element.38), channel_id=1, source_target_pairs={{0,2},{1,3},{2,0},{3,1},{4,6},{5,7},{6,4},{7,5},{8,10},{9,11},{10,... | collective-permute-start | bytes 1572872 | tf_op jit(solution)/shard_map/ppermute | solution.py:294
  96.4 3.6 %collective-permute-done.13 = bf16[8,16,16,128]{3,2,1,0:T(8,128)(2,1)S(1)} collective-permute-done((bf16[8,16,16,128]{3,2,1,0:T(8,128)(2,1)S(1)}, bf16[8,16,16,128]{3,2,1,0:T(8,128)(2,1)S(1)}, u32[]{:S(2)}, u32[]{:S(2)}) %collective-permute-start.13) | collective-permute-done | bytes 524320 | tf_op jit(solution)/shard_map/ppermute | solution.py:294
  100.0 0.1 add_convert_fusion.2
  100.1 8.1 %collective-permute-start.14 = (bf16[2,16,16,128]{3,2,1,0:T(8,128)(2,1)S(1)}, bf16[2,16,16,128]{3,2,1,0:T(8,128)(2,1)S(1)}, u32[]{:S(2)}, u32[]{:S(2)}) collective-permute-start(bf16[2,16,16,128]{3,2,1,0:T(8,128)(2,1)S(1)} %get-tuple-element.56), channel_id=1, source_target_pairs={{8,0},{9,1},{26,2},{27,3},{12,4},{13,5},{30,6},{31,7},{16,8},{17,9... | collective-permute-start | bytes 393224 | tf_op jit(solution)/shard_map/ppermute | solution.py:308
  108.2 5.8 %collective-permute-start.15 = (bf16[2,16,16,128]{3,2,1,0:T(8,128)(2,1)S(1)}, bf16[2,16,16,128]{3,2,1,0:T(8,128)(2,1)S(1)}, u32[]{:S(2)}, u32[]{:S(2)}) collective-permute-start(bf16[2,16,16,128]{3,2,1,0:T(8,128)(2,1)S(1)} %get-tuple-element.55), channel_id=1, source_target_pairs={{12,0},{13,1},{22,2},{23,3},{16,4},{17,5},{26,6},{27,7},{20,8},{21... | collective-permute-start | bytes 393224 | tf_op jit(solution)/shard_map/ppermute | solution.py:308
  114.0 5.3 %collective-permute-start.16 = (bf16[2,16,16,128]{3,2,1,0:T(8,128)(2,1)S(1)}, bf16[2,16,16,128]{3,2,1,0:T(8,128)(2,1)S(1)}, u32[]{:S(2)}, u32[]{:S(2)}) collective-permute-start(bf16[2,16,16,128]{3,2,1,0:T(8,128)(2,1)S(1)} %get-tuple-element.54), channel_id=1, source_target_pairs={{18,0},{19,1},{16,2},{17,3},{22,4},{23,5},{20,6},{21,7},{26,8},{27... | collective-permute-start | bytes 393224 | tf_op jit(solution)/shard_map/ppermute | solution.py:308
  119.3 5.1 %collective-permute-start.17 = (bf16[2,16,16,128]{3,2,1,0:T(8,128)(2,1)S(1)}, bf16[2,16,16,128]{3,2,1,0:T(8,128)(2,1)S(1)}, u32[]{:S(2)}, u32[]{:S(2)}) collective-permute-start(bf16[2,16,16,128]{3,2,1,0:T(8,128)(2,1)S(1)} %get-tuple-element.53), channel_id=1, source_target_pairs={{22,0},{23,1},{12,2},{13,3},{26,4},{27,5},{16,6},{17,7},{30,8},{31... | collective-permute-start | bytes 393224 | tf_op jit(solution)/shard_map/ppermute | solution.py:308
  124.4 12.5 %collective-permute-done.6 = bf16[8,16,16,128]{3,2,1,0:T(8,128)(2,1)S(1)} collective-permute-done((bf16[8,16,16,128]{3,2,1,0:T(8,128)(2,1)S(1)}, bf16[8,16,16,128]{3,2,1,0:T(8,128)(2,1)S(1)}, u32[]{:S(2)}, u32[]{:S(2)}) %collective-permute-start.6) | collective-permute-done | bytes 524320 | tf_op jit(solution)/shard_map/ppermute | solution.py:294
  136.9 0.1 add_convert_fusion
  137.1 2.1 %collective-permute-start.18 = (bf16[2,16,16,128]{3,2,1,0:T(8,128)(2,1)S(1)}, bf16[2,16,16,128]{3,2,1,0:T(8,128)(2,1)S(1)}, u32[]{:S(2)}, u32[]{:S(2)}) collective-permute-start(bf16[2,16,16,128]{3,2,1,0:T(8,128)(2,1)S(1)} %get-tuple-element.50), channel_id=1, source_target_pairs={{26,0},{27,1},{8,2},{9,3},{30,4},{31,5},{12,6},{13,7},{2,8},{3,9},... | collective-permute-start | bytes 393224 | tf_op jit(solution)/shard_map/ppermute | solution.py:308
  139.2 0.0 collective-permute-done.14.rest_2_
  139.2 5.7 %collective-permute-start.19 = (bf16[2,16,16,128]{3,2,1,0:T(8,128)(2,1)S(1)}, bf16[2,16,16,128]{3,2,1,0:T(8,128)(2,1)S(1)}, u32[]{:S(2)}, u32[]{:S(2)}) collective-permute-start(bf16[2,16,16,128]{3,2,1,0:T(8,128)(2,1)S(1)} %get-tuple-element.49), channel_id=1, source_target_pairs={{30,0},{31,1},{4,2},{5,3},{2,4},{3,5},{8,6},{9,7},{6,8},{7,9},{12,... | collective-permute-start | bytes 393224 | tf_op jit(solution)/shard_map/ppermute | solution.py:308
  144.9 0.0 collective-permute-done.15.rest_3_
  144.9 5.3 %collective-permute-start.7 = (bf16[2,16,16,128]{3,2,1,0:T(8,128)(2,1)S(1)}, bf16[2,16,16,128]{3,2,1,0:T(8,128)(2,1)S(1)}, u32[]{:S(2)}, u32[]{:S(2)}) collective-permute-start(bf16[2,16,16,128]{3,2,1,0:T(8,128)(2,1)S(1)} %get-tuple-element.51), channel_id=1, source_target_pairs={{4,0},{5,1},{30,2},{31,3},{8,4},{9,5},{2,6},{3,7},{12,8},{13,9},{6... | collective-permute-start | bytes 393224 | tf_op jit(solution)/shard_map/ppermute | solution.py:308
  150.2 0.0 collective-permute-done.16.rest_4_
  150.3 0.0 collective-permute-done.17.rest_5_
  150.3 0.1 collective-permute-done.18.rest_6_
  150.3 2.8 %collective-permute-done.19.rest_7_ = bf16[2,16,16,128]{3,2,1,0:T(8,128)(2,1)S(1)} collective-permute-done((bf16[2,16,16,128]{3,2,1,0:T(8,128)(2,1)S(1)}, bf16[2,16,16,128]{3,2,1,0:T(8,128)(2,1)S(1)}, u32[]{:S(2)}, u32[]{:S(2)}) %collective-permute-start.19) | collective-permute-done | bytes 131104 | tf_op jit(solution)/shard_map/ppermute | solution.py:308
  153.2 1.8 %collective-permute-done.7.rest_1_ = bf16[2,16,16,128]{3,2,1,0:T(8,128)(2,1)S(1)} collective-permute-done((bf16[2,16,16,128]{3,2,1,0:T(8,128)(2,1)S(1)}, bf16[2,16,16,128]{3,2,1,0:T(8,128)(2,1)S(1)}, u32[]{:S(2)}, u32[]{:S(2)}) %collective-permute-start.7) | collective-permute-done | bytes 131104 | tf_op jit(solution)/shard_map/ppermute | solution.py:308
  155.0 0.0 copy-done.2
  155.0 0.5 finish.3
  155.5 3.1 %collective-permute-start.20 = (bf16[48,3584]{1,0:T(8,128)(2,1)S(1)}, bf16[48,3584]{1,0:T(8,128)(2,1)S(1)}, u32[]{:S(2)}, u32[]{:S(2)}) collective-permute-start(bf16[48,3584]{1,0:T(8,128)(2,1)S(1)} %finish.3), channel_id=1, source_target_pairs={{0,32},{32,64},{64,96},{96,128},{128,160},{160,192},{192,224},{224... | collective-permute-start | bytes 1032200 | tf_op jit(solution)/shard_map/ppermute | solution.py:290
  158.6 0.5 finish.2
  159.1 2.7 %collective-permute-start.21 = (bf16[48,3584]{1,0:T(8,128)(2,1)S(1)}, bf16[48,3584]{1,0:T(8,128)(2,1)S(1)}, u32[]{:S(2)}, u32[]{:S(2)}) collective-permute-start(bf16[48,3584]{1,0:T(8,128)(2,1)S(1)} %finish.2), channel_id=1, source_target_pairs={{32,0},{64,32},{96,64},{128,96},{160,128},{192,160},{224,192},{256... | collective-permute-start | bytes 1032200 | tf_op jit(solution)/shard_map/ppermute | solution.py:290
  161.8 3.7 %collective-permute-done.20 = bf16[48,3584]{1,0:T(8,128)(2,1)S(1)} collective-permute-done((bf16[48,3584]{1,0:T(8,128)(2,1)S(1)}, bf16[48,3584]{1,0:T(8,128)(2,1)S(1)}, u32[]{:S(2)}, u32[]{:S(2)}) %collective-permute-start.20) | collective-permute-done | bytes 344096 | tf_op jit(solution)/shard_map/ppermute | solution.py:290
  165.6 5.4 %collective-permute-done.21 = bf16[48,3584]{1,0:T(8,128)(2,1)S(1)} collective-permute-done((bf16[48,3584]{1,0:T(8,128)(2,1)S(1)}, bf16[48,3584]{1,0:T(8,128)(2,1)S(1)}, u32[]{:S(2)}, u32[]{:S(2)}) %collective-permute-start.21) | collective-permute-done | bytes 344096 | tf_op jit(solution)/shard_map/ppermute | solution.py:290
  171.1 0.9 maximum_bitcast_fusion
  (12 shorter events, 0.2 us)
Async XLA Ops:
  0.0 77.5 %copy-start = (bf16[1,3584,256]{2,1,0:T(8,128)(2,1)S(1)}, bf16[1,3584,256]{2,1,0:T(8,128)(2,1)}, u32[]{:S(2)}) copy-start(bf16[1,3584,256]{2,1,0:T(8,128)(2,1)} %rest_0_.3) | copy-start | bytes 5505028
  0.0 9.3 %collective-permute-start = (bf16[1,3584,256]{2,1,0:T(8,128)(2,1)}, bf16[1,3584,256]{2,1,0:T(8,128)(2,1)S(1)}, u32[]{:S(2)}, u32[]{:S(2)}) collective-permute-start(bf16[1,3584,256]{2,1,0:T(8,128)(2,1)} %rest_0_.3), channel_id=1, source_target_pairs={{0,1},{1,0},{2,3},{3,2},{4,5},{5,4},{6,7},{7,6},{8,9},{9,8},{10,11... | collective-permute-start | bytes 5505032 | tf_op jit(solution)/shard_map/ppermute | solution.py:294
  2.0 7.2 %collective-permute-start.1 = (bf16[1,256,3584]{2,1,0:T(8,128)(2,1)}, bf16[1,256,3584]{2,1,0:T(8,128)(2,1)S(1)}, u32[]{:S(2)}, u32[]{:S(2)}) collective-permute-start(bf16[1,256,3584]{2,1,0:T(8,128)(2,1)} %rest_2_.3), channel_id=1, source_target_pairs={{0,1},{1,0},{2,3},{3,2},{4,5},{5,4},{6,7},{7,6},{8,9},{9,8},{10,11... | collective-permute-start | bytes 5505032 | tf_op jit(solution)/shard_map/ppermute | solution.py:294
  4.5 1.1 copy-start.1
  5.6 0.8 copy-start.3
  6.4 0.7 copy-start.4
  7.1 0.7 copy-start.5
  9.3 68.2 %copy-start.6 = (bf16[1,256,3584]{2,1,0:T(8,128)(2,1)}, bf16[1,256,3584]{2,1,0:T(8,128)(2,1)S(1)}, u32[]{:S(2)}) copy-start(bf16[1,256,3584]{2,1,0:T(8,128)(2,1)S(1)} %collective-permute-done.1.rest_3_) | copy-start | bytes 5505028
  9.3 33.8 %collective-permute-start.8 = (bf16[2,16,16,128]{3,2,1,0:T(8,128)(2,1)S(1)}, bf16[2,16,16,128]{3,2,1,0:T(8,128)(2,1)S(1)}, u32[]{:S(2)}, u32[]{:S(2)}) collective-permute-start(bf16[2,16,16,128]{3,2,1,0:T(8,128)(2,1)S(1)} %get-tuple-element.40), channel_id=1, source_target_pairs={{0,8},{1,9},{2,26},{3,27},{4,12},{5,13},{6,30},{7,31},{8,16},{9,17... | collective-permute-start | bytes 393224 | tf_op jit(solution)/shard_map/ppermute | solution.py:308
  18.4 29.5 %collective-permute-start.9 = (bf16[2,16,16,128]{3,2,1,0:T(8,128)(2,1)S(1)}, bf16[2,16,16,128]{3,2,1,0:T(8,128)(2,1)S(1)}, u32[]{:S(2)}, u32[]{:S(2)}) collective-permute-start(bf16[2,16,16,128]{3,2,1,0:T(8,128)(2,1)S(1)} %get-tuple-element.42), channel_id=1, source_target_pairs={{0,22},{1,23},{2,12},{3,13},{4,26},{5,27},{6,16},{7,17},{8,30},{9,... | collective-permute-start | bytes 393224 | tf_op jit(solution)/shard_map/ppermute | solution.py:308
  27.0 26.8 %collective-permute-start.10 = (bf16[2,16,16,128]{3,2,1,0:T(8,128)(2,1)S(1)}, bf16[2,16,16,128]{3,2,1,0:T(8,128)(2,1)S(1)}, u32[]{:S(2)}, u32[]{:S(2)}) collective-permute-start(bf16[2,16,16,128]{3,2,1,0:T(8,128)(2,1)S(1)} %get-tuple-element.44), channel_id=1, source_target_pairs={{0,12},{1,13},{2,22},{3,23},{4,16},{5,17},{6,26},{7,27},{8,20},{9,... | collective-permute-start | bytes 393224 | tf_op jit(solution)/shard_map/ppermute | solution.py:308
  33.1 25.4 %collective-permute-start.11 = (bf16[2,16,16,128]{3,2,1,0:T(8,128)(2,1)S(1)}, bf16[2,16,16,128]{3,2,1,0:T(8,128)(2,1)S(1)}, u32[]{:S(2)}, u32[]{:S(2)}) collective-permute-start(bf16[2,16,16,128]{3,2,1,0:T(8,128)(2,1)S(1)} %get-tuple-element.46), channel_id=1, source_target_pairs={{0,18},{1,19},{2,16},{3,17},{4,22},{5,23},{6,20},{7,21},{8,26},{9,... | collective-permute-start | bytes 393224 | tf_op jit(solution)/shard_map/ppermute | solution.py:308
  41.2 22.6 %collective-permute-start.2 = (bf16[2,16,16,128]{3,2,1,0:T(8,128)(2,1)S(1)}, bf16[2,16,16,128]{3,2,1,0:T(8,128)(2,1)S(1)}, u32[]{:S(2)}, u32[]{:S(2)}) collective-permute-start(bf16[2,16,16,128]{3,2,1,0:T(8,128)(2,1)S(1)} %get-tuple-element.32), channel_id=1, source_target_pairs={{0,30},{1,31},{2,4},{3,5},{4,2},{5,3},{6,8},{7,9},{8,6},{9,7},{10,... | collective-permute-start | bytes 393224 | tf_op jit(solution)/shard_map/ppermute | solution.py:308
  43.1 20.7 %collective-permute-start.3 = (bf16[2,16,16,128]{3,2,1,0:T(8,128)(2,1)S(1)}, bf16[2,16,16,128]{3,2,1,0:T(8,128)(2,1)S(1)}, u32[]{:S(2)}, u32[]{:S(2)}) collective-permute-start(bf16[2,16,16,128]{3,2,1,0:T(8,128)(2,1)S(1)} %get-tuple-element.34), channel_id=1, source_target_pairs={{0,4},{1,5},{2,30},{3,31},{4,8},{5,9},{6,2},{7,3},{8,12},{9,13},{1... | collective-permute-start | bytes 393224 | tf_op jit(solution)/shard_map/ppermute | solution.py:308
  47.9 20.3 %collective-permute-start.4 = (bf16[2,16,16,128]{3,2,1,0:T(8,128)(2,1)S(1)}, bf16[2,16,16,128]{3,2,1,0:T(8,128)(2,1)S(1)}, u32[]{:S(2)}, u32[]{:S(2)}) collective-permute-start(bf16[2,16,16,128]{3,2,1,0:T(8,128)(2,1)S(1)} %get-tuple-element.36), channel_id=1, source_target_pairs={{0,26},{1,27},{2,8},{3,9},{4,30},{5,31},{6,12},{7,13},{8,2},{9,3},... | collective-permute-start | bytes 393224 | tf_op jit(solution)/shard_map/ppermute | solution.py:308
  58.6 18.9 %collective-permute-start.12 = (bf16[8,16,16,128]{3,2,1,0:T(8,128)(2,1)S(1)}, bf16[8,16,16,128]{3,2,1,0:T(8,128)(2,1)S(1)}, u32[]{:S(2)}, u32[]{:S(2)}) collective-permute-start(bf16[8,16,16,128]{3,2,1,0:T(8,128)(2,1)S(1)} %constant_dynamic-update-slice_fusion.4.own_ref), channel_id=1, source_target_pairs={{0,2},{1,3},{2,0},{3,1},{4,6},{5,7},{6,4},{7,5},{8,10},{9,11},{10,... | collective-permute-start | bytes 1572872 | tf_op jit(solution)/shard_map/ppermute | solution.py:294
  68.1 20.6 %collective-permute-start.5 = (bf16[8,16,16,128]{3,2,1,0:T(8,128)(2,1)S(1)}, bf16[8,16,16,128]{3,2,1,0:T(8,128)(2,1)S(1)}, u32[]{:S(2)}, u32[]{:S(2)}) collective-permute-start(bf16[8,16,16,128]{3,2,1,0:T(8,128)(2,1)S(1)} %constant_dynamic-update-slice_fusion.own_ref), channel_id=1, source_target_pairs={{0,2},{1,3},{2,0},{3,1},{4,6},{5,7},{6,4},{7,5},{8,10},{9,11},{10,... | collective-permute-start | bytes 1572872 | tf_op jit(solution)/shard_map/ppermute | solution.py:294
  81.1 18.8 %collective-permute-start.13 = (bf16[8,16,16,128]{3,2,1,0:T(8,128)(2,1)S(1)}, bf16[8,16,16,128]{3,2,1,0:T(8,128)(2,1)S(1)}, u32[]{:S(2)}, u32[]{:S(2)}) collective-permute-start(bf16[8,16,16,128]{3,2,1,0:T(8,128)(2,1)S(1)} %get-tuple-element.48), channel_id=1, source_target_pairs={{0,2},{1,3},{2,0},{3,1},{4,6},{5,7},{6,4},{7,5},{8,10},{9,11},{10,... | collective-permute-start | bytes 1572872 | tf_op jit(solution)/shard_map/ppermute | solution.py:294
  92.4 62.6 %copy-start.2 = (bf16[2,1,48,3584]{3,2,1,0:T(8,128)(2,1)S(1)}, bf16[2,1,48,3584]{3,2,1,0:T(8,128)(2,1)}, u32[]{:S(2)}) copy-start(bf16[2,1,48,3584]{3,2,1,0:T(8,128)(2,1)} %x_ref.5) | copy-start | bytes 2064388
  92.4 44.5 %collective-permute-start.6 = (bf16[8,16,16,128]{3,2,1,0:T(8,128)(2,1)S(1)}, bf16[8,16,16,128]{3,2,1,0:T(8,128)(2,1)S(1)}, u32[]{:S(2)}, u32[]{:S(2)}) collective-permute-start(bf16[8,16,16,128]{3,2,1,0:T(8,128)(2,1)S(1)} %get-tuple-element.38), channel_id=1, source_target_pairs={{0,2},{1,3},{2,0},{3,1},{4,6},{5,7},{6,4},{7,5},{8,10},{9,11},{10,... | collective-permute-start | bytes 1572872 | tf_op jit(solution)/shard_map/ppermute | solution.py:294
  100.1 39.0 %collective-permute-start.14 = (bf16[2,16,16,128]{3,2,1,0:T(8,128)(2,1)S(1)}, bf16[2,16,16,128]{3,2,1,0:T(8,128)(2,1)S(1)}, u32[]{:S(2)}, u32[]{:S(2)}) collective-permute-start(bf16[2,16,16,128]{3,2,1,0:T(8,128)(2,1)S(1)} %get-tuple-element.56), channel_id=1, source_target_pairs={{8,0},{9,1},{26,2},{27,3},{12,4},{13,5},{30,6},{31,7},{16,8},{17,9... | collective-permute-start | bytes 393224 | tf_op jit(solution)/shard_map/ppermute | solution.py:308
  108.2 36.7 %collective-permute-start.15 = (bf16[2,16,16,128]{3,2,1,0:T(8,128)(2,1)S(1)}, bf16[2,16,16,128]{3,2,1,0:T(8,128)(2,1)S(1)}, u32[]{:S(2)}, u32[]{:S(2)}) collective-permute-start(bf16[2,16,16,128]{3,2,1,0:T(8,128)(2,1)S(1)} %get-tuple-element.55), channel_id=1, source_target_pairs={{12,0},{13,1},{22,2},{23,3},{16,4},{17,5},{26,6},{27,7},{20,8},{21... | collective-permute-start | bytes 393224 | tf_op jit(solution)/shard_map/ppermute | solution.py:308
  114.0 36.2 %collective-permute-start.16 = (bf16[2,16,16,128]{3,2,1,0:T(8,128)(2,1)S(1)}, bf16[2,16,16,128]{3,2,1,0:T(8,128)(2,1)S(1)}, u32[]{:S(2)}, u32[]{:S(2)}) collective-permute-start(bf16[2,16,16,128]{3,2,1,0:T(8,128)(2,1)S(1)} %get-tuple-element.54), channel_id=1, source_target_pairs={{18,0},{19,1},{16,2},{17,3},{22,4},{23,5},{20,6},{21,7},{26,8},{27... | collective-permute-start | bytes 393224 | tf_op jit(solution)/shard_map/ppermute | solution.py:308
  119.3 30.9 %collective-permute-start.17 = (bf16[2,16,16,128]{3,2,1,0:T(8,128)(2,1)S(1)}, bf16[2,16,16,128]{3,2,1,0:T(8,128)(2,1)S(1)}, u32[]{:S(2)}, u32[]{:S(2)}) collective-permute-start(bf16[2,16,16,128]{3,2,1,0:T(8,128)(2,1)S(1)} %get-tuple-element.53), channel_id=1, source_target_pairs={{22,0},{23,1},{12,2},{13,3},{26,4},{27,5},{16,6},{17,7},{30,8},{31... | collective-permute-start | bytes 393224 | tf_op jit(solution)/shard_map/ppermute | solution.py:308
  137.1 13.3 %collective-permute-start.18 = (bf16[2,16,16,128]{3,2,1,0:T(8,128)(2,1)S(1)}, bf16[2,16,16,128]{3,2,1,0:T(8,128)(2,1)S(1)}, u32[]{:S(2)}, u32[]{:S(2)}) collective-permute-start(bf16[2,16,16,128]{3,2,1,0:T(8,128)(2,1)S(1)} %get-tuple-element.50), channel_id=1, source_target_pairs={{26,0},{27,1},{8,2},{9,3},{30,4},{31,5},{12,6},{13,7},{2,8},{3,9},... | collective-permute-start | bytes 393224 | tf_op jit(solution)/shard_map/ppermute | solution.py:308
  139.2 14.0 %collective-permute-start.19 = (bf16[2,16,16,128]{3,2,1,0:T(8,128)(2,1)S(1)}, bf16[2,16,16,128]{3,2,1,0:T(8,128)(2,1)S(1)}, u32[]{:S(2)}, u32[]{:S(2)}) collective-permute-start(bf16[2,16,16,128]{3,2,1,0:T(8,128)(2,1)S(1)} %get-tuple-element.49), channel_id=1, source_target_pairs={{30,0},{31,1},{4,2},{5,3},{2,4},{3,5},{8,6},{9,7},{6,8},{7,9},{12,... | collective-permute-start | bytes 393224 | tf_op jit(solution)/shard_map/ppermute | solution.py:308
  144.9 10.1 %collective-permute-start.7 = (bf16[2,16,16,128]{3,2,1,0:T(8,128)(2,1)S(1)}, bf16[2,16,16,128]{3,2,1,0:T(8,128)(2,1)S(1)}, u32[]{:S(2)}, u32[]{:S(2)}) collective-permute-start(bf16[2,16,16,128]{3,2,1,0:T(8,128)(2,1)S(1)} %get-tuple-element.51), channel_id=1, source_target_pairs={{4,0},{5,1},{30,2},{31,3},{8,4},{9,5},{2,6},{3,7},{12,8},{13,9},{6... | collective-permute-start | bytes 393224 | tf_op jit(solution)/shard_map/ppermute | solution.py:308
  155.5 10.1 %collective-permute-start.20 = (bf16[48,3584]{1,0:T(8,128)(2,1)S(1)}, bf16[48,3584]{1,0:T(8,128)(2,1)S(1)}, u32[]{:S(2)}, u32[]{:S(2)}) collective-permute-start(bf16[48,3584]{1,0:T(8,128)(2,1)S(1)} %finish.3), channel_id=1, source_target_pairs={{0,32},{32,64},{64,96},{96,128},{128,160},{160,192},{192,224},{224... | collective-permute-start | bytes 1032200 | tf_op jit(solution)/shard_map/ppermute | solution.py:290
  159.1 11.9 %collective-permute-start.21 = (bf16[48,3584]{1,0:T(8,128)(2,1)S(1)}, bf16[48,3584]{1,0:T(8,128)(2,1)S(1)}, u32[]{:S(2)}, u32[]{:S(2)}) collective-permute-start(bf16[48,3584]{1,0:T(8,128)(2,1)S(1)} %finish.2), channel_id=1, source_target_pairs={{32,0},{64,32},{96,64},{128,96},{160,128},{192,160},{224,192},{256... | collective-permute-start | bytes 1032200 | tf_op jit(solution)/shard_map/ppermute | solution.py:290
